TPU v7x, 512 devices: a whole 4x8x8 slice. The times are simulated.
512 devices in a mesh: frame: 64 (over y, x, core), row: 8 (over z).
Axes of the slice: x: 4, y: 8, z: 8, core: 2. Of those that a mesh axis runs over, the one named last changes fastest.
Arguments:
- tokens: bfloat16 [64, 8, 128, 2048], P('frame', 'row'), may hold values from -6 to 6
- cotangent: bfloat16 [64, 8, 128, 2048], P('frame', 'row'), may hold values from -6 to 6
- timestep: int32 [4], replicated, may hold values from 0 to 999
- mod_weight: bfloat16 [256, 4096], P(None, 'frame'), may hold values from -0.375 to 0.375
- proj_weight: bfloat16 [2048, 256], P('frame'), may hold values from -0.125 to 0.125
- step_weight: bfloat16 [2048, 32], P('frame'), may hold values from -0.125 to 0.125
- step_bias: float32 [32], replicated, may hold values from -1 to 1
- rate_space: float32 [32], replicated, may hold values from 0.00029296876 to 0.05
- rate_time: float32 [32], replicated, may hold values from 0.0046875 to 1
- skip_gain: float32 [32], replicated, may hold values from 0.5 to 1.5
Outputs:
- mixed: bfloat16 [64, 8, 128, 2048], P('frame', 'row')
- d_tokens: bfloat16 [64, 8, 128, 2048], P('frame', 'row')
- grad_proj: float32 [2048, 256], P('frame')
- grad_step: float32 [2048, 32], P('frame')
- grad_mod: float32 [256, 4096], P(None, 'frame')
All inputs are finite; a program needn't handle non-finite values.
Results may differ from a plain program's by a relative error of at most 0.015.
Values may be sent and summed in bfloat16 or wider, within the bound.
A program may use at most 64 MiB of HBM per device.

v0:
```python
import math

import jax
import jax.numpy as jnp
from jax import lax
from jax.sharding import PartitionSpec as P

norm_eps = 1e-05


def prefix(array, axis, join, neutral):
    place = lax.axis_index(axis)
    gathered = jax.tree.map(
        lambda a, kind: lax.all_gather(a.astype(kind), axis), array, (jnp.bfloat16, jnp.bfloat16)
    )
    state = jax.tree.map(lambda a, e: jnp.zeros_like(a) + jnp.asarray(e, a.dtype), array, neutral)

    def prefix_one(hop, state):
        return join(
            state,
            jax.tree.map(
                lambda a, own: lax.dynamic_index_in_dim(a, hop, 0, False).astype(own.dtype),
                gathered,
                array,
            ),
        )

    return lax.fori_loop(0, place, prefix_one, state)


def carried_in(array, axis, join, neutral):
    count = lax.axis_size(axis)
    place = lax.axis_index(axis)
    ahead = count - 1 - place
    gathered = jax.tree.map(
        lambda a, kind: lax.all_gather(a.astype(kind), axis),
        array,
        jax.tree.map(lambda a: jnp.bfloat16 if a.dtype == jnp.float32 else a.dtype, array),
    )
    state = jax.tree.map(lambda a, e: jnp.zeros_like(a) + jnp.asarray(e, a.dtype), array, neutral)

    def carried_one(hop, state):
        source = count - 1 - hop
        return join(
            state,
            jax.tree.map(
                lambda a, own: lax.dynamic_index_in_dim(a, source, 0, False).astype(own.dtype),
                gathered,
                array,
            ),
        )

    return lax.fori_loop(0, ahead, carried_one, state)


def time_embed(timestep, embed_dim):
    half_dim = embed_dim // 2
    frequency = jnp.exp(-math.log(10000.0) * jnp.arange(half_dim, dtype=jnp.float32) / half_dim)
    angles = timestep.astype(jnp.float32)[:, None] * frequency[None, :]
    return jax.nn.silu(jnp.concatenate([jnp.cos(angles), jnp.sin(angles)], axis=1))


def normalize(values):
    return values * lax.rsqrt(jnp.mean(values * values, axis=-1, keepdims=True) + norm_eps)


def block_parts(normed, coeffs, logits, step_bias, decay_rate, need_end):
    seq_count, length, feat_width = normed.shape
    head_count = decay_rate.shape[0]
    inputs = normed.reshape(seq_count, length, head_count, feat_width // head_count)
    state_size = coeffs.shape[-1] // 2
    b_part = coeffs[..., :state_size]
    c_part = coeffs[..., state_size:]
    step_size = jax.nn.softplus(logits.astype(jnp.float32) + step_bias)
    cum_log = jnp.cumsum(-step_size * decay_rate, axis=1)
    scores = (
        jnp.einsum("stn,sun->stu", c_part, b_part, preferred_element_type=jnp.float32) / state_size
    )
    lag_rows = jnp.swapaxes(cum_log, 1, 2)
    causal = jnp.tril(jnp.ones((length, length), dtype=bool))
    differences = lag_rows[:, :, :, None] - lag_rows[:, :, None, :]
    decays = jnp.where(causal, jnp.exp(jnp.where(causal, differences, 0.0)), 0.0)
    spread = jnp.swapaxes(step_size, 1, 2)
    weights = (scores[:, None, :, :] * decays * spread[:, :, None, :]).astype(jnp.bfloat16)
    inner_out = jnp.einsum("shtu,suhp->sthp", weights, inputs, preferred_element_type=jnp.float32)
    inner_out = inner_out.reshape(seq_count, length, feat_width)
    if need_end:
        end_log = cum_log[:, -1:, :]
        lead_decay = jnp.exp(end_log - cum_log) * step_size
        scaled = (inputs.astype(jnp.float32) * lead_decay[..., None]).astype(jnp.bfloat16)
        end_local = jnp.einsum("sthp,stn->shpn", scaled, b_part, preferred_element_type=jnp.float32)
    else:
        end_local = jnp.zeros(
            (seq_count, head_count, feat_width // head_count, state_size), jnp.float32
        )
    return (inner_out, end_local, cum_log, c_part)


def carry_term(cum_log, c_part, state_in):
    seq_count, length, head_count = cum_log.shape
    state_size = c_part.shape[-1]
    reached = jnp.einsum(
        "stn,shpn->sthp", c_part.astype(jnp.float32), state_in, precision=lax.Precision.HIGHEST
    )
    return (reached * jnp.exp(cum_log)[..., None] / state_size).reshape(seq_count, length, -1)


def combine_forward(earlier, later):
    return (earlier[0] * later[0], later[0][:, :, None, None] * earlier[1] + later[1])


def combine_backward(earlier, later):
    return (earlier[0] * later[0], later[1] + later[0][:, :, None, None] * earlier[1])


def per_device(
    tokens,
    cotangent,
    timestep,
    mod_weight,
    proj_weight,
    step_weight,
    step_bias,
    rate_space,
    rate_time,
    skip_gain,
):
    frame_count = lax.axis_size("frame")
    row_count = lax.axis_size("row")
    frame_id = lax.axis_index("frame")
    feat_width = tokens.shape[-1]
    band_len = tokens.shape[1] * tokens.shape[2]
    clip_count = timestep.shape[0]
    clip_frames = frame_count // clip_count
    site_count = band_len // frame_count
    head_count = rate_space.shape[0]
    clip_id = frame_id // clip_frames
    factor = (frame_count * row_count * band_len) ** (-0.5)
    activated = time_embed(timestep, mod_weight.shape[0]).astype(jnp.bfloat16)
    proj_full, step_full = (
        lax.all_gather(proj_weight, "frame", axis=0, tiled=True),
        lax.all_gather(step_weight, "frame", axis=0, tiled=True),
    )
    mod_full = lax.all_gather(mod_weight, "frame", axis=1, tiled=True)
    modulation = jnp.dot(activated, mod_full, preferred_element_type=jnp.float32)
    clip_mod = lax.dynamic_index_in_dim(modulation, clip_id, 0, keepdims=False)
    shift_vec = clip_mod[:feat_width]
    scale_vec = clip_mod[feat_width:]
    tokens_wide = tokens.reshape(band_len, feat_width).astype(jnp.float32)
    unit_rows = normalize(tokens_wide)
    normed = (unit_rows * (1.0 + scale_vec) + shift_vec).astype(jnp.bfloat16)
    projected = jnp.dot(normed, proj_full, preferred_element_type=jnp.float32).astype(jnp.bfloat16)
    logits = jnp.dot(normed, step_full, preferred_element_type=jnp.float32).astype(jnp.bfloat16)
    skip_full = jnp.repeat(skip_gain, feat_width // head_count)
    flat_grad = cotangent.reshape(band_len, feat_width)

    def space_parts(normed_band, proj_band, logit_band):
        return block_parts(normed_band, proj_band, logit_band, step_bias, rate_space, True)

    parts_out, parts_pull = jax.vjp(space_parts, normed[None], projected[None], logits[None])
    inner_out, end_local, cum_log, c_part = parts_out
    end_decay = jnp.exp(cum_log[:, -1, :])
    identity = (jnp.ones_like(end_decay), jnp.zeros_like(end_local))
    prefix_decay, state_in = prefix((end_decay, end_local), "row", combine_forward, identity)
    carried, carry_pull = jax.vjp(carry_term, cum_log, c_part, state_in)
    space_out = (inner_out + carried)[0]
    site_normed, site_grad, site_proj, site_logits = (
        lax.all_to_all(normed, "frame", split_axis=0, concat_axis=0, tiled=True),
        lax.all_to_all(flat_grad, "frame", split_axis=0, concat_axis=0, tiled=True),
        lax.all_to_all(projected, "frame", split_axis=0, concat_axis=0, tiled=True),
        lax.all_to_all(logits, "frame", split_axis=0, concat_axis=0, tiled=True),
    )

    def to_seq(member):
        shaped = member.reshape(frame_count, site_count, member.shape[-1])
        return shaped.transpose(1, 0, 2)

    def from_seq(member):
        return member.transpose(1, 0, 2).reshape(frame_count * site_count, member.shape[-1])

    def time_path(normed_seq, proj_seq, logit_seq):
        return block_parts(normed_seq, proj_seq, logit_seq, step_bias, rate_time, False)[0]

    time_out, time_pull = jax.vjp(
        time_path, to_seq(site_normed), to_seq(site_proj), to_seq(site_logits)
    )
    time_low = from_seq(time_out.astype(jnp.bfloat16))
    time_dnorm, time_dproj, time_dlogit = time_pull(to_seq(site_grad).astype(jnp.float32))
    space_time, back_dnorm, back_dproj, back_dlogit = (
        lax.all_to_all(time_low, "frame", split_axis=0, concat_axis=0, tiled=True),
        lax.all_to_all(from_seq(time_dnorm), "frame", split_axis=0, concat_axis=0, tiled=True),
        lax.all_to_all(from_seq(time_dproj), "frame", split_axis=0, concat_axis=0, tiled=True),
        lax.all_to_all(from_seq(time_dlogit), "frame", split_axis=0, concat_axis=0, tiled=True),
    )
    time_back = (
        back_dnorm.astype(jnp.float32)
        + jnp.dot(back_dproj, proj_full.T, preferred_element_type=jnp.float32)
        + jnp.dot(back_dlogit, step_full.T, preferred_element_type=jnp.float32)
    ).astype(jnp.bfloat16)
    proj_time = jnp.dot(normed.T, back_dproj, preferred_element_type=jnp.float32)
    step_time = jnp.dot(normed.T, back_dlogit, preferred_element_type=jnp.float32)
    mixed = (
        space_out + space_time.astype(jnp.float32) + skip_full * normed.astype(jnp.float32)
    ).astype(jnp.bfloat16)
    upstream = flat_grad.astype(jnp.float32)
    carry_dcum, carry_dc, own_state = carry_pull(upstream[None])
    suffix_decay, later_grad = carried_in((end_decay, own_state), "row", combine_backward, identity)
    end_dlog = jnp.sum(later_grad * state_in, axis=(2, 3)) * end_decay
    carry_dcum = carry_dcum.at[:, -1, :].add(end_dlog)
    space_dnorm, space_dproj, space_dlogit = parts_pull(
        (upstream[None], later_grad, carry_dcum, carry_dc)
    )
    skip_dnorm = (upstream * skip_full).astype(jnp.bfloat16)
    total_dnorm = space_dnorm[0] + skip_dnorm
    pre_grad = (
        total_dnorm.astype(jnp.float32)
        + jnp.dot(space_dproj[0], proj_full.T, preferred_element_type=jnp.float32)
        + jnp.dot(space_dlogit[0], step_full.T, preferred_element_type=jnp.float32)
        + time_back.astype(jnp.float32)
    )
    proj_term = jnp.dot(normed.T, space_dproj[0], preferred_element_type=jnp.float32) + proj_time
    step_term = jnp.dot(normed.T, space_dlogit[0], preferred_element_type=jnp.float32) + step_time
    shift_grad = jnp.sum(pre_grad, axis=0)
    scale_grad = jnp.sum(pre_grad * unit_rows, axis=0)
    picked = (jnp.arange(clip_count) == clip_id).astype(jnp.float32)
    mod_term = jnp.concatenate([shift_grad, scale_grad])[:, None] * picked[None, :]
    proj_sum, step_sum, mod_sum = (
        lax.psum(proj_term.astype(jnp.bfloat16), "row").astype(jnp.float32),
        lax.psum(step_term.astype(jnp.bfloat16), "row").astype(jnp.float32),
        lax.psum(mod_term.astype(jnp.bfloat16), "row").astype(jnp.float32),
    )
    proj_sum, step_sum, mod_sum = (
        lax.psum_scatter(proj_sum, "frame", scatter_dimension=0, tiled=True),
        lax.psum_scatter(step_sum, "frame", scatter_dimension=0, tiled=True),
        lax.psum_scatter(mod_sum, "frame", scatter_dimension=0, tiled=True),
    )
    grad_proj = proj_sum * factor
    grad_step = step_sum * factor
    grad_mod = (
        jnp.dot(activated.astype(jnp.float32).T, mod_sum.T, precision=lax.Precision.HIGHEST)
        * factor
    )
    unused, norm_pull = jax.vjp(normalize, tokens_wide)
    (tokens_grad,) = norm_pull(pre_grad * (1.0 + scale_vec))
    d_tokens = tokens_grad.astype(jnp.bfloat16).reshape(tokens.shape)
    return (mixed.reshape(tokens.shape), d_tokens, grad_proj, grad_step, grad_mod)


def solution(mesh):
    placed = (
        P("frame", "row", None, None),
        P("frame", "row", None, None),
        P(),
        P(None, "frame"),
        P("frame", None),
        P("frame", None),
        P(),
        P(),
        P(),
        P(),
    )
    return jax.shard_map(
        per_device,
        mesh=mesh,
        in_specs=placed,
        out_specs=(
            P("frame", "row", None, None),
            P("frame", "row", None, None),
            P("frame", None),
            P("frame", None),
            P(None, "frame"),
        ),
        check_vma=False,
    )
```

profile of v0, /device:TPU:1, one launch (start us, length us, event | category | flops | bytes accessed | tf_op | source)
XLA Modules:
  0.0 985.7 jit_solution(17115962391884468408)
XLA Ops:
  10.7 54.4 %all_gather.29 = bf16[2048,32]{1,0:T(8,128)(2,1)S(1)} all-gather(bf16[32,32]{1,0:T(8,128)(2,1)} %param.21), channel_id=1, replica_groups=mesh['frame'=64,'row'=8] {'frame'}, dimensions={0}, use_global_device_ids=true | all-gather | bytes 133120 | tf_op jit(solution)/shard_map/all_gather | solution.py:142
  65.2 34.6 %all-gather.7.cloned.1.call-done = bf16[256,4096]{0,1:T(8,128)(2,1)} async-done(((bf16[256,64]{0,1:T(8,128)(2,1)}), bf16[256,4096]{0,1:T(8,128)(2,1)}) %all-gather.7.cloned.1.call-update) | async-done | bytes 2097168 | tf_op jit(solution)/shard_map/all_gather | solution.py:144
  99.8 2.2 fusion.142
  106.5 1.6 copy.297
  108.1 1.6 convert_multiply_fusion
  109.7 1.5 copy.298
  111.2 71.5 %all-gather.9.cloned.1.call-done = bf16[2048,256]{1,0:T(8,128)(2,1)} async-done(((bf16[32,256]{1,0:T(8,128)(2,1)}), bf16[2048,256]{1,0:T(8,128)(2,1)}) %all-gather.9.cloned.1.call-update) | async-done | bytes 1048592 | tf_op jit(solution)/shard_map/all_gather | solution.py:141
  182.7 1.6 convolution_convert_fusion.8
  187.2 13.4 %all_gather.30 = bf16[8,1,32]{2,1,0:T(2,128)(2,1)S(1)} all-gather(bf16[1,1,32]{2,1,0:T(2,128)(2,1)S(1)} %get-tuple-element.263), channel_id=1, replica_groups=mesh['frame'=64,'row'=8] {'row'}, dimensions={0}, use_global_device_ids=true | all-gather | bytes 576 | tf_op jit(solution)/shard_map/all_gather | solution.py:14
  200.6 41.2 %all-gather.13.cloned.1.call-done = bf16[256,64,128]{2,1,0:T(8,128)(2,1)} async-done(((bf16[32,64,128]{2,1,0:T(8,128)(2,1)}), bf16[256,64,128]{2,1,0:T(8,128)(2,1)}) %all-gather.13.cloned.1.call-update) | async-done | bytes 4194320 | tf_op jit(solution)/shard_map/all_gather | solution.py:36
  241.9 9.4 while.28
  252.0 2.5 multiply_reduce_fusion.2
  254.6 2.0 fusion.150
  257.7 2.6 copy.283
  260.3 2.3 fusion.40
  266.1 28.2 %all_to_all.63 = bf16[64,2,2048]{2,1,0:T(2,128)(2,1)} all-to-all(bf16[64,2,2048]{2,1,0:T(2,128)(2,1)} %all_to_all.48), channel_id=1, replica_groups=mesh['frame'=64,'row'=8] {'frame'}, dimensions={0} | all-to-all | bytes 1048576 | tf_op jit(solution)/shard_map/all_to_all | solution.py:169
  294.3 5.7 all-to-all-start.2
  300.2 1.6 reshape.856
  302.5 6.9 all-to-all-done.2
  309.4 5.0 all-to-all-start.1
  314.4 2.7 add_convert_fusion.1
  317.1 7.3 all-to-all-done.1
  324.4 5.2 all-to-all-start
  329.7 2.3 copy.312
  335.2 12.2 %all-to-all-done = bf16[64,2,2048]{2,1,0:T(2,128)(2,1)} async-done(((bf16[64,2,2048]{2,1,0:T(2,128)(2,1)}), bf16[64,2,2048]{2,1,0:T(2,128)(2,1)}, u32[]{:S(2)}, u32[]{:S(2)}) %all-to-all-start) | async-done | bytes 524320 | tf_op jit(solution)/shard_map/all_to_all | solution.py:168
  347.4 2.3 copy.289
  349.7 4.2 fusion.26
  355.0 5.7 all-to-all-start.6
  360.7 2.6 fusion.27
  363.4 1.7 copy.314
  365.0 2.7 reshape.848
  367.8 2.4 copy.315
  370.8 10.0 %all-to-all-start.5 = ((bf16[64,2,2048]{2,1,0:T(2,128)(2,1)}), bf16[64,2,2048]{2,1,0:T(2,128)(2,1)}, u32[]{:S(2)}, u32[]{:S(2)}) async-start(bf16[64,2,2048]{2,1,0:T(2,128)(2,1)} %copy.315), calls=%async_computation.5 | async-start | bytes 1048576 | tf_op jit(solution)/shard_map/all_to_all | solution.py:191
  383.1 2.5 copy.307
  392.3 6.1 all-to-all-done.5
  398.4 5.7 all-to-all-start.7
  404.2 2.2 reshape.860
  406.4 3.0 convolution_add_fusion.4
  409.4 4.1 all-to-all-done.7
  413.5 2.5 fusion.3
  416.1 1.5 copy.286
  418.3 4.6 fusion.24
  424.3 1.4 copy.311
  427.2 2.9 fusion.32
  430.2 2.1 copy.302
  434.2 1.8 fusion.33
  436.1 1.7 multiply_reduce_fusion.1
  442.5 1.5 fusion
  445.6 1.6 fusion.55
  447.3 26.7 %psum.23 = bf16[4096,4]{0,1:T(4,128)(2,1)S(1)} all-reduce(bf16[4096,4]{0,1:T(4,128)(2,1)S(1)} %multiply_convert_fusion.7), channel_id=1, replica_groups=mesh['frame'=64,'row'=8] {'row'}, use_global_device_ids=true, to_apply=%region_28.29 | all-reduce | flops 16384 | bytes 65536 | tf_op jit(solution)/shard_map/psum | solution.py:230
  474.0 1.7 copy.330
  475.8 46.5 %all-reduce.8.cloned.1.call-done = (bf16[2048,256]{1,0:T(8,128)(2,1)}, bf16[2048,32]{1,0:T(8,128)(2,1)}) async-done(((bf16[2048,256]{1,0:T(8,128)(2,1)}, bf16[2048,32]{1,0:T(8,128)(2,1)}), (bf16[2048,256]{1,0:T(8,128)(2,1)}, bf16[2048,32]{1,0:T(8,128)(2,1)})) %all-reduce.8.cloned.1.call-update) | async-done | bytes 1179664 | tf_op jit(solution)/shard_map/psum | solution.py:228
  522.3 2.2 convert_element_type.502
  524.7 1.5 convert_element_type.500
  526.2 1.9 convolution_convert_fusion.3
  528.1 1.7 copy.295
  529.8 31.3 %all_to_all.64 = bf16[64,2,2048]{2,1,0:T(2,128)(2,1)S(1)} all-to-all(bf16[64,2,2048]{2,1,0:T(2,128)(2,1)S(1)} %bitcast.405), channel_id=1, replica_groups=mesh['frame'=64,'row'=8] {'frame'}, dimensions={0} | all-to-all | bytes 1048576 | tf_op jit(solution)/shard_map/all_to_all | solution.py:190
  561.3 2.8 fusion.61
  564.1 2.7 copy.287
  568.1 2.4 fusion.62
  571.8 101.1 %reduce-scatter.10.cloned.1.call-done = f32[64,4]{1,0:T(8,128)} async-done(((f32[4096,4]{1,0:T(8,128)}), f32[64,4]{1,0:T(8,128)}) %reduce-scatter.10.cloned.1.call-update) | async-done | bytes 1040
  672.9 1.6 convolution_multiply_fusion
  674.4 149.5 %reduce-scatter.8.cloned.1.call-done = f32[32,32]{1,0:T(8,128)} async-done(((f32[2048,32]{1,0:T(8,128)}), f32[32,32]{1,0:T(8,128)}) %reduce-scatter.8.cloned.1.call-update) | async-done | bytes 4112 | tf_op jit(solution)/shard_map/reduce_scatter | solution.py:234
  825.2 151.8 %reduce-scatter.6.cloned.1.call-done = f32[32,256]{1,0:T(8,128)} async-done(((f32[2048,256]{1,0:T(8,128)}), f32[32,256]{1,0:T(8,128)}) %reduce-scatter.6.cloned.1.call-update) | async-done | bytes 32784 | tf_op jit(solution)/shard_map/reduce_scatter | solution.py:233
  (227 shorter events, 57.4 us)
Async XLA Ops:
  7.2 96.1 %copy-start = (bf16[1,1,128,2048]{3,2,1,0:T(8,128)(2,1)S(1)}, bf16[1,1,128,2048]{3,2,1,0:T(8,128)(2,1)}, u32[]{:S(2)}) copy-start(bf16[1,1,128,2048]{3,2,1,0:T(8,128)(2,1)} %param.16) | copy-start | bytes 1572868
  7.2 92.6 %all-gather.7.cloned.1.call-start = ((), (), s32[]{:S(2)}) async-start(), calls=%async_computation.11 | async-start | bytes 2129920 | tf_op jit(solution)/shard_map/all_gather | solution.py:144
  7.9 174.8 %all-gather.9.cloned.1.call-start = ((), (), s32[]{:S(2)}) async-start(), calls=%async_computation.12 | async-start | bytes 1064960 | tf_op jit(solution)/shard_map/all_gather | solution.py:141
  8.7 233.2 %all-gather.13.cloned.1.call-start = ((), (), s32[]{:S(2)}) async-start(), calls=%async_computation.16 | async-start | bytes 4718592 | tf_op jit(solution)/shard_map/all_gather | solution.py:36
  10.6 93.6 %copy-start.53 = (f32[128]{0:T(128)}, f32[128]{0:T(128)S(1)}, u32[]{:S(2)}) copy-start(f32[128]{0:T(128)S(1)} %fusion.59) | copy-start | bytes 1540
  10.6 93.6 %copy-start.36 = (f32[32]{0:T(128)S(1)}, f32[32]{0:T(128)}, u32[]{:S(2)}) copy-start(f32[32]{0:T(128)} %param.22) | copy-start | bytes 388
  10.6 93.6 %copy-start.48 = (f32[32]{0:T(128)S(1)}, f32[32]{0:T(128)}, u32[]{:S(2)}) copy-start(f32[32]{0:T(128)} %param.23) | copy-start | bytes 388
  65.0 348.5 %copy-start.4 = (bf16[2048,32]{1,0:T(8,128)(2,1)}, bf16[2048,32]{1,0:T(8,128)(2,1)S(1)}, u32[]{:S(2)}) copy-start(bf16[2048,32]{1,0:T(8,128)(2,1)S(1)} %all_gather.29) | copy-start | bytes 393220
  65.1 36.8 %copy-start.37 = (f32[4,128]{1,0:T(4,128)}, f32[4,128]{1,0:T(4,128)S(1)}, u32[]{:S(2)}) copy-start(f32[4,128]{1,0:T(4,128)S(1)} %get-tuple-element.267) | copy-start | bytes 6148
  65.2 36.8 %copy-start.39 = (f32[4,128]{1,0:T(4,128)}, f32[4,128]{1,0:T(4,128)S(1)}, u32[]{:S(2)}) copy-start(f32[4,128]{1,0:T(4,128)S(1)} %get-tuple-element.268) | copy-start | bytes 6148
  104.3 3.8 copy-start.3
  111.2 74.6 %copy-start.1 = (f32[1,1,128,2048]{2,3,1,0:T(8,128)}, f32[1,1,128,2048]{2,3,1,0:T(8,128)S(1)}, u32[]{:S(2)}) copy-start(f32[1,1,128,2048]{2,3,1,0:T(8,128)S(1)} %copy.298) | copy-start | bytes 3145732
  185.8 247.1 %all-gather.11.cloned.1.call-start = ((), (), s32[]{:S(2)}) async-start(), calls=%async_computation.15 | async-start | bytes 4718592 | tf_op jit(solution)/shard_map/all_gather | solution.py:14
  187.1 64.9 %copy-start.26 = (f32[32,64]{1,0:T(8,128)}, f32[32,64]{1,0:T(8,128)S(1)}, u32[]{:S(2)}) copy-start(f32[32,64]{1,0:T(8,128)S(1)} %add.245) | copy-start | bytes 24580
  187.2 64.8 %copy-start.28 = (f32[32,64]{1,0:T(8,128)}, f32[32,64]{1,0:T(8,128)S(1)}, u32[]{:S(2)}) copy-start(f32[32,64]{1,0:T(8,128)S(1)} %mul.509) | copy-start | bytes 24580
  187.2 67.4 %copy-start.50 = (f32[32]{0:T(128)}, f32[32]{0:T(128)S(1)}, u32[]{:S(2)}) copy-start(f32[32]{0:T(128)S(1)} %get-tuple-element.262) | copy-start | bytes 388
  294.3 15.0 %all-to-all-start.2 = ((bf16[64,2,32]{2,1,0:T(2,128)(2,1)}), bf16[64,2,32]{2,1,0:T(2,128)(2,1)S(1)}, u32[]{:S(2)}, u32[]{:S(2)}) async-start(bf16[64,2,32]{2,1,0:T(2,128)(2,1)} %bitcast.34), calls=%async_computation.2 | async-start | bytes 65536 | tf_op jit(solution)/shard_map/all_to_all | solution.py:171
  309.4 15.1 %all-to-all-start.1 = ((bf16[64,2,256]{2,1,0:T(2,128)(2,1)}), bf16[64,2,256]{2,1,0:T(2,128)(2,1)S(1)}, u32[]{:S(2)}, u32[]{:S(2)}) async-start(bf16[64,2,256]{2,1,0:T(2,128)(2,1)} %all_to_all.43), calls=%async_computation.1 | async-start | bytes 131072 | tf_op jit(solution)/shard_map/all_to_all | solution.py:170
  314.4 17.6 %copy-start.47 = (f32[32]{0:T(128)S(1)}, f32[32]{0:T(128)}, u32[]{:S(2)}) copy-start(f32[32]{0:T(128)} %param.24) | copy-start | bytes 388
  324.4 23.0 %all-to-all-start = ((bf16[64,2,2048]{2,1,0:T(2,128)(2,1)}), bf16[64,2,2048]{2,1,0:T(2,128)(2,1)}, u32[]{:S(2)}, u32[]{:S(2)}) async-start(bf16[64,2,2048]{2,1,0:T(2,128)(2,1)} %add_convert_fusion.1), calls=%async_computation | async-start | bytes 1048576 | tf_op jit(solution)/shard_map/all_to_all | solution.py:168
  329.7 31.0 %copy-start.44 = (pred[64,64]{1,0:T(8,128)(4,1)}, pred[64,64]{1,0:T(8,128)(4,1)S(1)}, u32[]{:S(2)}) copy-start(pred[64,64]{1,0:T(8,128)(4,1)S(1)} %iota_compare_fusion.1) | copy-start | bytes 12292
  335.2 25.5 %copy-start.30 = (f32[2,64,64]{2,1,0:T(8,128)}, f32[2,64,64]{2,1,0:T(8,128)S(1)}, u32[]{:S(2)}) copy-start(f32[2,64,64]{2,1,0:T(8,128)S(1)} %convolution_multiply_fusion.1) | copy-start | bytes 98308
  355.0 15.8 %all-to-all-start.6 = ((bf16[64,2,256]{2,1,0:T(2,128)(2,1)}), bf16[64,2,256]{2,1,0:T(2,128)(2,1)S(1)}, u32[]{:S(2)}, u32[]{:S(2)}) async-start(bf16[64,2,256]{2,1,0:T(2,128)(2,1)} %copy.319), calls=%async_computation.6 | async-start | bytes 131072 | tf_op jit(solution)/shard_map/all_to_all | solution.py:192
  365.0 16.8 %copy-start.56 = (f32[32]{0:T(128)S(1)}, f32[32]{0:T(128)}, u32[]{:S(2)}) copy-start(f32[32]{0:T(128)} %param.25) | copy-start | bytes 388
  370.1 18.4 %copy-start.35 = (f32[2,32,64]{2,1,0:T(8,128)S(1)}, f32[2,32,64]{2,1,0:T(8,128)}, u32[]{:S(2)}) copy-start(f32[2,32,64]{2,1,0:T(8,128)} %get-tuple-element.223) | copy-start | bytes 49156
  370.8 14.8 %copy-start.23 = (bf16[64,2,256]{2,1,0:T(2,128)(2,1)}, bf16[64,2,256]{2,1,0:T(2,128)(2,1)S(1)}, u32[]{:S(2)}) copy-start(bf16[64,2,256]{2,1,0:T(2,128)(2,1)S(1)} %all-to-all-done.6) | copy-start | bytes 196612
  370.8 27.6 %all-to-all-start.5 = ((bf16[64,2,2048]{2,1,0:T(2,128)(2,1)}), bf16[64,2,2048]{2,1,0:T(2,128)(2,1)}, u32[]{:S(2)}, u32[]{:S(2)}) async-start(bf16[64,2,2048]{2,1,0:T(2,128)(2,1)} %copy.315), calls=%async_computation.5 | async-start | bytes 1048576 | tf_op jit(solution)/shard_map/all_to_all | solution.py:191
  398.4 15.1 %all-to-all-start.7 = ((bf16[64,2,32]{2,1,0:T(2,128)(2,1)}), bf16[64,2,32]{2,1,0:T(2,128)(2,1)S(1)}, u32[]{:S(2)}, u32[]{:S(2)}) async-start(bf16[64,2,32]{2,1,0:T(2,128)(2,1)} %copy.322), calls=%async_computation.7 | async-start | bytes 65536 | tf_op jit(solution)/shard_map/all_to_all | solution.py:193
  404.1 118.2 %all-reduce.8.cloned.1.call-start = ((), (), s32[]{:S(2)}) async-start(), calls=%async_computation.18 | async-start | bytes 3145728 | tf_op jit(solution)/shard_map/psum | solution.py:228
  409.4 8.2 copy-start.24
  418.3 9.0 copy-start.16
  422.9 9.4 copy-start.21
  433.0 3.1 copy-start.8
  433.0 3.1 copy-start.25
  436.0 2.0 copy-start.22
  436.1 2.1 copy-start.18
  436.1 2.1 copy-start.19
  436.1 2.1 copy-start.20
  436.1 2.1 copy-start.52
  436.1 3.3 copy-start.17
  436.1 3.3 copy-start.49
  436.1 3.3 copy-start.51
  442.5 1.9 copy-start.6
  442.5 1.9 copy-start.13
  444.1 228.8 %reduce-scatter.10.cloned.1.call-start = ((), (), s32[]{:S(2)}) async-start(), calls=%async_computation.17 | async-start | bytes 2129920
  445.6 1.6 copy-start.55
  475.8 348.1 %reduce-scatter.8.cloned.1.call-start = ((), (), s32[]{:S(2)}) async-start(), calls=%async_computation.14 | async-start | bytes 1064960 | tf_op jit(solution)/shard_map/reduce_scatter | solution.py:234
  522.3 2.3 copy-start.14
  524.5 452.5 %reduce-scatter.6.cloned.1.call-start = ((), (), s32[]{:S(2)}) async-start(), calls=%async_computation.13 | async-start | bytes 2129920 | tf_op jit(solution)/shard_map/reduce_scatter | solution.py:233
  524.6 1.5 copy-start.15
  524.6 1.5 copy-start.31
  528.0 33.2 %copy-start.11 = (f32[1,1,128,2048]{2,3,1,0:T(8,128)S(1)}, f32[1,1,128,2048]{2,3,1,0:T(8,128)}, u32[]{:S(2)}) copy-start(f32[1,1,128,2048]{2,3,1,0:T(8,128)} %copy.277) | copy-start | bytes 3145732
  528.0 33.2 %copy-start.27 = (f32[32,64]{1,0:T(8,128)S(1)}, f32[32,64]{1,0:T(8,128)}, u32[]{:S(2)}) copy-start(f32[32,64]{1,0:T(8,128)} %copy-done.26) | copy-start | bytes 24580
  528.1 33.2 %copy-start.29 = (f32[32,64]{1,0:T(8,128)S(1)}, f32[32,64]{1,0:T(8,128)}, u32[]{:S(2)}) copy-start(f32[32,64]{1,0:T(8,128)} %copy-done.28) | copy-start | bytes 24580
  528.1 33.2 %copy-start.32 = (f32[128,128]{1,0:T(8,128)S(1)}, f32[128,128]{1,0:T(8,128)}, u32[]{:S(2)}) copy-start(f32[128,128]{1,0:T(8,128)} %convolution_multiply_fusion.2) | copy-start | bytes 196612
  528.1 33.2 %copy-start.41 = (f32[32,128]{1,0:T(8,128)S(1)}, f32[32,128]{1,0:T(8,128)}, u32[]{:S(2)}) copy-start(f32[32,128]{1,0:T(8,128)} %copy.279) | copy-start | bytes 49156
  528.1 33.2 %copy-start.42 = (f32[32,128]{1,0:T(8,128)S(1)}, f32[32,128]{1,0:T(8,128)}, u32[]{:S(2)}) copy-start(f32[32,128]{1,0:T(8,128)} %copy.281) | copy-start | bytes 49156
  528.1 33.2 %copy-start.43 = (pred[128,128]{1,0:T(8,128)(4,1)S(1)}, pred[128,128]{1,0:T(8,128)(4,1)}, u32[]{:S(2)}) copy-start(pred[128,128]{1,0:T(8,128)(4,1)} %iota_compare_fusion) | copy-start | bytes 49156
  564.1 2.7 copy-start.7
  564.1 4.0 copy-start.54
  568.1 2.5 copy-start.9
  568.1 2.5 copy-start.10
  570.6 102.3 %copy-start.38 = (f32[4,128]{1,0:T(4,128)S(1)}, f32[4,128]{1,0:T(4,128)}, u32[]{:S(2)}) copy-start(f32[4,128]{1,0:T(4,128)} %copy-done.37) | copy-start | bytes 6148
  570.6 102.3 %copy-start.40 = (f32[4,128]{1,0:T(4,128)S(1)}, f32[4,128]{1,0:T(4,128)}, u32[]{:S(2)}) copy-start(f32[4,128]{1,0:T(4,128)} %copy-done.39) | copy-start | bytes 6148
  (7 other events, 8.7 us)
Sparse Core Ops, SparseCore 0:
  11.4 88.3 all-gather.6
  103.1 79.5 all-gather.8
  185.9 55.8 all-gather.12
  265.1 54.0 all-gather.10
  444.2 78.1 all-reduce.7
  526.8 145.9 reduce-scatter.9
  678.1 145.7 reduce-scatter.7
  829.2 147.7 reduce-scatter.5
where the time goes:
time: 1000 us; the launch traced here: 986 us
  waiting for transfers between devices  635 us (64%)
  blocking collectives  154 us (15%)
  local copies, waits for them, and re-layouts  56 us (6%)
  matrix products  47.3 us (5%)
  other arithmetic  39.8 us (4%)
  starting transfers between devices  38 us (4%)
  between operations  15.4 us (2%)
    reduce_scatter x1, waiting for transfers between devices, per_device(): lax.psum_scatter(proj_sum, 'frame', scatter_dimension=0, tiled=True)  152 us
    reduce_scatter x1, waiting for transfers between devices, per_device(): lax.psum_scatter(step_sum, 'frame', scatter_dimension=0, tiled=True)  150 us
    unnamed x9, waiting for transfers between devices  103 us
    all_gather x1, waiting for transfers between devices, per_device(): lax.all_gather(proj_weight, 'frame', axis=0, tiled=True)  71.5 us
    all_gather x1, blocking collectives, per_device(): lax.all_gather(step_weight, 'frame', axis=0, tiled=True)  54.4 us
    psum x1, waiting for transfers between devices, per_device(): lax.psum(proj_term.astype(jnp.bfloat16), 'row').astype(jnp.float32)  46.5 us
    all_gather x1, waiting for transfers between devices, carried_in(): lax.all_gather(a.astype(kind), axis)  41.2 us
    all_gather x1, waiting for transfers between devices, per_device(): mod_full = lax.all_gather(mod_weight, 'frame', axis=1, tiled=True)  34.6 us
  transfers between devices with their start and end apart: 14, of which 13 were waited for; matrix products, arithmetic and copies ran while one was open for 10% of the time, Pallas kernels for 0%

commit v1 on v0

v1 whole, which is shorter than its diff:
```python
import functools
import math

import jax
import jax.numpy as jnp
from jax import lax
from jax.experimental import pallas as pl
from jax.experimental.pallas import tpu as pltpu
from jax.sharding import PartitionSpec as P

norm_eps = 1e-05
MESH = pl.DeviceIdType.MESH
ANY = pl.BlockSpec(memory_space=pl.ANY)
VMEM = pl.BlockSpec(memory_space=pltpu.VMEM)
SMEM = pl.BlockSpec(memory_space=pltpu.SMEM)
CHAIN_CHUNKS = 8


def at(frame=None, row=None):
    place = {}
    if frame is not None:
        place["frame"] = frame
    if row is not None:
        place["row"] = row
    return place


def tell(sem, **place):
    pl.semaphore_signal(sem, inc=1, device_id=at(**place), device_id_type=MESH)


def push(src, dst, send_sem, recv_sem, **place):
    return pltpu.make_async_remote_copy(
        src_ref=src,
        dst_ref=dst,
        send_sem=send_sem,
        recv_sem=recv_sem,
        device_id=at(**place),
        device_id_type=MESH,
    )


def each(start, stop, body):
    def step(k, carry):
        body(k)
        return carry

    lax.fori_loop(start, stop, step, 0)


def gather_kernel(src, out, send1, recv1, send2, recv2, local_sem):
    frame = lax.axis_index("frame")
    chips = lax.axis_size("frame") // 2
    chip, core = frame // 2, frame % 2
    sibling = chip * 2 + (1 - core)
    barrier = pltpu.get_barrier_semaphore()
    each(1, chips, lambda k: tell(barrier, frame=(chip + k) % chips * 2 + core))
    tell(barrier, frame=sibling)
    own = pltpu.make_async_copy(src, out.at[frame], local_sem)
    own.start()
    pl.semaphore_wait(barrier, chips)

    def direct(k):
        peer = (chip + k) % chips * 2 + core
        return push(src, out.at[frame], send1.at[k], recv1.at[k], frame=peer)

    def relay(k):
        origin = (chip + chips - k) % chips * 2 + core
        return push(out.at[origin], out.at[origin], send2.at[k], recv2.at[k], frame=sibling)

    def first(k):
        return push(src, out.at[frame], send2.at[k], recv2.at[k], frame=sibling)

    first(0).start()
    each(1, chips, lambda k: direct(k).start())

    def pass_on(k):
        origin = (chip + chips - k) % chips * 2 + core
        push(src, out.at[origin], send1.at[k], recv1.at[k], frame=sibling).wait_recv()
        relay(k).start()

    each(1, chips, pass_on)

    def finish(k):
        origin = (chip + chips - k) % chips * 2 + (1 - core)
        push(src, out.at[origin], send2.at[k], recv2.at[k], frame=sibling).wait_recv()

    each(0, chips, finish)
    first(0).wait_send()
    each(1, chips, lambda k: direct(k).wait_send())
    each(1, chips, lambda k: relay(k).wait_send())
    own.wait()


def gather(chunk):
    count = lax.axis_size("frame")
    return pl.pallas_call(
        gather_kernel,
        out_shape=jax.ShapeDtypeStruct((count, *chunk.shape), chunk.dtype),
        in_specs=[VMEM],
        out_specs=VMEM,
        scratch_shapes=[
            pltpu.SemaphoreType.DMA((count // 2,)),
            pltpu.SemaphoreType.DMA((count // 2,)),
            pltpu.SemaphoreType.DMA((count // 2,)),
            pltpu.SemaphoreType.DMA((count // 2,)),
            pltpu.SemaphoreType.DMA,
        ],
        compiler_params=pltpu.CompilerParams(collective_id=0, has_side_effects=True),
        name="gather",
    )(chunk)


def plane_copies(frame, count, pairs, send, recv):
    def out_piece(i, k):
        peer = (frame + k) % count
        src, dst = pairs[i]
        return push(src.at[peer], dst.at[frame], send.at[i, k], recv.at[i, k], frame=peer)

    def in_piece(i, k):
        origin = (frame + count - k) % count
        src, dst = pairs[i]
        return push(src.at[origin], dst.at[origin], send.at[i, k], recv.at[i, k], frame=origin)

    return out_piece, in_piece


def plane_start(frame, count, pairs, send, recv, own_sem):
    out_piece, unused = plane_copies(frame, count, pairs, send, recv)
    for i, (src, dst) in enumerate(pairs):
        pltpu.make_async_copy(src.at[frame], dst.at[frame], own_sem.at[i]).start()

    def begin(k):
        for i in range(len(pairs)):
            out_piece(i, k).start()

    each(1, count, begin)


def plane_wait(frame, count, pairs, send, recv, own_sem):
    out_piece, in_piece = plane_copies(frame, count, pairs, send, recv)

    def end(k):
        for i in range(len(pairs)):
            in_piece(i, k).wait_recv()
            out_piece(i, k).wait_send()

    each(1, count, end)
    for i, (src, dst) in enumerate(pairs):
        pltpu.make_async_copy(src.at[frame], dst.at[frame], own_sem.at[i]).wait()


def exchange_chain_kernel(
    xs, gs, end_local, own_grad, decay, rx, rg, state_in, later, fwd_out, bwd_out, send, recv, own_sem,
    fwd_send, fwd_recv, bwd_send, bwd_recv,
):
    frame, row = lax.axis_index("frame"), lax.axis_index("row")
    count, bands = lax.axis_size("frame"), lax.axis_size("row")
    height = end_local.shape[0] // CHAIN_CHUNKS
    heads = decay.shape[0]
    per_head = end_local.shape[0] // heads
    barrier = pltpu.get_barrier_semaphore()
    each(1, count, lambda k: tell(barrier, frame=(frame + k) % count))

    @pl.when(row > 0)
    def _():
        tell(barrier, row=row - 1)

    @pl.when(row < bands - 1)
    def _():
        tell(barrier, row=row + 1)

    neighbours = jnp.where(row > 0, 1, 0) + jnp.where(row < bands - 1, 1, 0)
    pl.semaphore_wait(barrier, count - 1 + neighbours)

    def rows_of(c):
        return pl.ds(c * height, height)

    def fwd(c):
        where = rows_of(c)
        return push(fwd_out.at[where], state_in.at[where], fwd_send.at[c], fwd_recv.at[c], row=row + 1)

    def bwd(c):
        where = rows_of(c)
        return push(bwd_out.at[where], later.at[where], bwd_send.at[c], bwd_recv.at[c], row=row - 1)

    def fwd_in(c):
        where = rows_of(c)
        return push(fwd_out.at[where], state_in.at[where], fwd_send.at[c], fwd_recv.at[c], row=row - 1)

    def bwd_in(c):
        where = rows_of(c)
        return push(bwd_out.at[where], later.at[where], bwd_send.at[c], bwd_recv.at[c], row=row + 1)

    def join(c, before, own, result):
        for j in range(height // per_head):
            where = pl.ds(c * height + j * per_head, per_head)
            factor = decay[c * (height // per_head) + j]
            result[where, :] = (
                before[where, :].astype(jnp.float32) * factor + own[where, :]
            ).astype(result.dtype)

    @pl.when(row == 0)
    def _():
        state_in[...] = jnp.zeros_like(state_in)
        for c in range(CHAIN_CHUNKS):
            fwd_out[rows_of(c), :] = end_local[rows_of(c), :].astype(fwd_out.dtype)
            fwd(c).start()

    @pl.when(row == bands - 1)
    def _():
        later[...] = jnp.zeros_like(later)
        for c in range(CHAIN_CHUNKS):
            bwd_out[rows_of(c), :] = own_grad[rows_of(c), :].astype(bwd_out.dtype)
            bwd(c).start()

    plane_start(frame, count, [(xs, rx), (gs, rg)], send, recv, own_sem)
    for c in range(CHAIN_CHUNKS):

        @pl.when(row > 0)
        def _():
            fwd_in(c).wait_recv()

            @pl.when(row < bands - 1)
            def _():
                join(c, state_in, end_local, fwd_out)
                fwd(c).start()

        @pl.when(row < bands - 1)
        def _():
            bwd_in(c).wait_recv()

            @pl.when(row > 0)
            def _():
                join(c, later, own_grad, bwd_out)
                bwd(c).start()

    plane_wait(frame, count, [(xs, rx), (gs, rg)], send, recv, own_sem)

    @pl.when(row < bands - 1)
    def _():
        for c in range(CHAIN_CHUNKS):
            fwd(c).wait_send()

    @pl.when(row > 0)
    def _():
        for c in range(CHAIN_CHUNKS):
            bwd(c).wait_send()


def exchange_chain(xs, gs, end_local, own_grad, decay):
    count = lax.axis_size("frame")
    state = jax.ShapeDtypeStruct(end_local.shape, jnp.bfloat16)
    return pl.pallas_call(
        exchange_chain_kernel,
        out_shape=(
            jax.ShapeDtypeStruct(xs.shape, xs.dtype),
            jax.ShapeDtypeStruct(gs.shape, gs.dtype),
            state,
            state,
        ),
        in_specs=[ANY, ANY, VMEM, VMEM, SMEM],
        out_specs=(ANY, ANY, VMEM, VMEM),
        scratch_shapes=[
            pltpu.VMEM(end_local.shape, jnp.bfloat16),
            pltpu.VMEM(end_local.shape, jnp.bfloat16),
            pltpu.SemaphoreType.DMA((2, count)),
            pltpu.SemaphoreType.DMA((2, count)),
            pltpu.SemaphoreType.DMA((2,)),
            pltpu.SemaphoreType.DMA((CHAIN_CHUNKS,)),
            pltpu.SemaphoreType.DMA((CHAIN_CHUNKS,)),
            pltpu.SemaphoreType.DMA((CHAIN_CHUNKS,)),
            pltpu.SemaphoreType.DMA((CHAIN_CHUNKS,)),
        ],
        compiler_params=pltpu.CompilerParams(collective_id=1, has_side_effects=True),
        name="exchange_chain",
    )(xs, gs, end_local, own_grad, decay)


def back_kernel(
    ts, bs, wp, ws, rt, rb, rp, rs, send, recv, own_sem, z_send, z_recv, z_own
):
    frame, row = lax.axis_index("frame"), lax.axis_index("row")
    count, bands = lax.axis_size("frame"), lax.axis_size("row")
    share = wp.shape[0] // bands
    barrier = pltpu.get_barrier_semaphore()
    each(1, count, lambda k: tell(barrier, frame=(frame + k) % count))
    each(1, bands, lambda k: tell(barrier, row=(row + k) % bands))
    pl.semaphore_wait(barrier, count - 1 + bands - 1)

    def pieces(j):
        start = pl.multiple_of(j * share, share)
        return (wp.at[pl.ds(start, share), :], rp), (ws.at[:, pl.ds(start, share)], rs)

    def z_out(i, k):
        peer = (row + k) % bands
        src, dst = pieces(peer)[i]
        return push(src, dst.at[row], z_send.at[i, k], z_recv.at[i, k], row=peer)

    def z_in(i, k):
        origin = (row + bands - k) % bands
        src, dst = pieces(origin)[i]
        return push(src, dst.at[origin], z_send.at[i, k], z_recv.at[i, k], row=origin)

    def z_self(i):
        src, dst = pieces(row)[i]
        return pltpu.make_async_copy(src, dst.at[row], z_own.at[i])

    for i in range(2):
        z_self(i).start()

    def begin(k):
        for i in range(2):
            z_out(i, k).start()

    each(1, bands, begin)
    plane_start(frame, count, [(ts, rt), (bs, rb)], send, recv, own_sem)
    plane_wait(frame, count, [(ts, rt), (bs, rb)], send, recv, own_sem)

    def end(k):
        for i in range(2):
            z_in(i, k).wait_recv()
            z_out(i, k).wait_send()

    each(1, bands, end)
    for i in range(2):
        z_self(i).wait()


def back(ts, bs, wp, ws):
    count, bands = lax.axis_size("frame"), lax.axis_size("row")
    share = wp.shape[0] // bands
    return pl.pallas_call(
        back_kernel,
        out_shape=(
            jax.ShapeDtypeStruct(ts.shape, ts.dtype),
            jax.ShapeDtypeStruct(bs.shape, bs.dtype),
            jax.ShapeDtypeStruct((bands, share, wp.shape[1]), wp.dtype),
            jax.ShapeDtypeStruct((bands, ws.shape[0], share), ws.dtype),
        ),
        in_specs=[ANY] * 4,
        out_specs=(ANY,) * 4,
        scratch_shapes=[
            pltpu.SemaphoreType.DMA((2, count)),
            pltpu.SemaphoreType.DMA((2, count)),
            pltpu.SemaphoreType.DMA((2,)),
            pltpu.SemaphoreType.DMA((2, bands)),
            pltpu.SemaphoreType.DMA((2, bands)),
            pltpu.SemaphoreType.DMA((2,)),
        ],
        compiler_params=pltpu.CompilerParams(collective_id=2, has_side_effects=True),
        name="back",
    )(ts, bs, wp, ws)


def plane_kernel(src, out, send, recv, own_sem):
    frame, count = lax.axis_index("frame"), lax.axis_size("frame")
    barrier = pltpu.get_barrier_semaphore()
    each(1, count, lambda k: tell(barrier, frame=(frame + k) % count))
    pl.semaphore_wait(barrier, count - 1)
    plane_start(frame, count, [(src, out)], send, recv, own_sem)
    plane_wait(frame, count, [(src, out)], send, recv, own_sem)


def plane(src):
    count = lax.axis_size("frame")
    return pl.pallas_call(
        plane_kernel,
        out_shape=jax.ShapeDtypeStruct(src.shape, src.dtype),
        in_specs=[VMEM],
        out_specs=VMEM,
        scratch_shapes=[
            pltpu.SemaphoreType.DMA((1, count)),
            pltpu.SemaphoreType.DMA((1, count)),
            pltpu.SemaphoreType.DMA((1,)),
        ],
        compiler_params=pltpu.CompilerParams(collective_id=3, has_side_effects=True),
        name="plane",
    )(src)


def deliver_kernel(weights, mods, rw, rm, w_send, w_recv, w_own, m_send, m_recv, m_own):
    frame, row = lax.axis_index("frame"), lax.axis_index("row")
    count, bands = lax.axis_size("frame"), lax.axis_size("row")
    per = count // bands
    home = row * per + frame // bands
    slot = frame % bands
    from_row, from_frame = frame // per, (frame % per) * bands
    barrier = pltpu.get_barrier_semaphore()

    def other(f, r):
        return jnp.logical_or(f != frame, r != row)

    def ready(i):
        @pl.when(other(from_frame + i, from_row))
        def _():
            tell(barrier, frame=from_frame + i, row=from_row)

    each(0, bands, ready)
    each(1, bands, lambda k: tell(barrier, row=(row + k) % bands))
    local = jnp.where(home == frame, 1, 0)
    pl.semaphore_wait(barrier, bands - local + bands - 1)

    def w_out(r):
        return push(weights, rw.at[slot], w_send.at[r], w_recv.at[slot], frame=home, row=r)

    def w_in(i):
        return push(weights, rw.at[i], w_send.at[i], w_recv.at[i], frame=from_frame + i, row=from_row)

    w_self = pltpu.make_async_copy(weights, rw.at[slot], w_own)
    m_self = pltpu.make_async_copy(mods, rm.at[row], m_own)
    m_self.start()

    def m_out(k):
        return push(mods, rm.at[row], m_send.at[k], m_recv.at[k], row=(row + k) % bands)

    def m_in(k):
        origin = (row + bands - k) % bands
        return push(mods, rm.at[origin], m_send.at[k], m_recv.at[k], row=origin)

    def start_weights(r):
        @pl.when(other(home, r))
        def _():
            w_out(r).start()

        @pl.when(jnp.logical_not(other(home, r)))
        def _():
            w_self.start()

    each(0, bands, start_weights)
    each(1, bands, lambda k: m_out(k).start())

    def end_weights(i):
        @pl.when(other(from_frame + i, from_row))
        def _():
            w_in(i).wait_recv()

        @pl.when(jnp.logical_not(other(from_frame + i, from_row)))
        def _():
            w_self.wait()

        @pl.when(other(home, i))
        def _():
            w_out(i).wait_send()

    each(0, bands, end_weights)

    def end_mods(k):
        m_in(k).wait_recv()
        m_out(k).wait_send()

    each(1, bands, end_mods)
    m_self.wait()


def deliver(weights, mods):
    bands = lax.axis_size("row")
    return pl.pallas_call(
        deliver_kernel,
        out_shape=(
            jax.ShapeDtypeStruct((bands, *weights.shape), weights.dtype),
            jax.ShapeDtypeStruct((bands, *mods.shape), mods.dtype),
        ),
        in_specs=[VMEM, VMEM],
        out_specs=(VMEM, VMEM),
        scratch_shapes=[
            pltpu.SemaphoreType.DMA((bands,)),
            pltpu.SemaphoreType.DMA((bands,)),
            pltpu.SemaphoreType.DMA,
            pltpu.SemaphoreType.DMA((bands,)),
            pltpu.SemaphoreType.DMA((bands,)),
            pltpu.SemaphoreType.DMA,
        ],
        compiler_params=pltpu.CompilerParams(collective_id=4, has_side_effects=True),
        name="deliver",
    )(weights, mods)


def time_embed(timestep, embed_dim):
    half_dim = embed_dim // 2
    frequency = jnp.exp(-math.log(10000.0) * jnp.arange(half_dim, dtype=jnp.float32) / half_dim)
    angles = timestep.astype(jnp.float32)[:, None] * frequency[None, :]
    return jax.nn.silu(jnp.concatenate([jnp.cos(angles), jnp.sin(angles)], axis=1))


def running_sum(values):
    length = values.shape[1]
    lower = jnp.tril(jnp.ones((length, length), jnp.float32))
    return jnp.einsum("tu,suh->sth", lower, values, precision=lax.Precision.HIGHEST)


def block_parts(normed, coeffs, logits, step_bias, decay_rate, need_end):
    seq_count, length, feat_width = normed.shape
    head_count = decay_rate.shape[0]
    inputs = normed.reshape(seq_count, length, head_count, feat_width // head_count)
    state_size = coeffs.shape[-1] // 2
    b_part = coeffs[..., :state_size]
    c_part = coeffs[..., state_size:]
    step_size = jax.nn.softplus(logits.astype(jnp.float32) + step_bias)
    cum_log = running_sum(-step_size * decay_rate)
    scores = (
        jnp.einsum("stn,sun->stu", c_part, b_part, preferred_element_type=jnp.float32) / state_size
    )
    lag_rows = jnp.swapaxes(cum_log, 1, 2)
    causal = jnp.tril(jnp.ones((length, length), dtype=bool))
    differences = lag_rows[:, :, :, None] - lag_rows[:, :, None, :]
    decays = jnp.where(causal, jnp.exp(jnp.where(causal, differences, 0.0)), 0.0)
    spread = jnp.swapaxes(step_size, 1, 2)
    weights = (scores[:, None, :, :] * decays * spread[:, :, None, :]).astype(jnp.bfloat16)
    inner_out = jnp.einsum("shtu,suhp->sthp", weights, inputs, preferred_element_type=jnp.float32)
    inner_out = inner_out.reshape(seq_count, length, feat_width)
    if need_end:
        end_log = cum_log[:, -1:, :]
        lead_decay = jnp.exp(end_log - cum_log) * step_size
        scaled = (inputs.astype(jnp.float32) * lead_decay[..., None]).astype(jnp.bfloat16)
        end_local = jnp.einsum("sthp,stn->shpn", scaled, b_part, preferred_element_type=jnp.float32)
    else:
        end_local = jnp.zeros(
            (seq_count, head_count, feat_width // head_count, state_size), jnp.float32
        )
    return (inner_out, end_local, cum_log, c_part)


def carry_term(cum_log, c_part, state_in):
    seq_count, length, head_count = cum_log.shape
    state_size = c_part.shape[-1]
    reached = jnp.einsum(
        "stn,shpn->sthp", c_part.astype(jnp.float32), state_in, precision=lax.Precision.HIGHEST
    )
    return (reached * jnp.exp(cum_log)[..., None] / state_size).reshape(seq_count, length, -1)


def three_parts(values):
    first = lax.reduce_precision(values, 8, 7)
    second = lax.reduce_precision(values - first, 8, 7)
    return first, second, values - first - second


def per_device(
    tokens,
    cotangent,
    timestep,
    mod_weight,
    proj_weight,
    step_weight,
    step_bias,
    rate_space,
    rate_time,
    skip_gain,
):
    frame_count = lax.axis_size("frame")
    row_count = lax.axis_size("row")
    frame_id = lax.axis_index("frame")
    feat_width = tokens.shape[-1]
    band_len = tokens.shape[1] * tokens.shape[2]
    clip_count = timestep.shape[0]
    clip_frames = frame_count // clip_count
    site_count = band_len // frame_count
    head_count = rate_space.shape[0]
    state_size = proj_weight.shape[1] // 2
    depth = proj_weight.shape[0]
    clip_id = frame_id // clip_frames
    factor = (frame_count * row_count * band_len) ** (-0.5)
    tokens = tokens.reshape(band_len, feat_width)
    flat_grad = cotangent.reshape(band_len, feat_width)

    activated = time_embed(timestep, mod_weight.shape[0]).astype(jnp.bfloat16)
    mod_cols = jnp.dot(activated, mod_weight, preferred_element_type=jnp.float32)
    lane = state_size
    mod_rows = [part.reshape(-1, lane).astype(jnp.bfloat16) for part in three_parts(mod_cols)]
    rows = [proj_weight[:, :state_size], proj_weight[:, state_size:], step_weight.reshape(-1, lane), *mod_rows]
    used = sum(r.shape[0] for r in rows)
    chunk = jnp.concatenate([*rows, jnp.zeros((-used % 16, lane), jnp.bfloat16)], axis=0)
    gathered = gather(chunk)
    b_weight = gathered[:, :depth].reshape(feat_width, state_size)
    c_weight = gathered[:, depth : 2 * depth].reshape(feat_width, state_size)
    proj_full = jnp.concatenate([b_weight, c_weight], axis=1)
    step_rows = depth * head_count // lane
    step_full = gathered[:, 2 * depth : 2 * depth + step_rows].reshape(feat_width, head_count)
    mod_height = mod_rows[0].shape[0]
    mod_parts = gathered[:, 2 * depth + step_rows : 2 * depth + step_rows + 3 * mod_height]
    mod_parts = mod_parts.astype(jnp.float32).reshape(frame_count, 3, clip_count, -1)
    modulation = mod_parts[:, 0] + mod_parts[:, 1] + mod_parts[:, 2]
    modulation = modulation.transpose(1, 0, 2).reshape(clip_count, 2 * feat_width)
    shift_all, scale_all = modulation[:, :feat_width], modulation[:, feat_width:]
    shift_vec = lax.dynamic_index_in_dim(shift_all, clip_id, 0, keepdims=False)
    scale_vec = lax.dynamic_index_in_dim(scale_all, clip_id, 0, keepdims=False)

    tokens_wide = tokens.astype(jnp.float32)
    inverse = lax.rsqrt(jnp.mean(tokens_wide * tokens_wide, axis=-1, keepdims=True) + norm_eps)
    unit_rows = tokens_wide * inverse
    normed = (unit_rows * (1.0 + scale_vec) + shift_vec).astype(jnp.bfloat16)
    projected = jnp.dot(normed, proj_full, preferred_element_type=jnp.float32).astype(jnp.bfloat16)
    logits = jnp.dot(normed, step_full, preferred_element_type=jnp.float32).astype(jnp.bfloat16)
    skip_full = jnp.repeat(skip_gain, feat_width // head_count)
    upstream = flat_grad.astype(jnp.float32)

    def space_parts(normed_band, proj_band, logit_band):
        return block_parts(normed_band, proj_band, logit_band, step_bias, rate_space, True)

    parts_out, parts_pull = jax.vjp(space_parts, normed[None], projected[None], logits[None])
    inner_out, end_local, cum_log, c_part = parts_out
    end_decay = jnp.exp(cum_log[:, -1, :])
    by_head = upstream.reshape(band_len, head_count, -1) * jnp.exp(cum_log[0])[..., None] / state_size
    own_grad = jnp.einsum(
        "thp,tn->hpn",
        by_head.astype(jnp.bfloat16),
        c_part[0],
        preferred_element_type=jnp.float32,
    )
    site_tokens, site_grad, state_in, later_grad = exchange_chain(
        tokens.reshape(frame_count, site_count, feat_width),
        flat_grad.reshape(frame_count, site_count, feat_width),
        end_local.reshape(feat_width, state_size),
        own_grad.reshape(feat_width, state_size),
        end_decay.reshape(head_count),
    )
    state_in = state_in.reshape(end_local.shape).astype(jnp.float32)
    later_grad = later_grad.reshape(end_local.shape).astype(jnp.float32)

    site_wide = site_tokens.astype(jnp.float32)
    site_unit = site_wide * lax.rsqrt(jnp.mean(site_wide * site_wide, axis=-1, keepdims=True) + norm_eps)
    by_clip = site_unit.reshape(clip_count, -1, feat_width)
    site_normed = (by_clip * (1.0 + scale_all[:, None, :]) + shift_all[:, None, :]).astype(jnp.bfloat16)
    site_normed = site_normed.reshape(frame_count * site_count, feat_width)
    site_proj = jnp.dot(site_normed, proj_full, preferred_element_type=jnp.float32).astype(jnp.bfloat16)
    site_logits = jnp.dot(site_normed, step_full, preferred_element_type=jnp.float32).astype(jnp.bfloat16)

    def to_seq(member):
        return member.reshape(frame_count, site_count, member.shape[-1]).transpose(1, 0, 2)

    def from_seq(member):
        return member.transpose(1, 0, 2).reshape(frame_count * site_count, member.shape[-1])

    def time_path(normed_seq, proj_seq, logit_seq):
        return block_parts(normed_seq, proj_seq, logit_seq, step_bias, rate_time, False)[0]

    time_out, time_pull = jax.vjp(time_path, to_seq(site_normed), to_seq(site_proj), to_seq(site_logits))
    time_dnorm, time_dproj, time_dlogit = time_pull(to_seq(site_grad).astype(jnp.float32))
    time_dnorm, time_dproj, time_dlogit = from_seq(time_dnorm), from_seq(time_dproj), from_seq(time_dlogit)
    time_back = (
        time_dnorm.astype(jnp.float32)
        + jnp.dot(time_dproj, proj_full.T, preferred_element_type=jnp.float32)
        + jnp.dot(time_dlogit, step_full.T, preferred_element_type=jnp.float32)
    ).astype(jnp.bfloat16)

    carried, carry_pull = jax.vjp(carry_term, cum_log, c_part, state_in)
    space_out = (inner_out + carried)[0]
    carry_dcum, carry_dc, unused = carry_pull(upstream[None])
    end_dlog = jnp.sum(later_grad * state_in, axis=(2, 3)) * end_decay
    carry_dcum = carry_dcum.at[:, -1, :].add(end_dlog)
    space_dnorm, space_dproj, space_dlogit = parts_pull(
        (upstream[None], later_grad, carry_dcum, carry_dc)
    )
    proj_term = jnp.dot(
        normed.T, space_dproj[0], preferred_element_type=jnp.float32
    ) + jnp.dot(site_normed.T, time_dproj, preferred_element_type=jnp.float32)
    step_term = jnp.dot(
        space_dlogit[0].T, normed, preferred_element_type=jnp.float32
    ) + jnp.dot(time_dlogit.T, site_normed, preferred_element_type=jnp.float32)
    frame_time, frame_back, proj_parts, step_parts = back(
        from_seq(time_out.astype(jnp.bfloat16)).reshape(frame_count, site_count, feat_width),
        time_back.reshape(frame_count, site_count, feat_width),
        proj_term.astype(jnp.bfloat16),
        step_term.astype(jnp.bfloat16),
    )
    frame_time = frame_time.reshape(band_len, feat_width)
    frame_back = frame_back.reshape(band_len, feat_width)
    mixed = (
        space_out + frame_time.astype(jnp.float32) + skip_full * normed.astype(jnp.float32)
    ).astype(jnp.bfloat16)
    skip_dnorm = (upstream * skip_full).astype(jnp.bfloat16)
    total_dnorm = space_dnorm[0] + skip_dnorm
    pre_grad = (
        total_dnorm.astype(jnp.float32)
        + jnp.dot(space_dproj[0], proj_full.T, preferred_element_type=jnp.float32)
        + jnp.dot(space_dlogit[0], step_full.T, preferred_element_type=jnp.float32)
        + frame_back.astype(jnp.float32)
    )
    shift_grad = jnp.sum(pre_grad, axis=0)
    scale_grad = jnp.sum(pre_grad * unit_rows, axis=0)
    unit_grad = pre_grad * (1.0 + scale_vec)
    d_tokens = inverse * (unit_grad - unit_rows * jnp.mean(unit_grad * unit_rows, axis=-1, keepdims=True))

    proj_sum = jnp.sum(proj_parts.astype(jnp.float32), axis=0).reshape(frame_count, -1)
    step_sum = jnp.sum(step_parts.astype(jnp.float32), axis=0).T.reshape(frame_count, -1)
    mod_term = jnp.concatenate([shift_grad, scale_grad]).reshape(frame_count, -1)
    payload = jnp.concatenate([proj_sum, step_sum, mod_term], axis=1)
    payload = jnp.pad(payload, ((0, 0), (0, -payload.shape[1] % (16 * lane))))
    arrived = plane(payload.reshape(frame_count, -1, lane).astype(jnp.bfloat16)).astype(jnp.float32)
    by_clip = jnp.sum(arrived.reshape(clip_count, clip_frames, *arrived.shape[1:]), axis=1)
    weight_sum = jnp.sum(by_clip, axis=0)
    mod_start = proj_sum.shape[1] + step_sum.shape[1]
    mod_width = mod_term.shape[1]
    mod_part = by_clip.reshape(clip_count, -1)[:, mod_start : mod_start + mod_width]
    mod_box = jnp.pad(mod_part, ((0, -clip_count % 8), (0, -mod_width % 128)))
    weight_box, mod_boxes = deliver(weight_sum, mod_box)
    weight_flat = weight_box.reshape(row_count, -1)
    grad_proj = weight_flat[:, : proj_sum.shape[1]].reshape(depth, 2 * state_size) * factor
    grad_step = weight_flat[:, proj_sum.shape[1] : mod_start].reshape(depth, head_count) * factor
    mod_sum = jnp.sum(mod_boxes, axis=0)[:clip_count, :mod_width]
    grad_mod = (
        jnp.dot(activated.astype(jnp.float32).T, mod_sum, precision=lax.Precision.HIGHEST) * factor
    )
    shape = cotangent.shape
    return (
        mixed.reshape(shape),
        d_tokens.astype(jnp.bfloat16).reshape(shape),
        grad_proj,
        grad_step,
        grad_mod,
    )


def solution(mesh):
    placed = (
        P("frame", "row", None, None),
        P("frame", "row", None, None),
        P(),
        P(None, "frame"),
        P("frame", None),
        P("frame", None),
        P(),
        P(),
        P(),
        P(),
    )
    return jax.shard_map(
        per_device,
        mesh=mesh,
        in_specs=placed,
        out_specs=(
            P("frame", "row", None, None),
            P("frame", "row", None, None),
            P("frame", None),
            P("frame", None),
            P(None, "frame"),
        ),
        check_vma=False,
    )
```

time: 1000 us -> 501 us (0.50); the launches traced: 986 us -> 497 us
  waiting for transfers between devices: 635 us -> 0 us
  Pallas kernels: 0 us -> 386 us
  blocking collectives: 154 us -> 0 us
  starting transfers between devices: 38 us -> 0 us
  other arithmetic: 39.8 us -> 22.5 us
  between operations: 15.4 us -> 1.67 us
  local copies, waits for them, and re-layouts: 56 us -> 43.8 us
    pallas_call x0 -> x5, Pallas kernels: none -> 386 us  [the longest x1 226 us: exchange_chain(): pl.pallas_call(exchange_chain_kernel, out_shape=(jax.ShapeDtypeStruct(xs....]
    reduce_scatter x2 -> x0, waiting for transfers between devices: 301 us -> none  [the longest x1 152 us: per_device(): lax.psum_scatter(proj_sum, 'frame', scatter_dimension=0, tiled=True)]
    all_gather x4 -> x0, waiting for transfers between devices: 147 us -> none  [the longest x1 71.5 us: per_device(): lax.all_gather(proj_weight, 'frame', axis=0, tiled=True)]
    unnamed x9 -> x0, waiting for transfers between devices: 103 us -> none
    all_gather x2 -> x0, blocking collectives: 67.7 us -> none  [the longest x1 54.4 us: per_device(): lax.all_gather(step_weight, 'frame', axis=0, tiled=True)]
    all_to_all x2 -> x0, blocking collectives: 59.5 us -> none  [the longest x1 31.3 us: per_device(): lax.all_to_all(time_low, 'frame', split_axis=0, concat_axis=0, tiled=True)]
    psum x1 -> x0, waiting for transfers between devices: 46.5 us -> none  [per_device(): lax.psum(proj_term.astype(jnp.bfloat16), 'row').astype(jnp.float32)]
    all_to_all x6 -> x0, starting transfers between devices: 37.4 us -> none  [the longest x1 9.98 us: per_device(): lax.all_to_all(from_seq(time_dnorm), 'frame', split_axis=0, concat_axis=0...]
  transfers between devices with their start and end apart: 14 -> 0, of which waited for: 13 -> 0; matrix products, arithmetic and copies ran while one was open for 10% -> 0% of each run, Pallas kernels for 0% -> 0%
where the time goes in v1:
time: 501 us; the launch traced here: 497 us
  Pallas kernels  386 us (77%)
  local copies, waits for them, and re-layouts  43.8 us (9%)
  matrix products  42.4 us (8%)
  other arithmetic  22.5 us (4%)
    pallas_call x1, Pallas kernels, exchange_chain(): pl.pallas_call(exchange_chain_kernel, out_shape=(jax.ShapeDtypeStruct(xs....  226 us
    pallas_call x1, Pallas kernels, back(): pl.pallas_call(back_kernel, out_shape=(jax.ShapeDtypeStruct(ts.shape, ts....  99.7 us
    pallas_call x1, Pallas kernels, gather(): pl.pallas_call(gather_kernel, out_shape=jax.ShapeDtypeStruct((count, *chu...  29.9 us
    pallas_call x1, Pallas kernels, plane(): pl.pallas_call(plane_kernel, out_shape=jax.ShapeDtypeStruct(src.shape, sr...  20.1 us
    dot_general x6, matrix products, block_parts(): jnp.einsum('shtu,suhp->sthp', weights, inputs, preferred_element_type=jnp...  17.7 us
    pallas_call x1, Pallas kernels, deliver(): pl.pallas_call(deliver_kernel, out_shape=(jax.ShapeDtypeStruct((bands, *w...  11.3 us

profile of v1, /device:TPU:1, one launch (start us, length us, event | category | flops | bytes accessed | tf_op | source)
XLA Modules:
  0.0 496.8 jit_solution(5101955258443999535)
XLA Ops:
  0.7 0.7 convert_element_type.417
  2.1 0.7 fusion.204
  2.8 0.8 reshape.744
  3.6 2.4 concatenate.25.src
  6.0 29.9 %gather.1 = bf16[64,80,128]{2,1,0:T(8,128)(2,1)} custom-call(bf16[80,128]{1,0:T(8,128)(2,1)} %concatenate.25.src), custom_call_target="tpu_custom_call" | custom-call | tf_op jit(solution)/shard_map/gather/pallas_call | solution.py:97
  35.9 1.1 slice_convert_fusion
  37.9 0.7 fusion.200
  41.4 1.3 fusion.125.own_grad
  43.0 1.4 multiply_convert_fusion.5
  44.4 1.3 fusion.121.end_local
  46.2 1.1 reshape_reshape.7.xs
  47.4 1.1 reshape_reshape.8.gs
  48.5 225.5 %exchange_chain.1 = (bf16[64,2,2048]{2,1,0:T(2,128)(2,1)}, bf16[64,2,2048]{2,1,0:T(2,128)(2,1)}, bf16[2048,128]{1,0:T(8,128)(2,1)}, bf16[2048,128]{1,0:T(8,128)(2,1)}) custom-call(bf16[64,2,2048]{2,1,0:T(2,128)(2,1)} %reshape_reshape.7.xs, bf16[64,2,2048]{2,1,0:T(2,128)(2,1)} %reshape_reshape.8.gs, f32[2048,128]{1,0:T(8,128)} %fusion.121.end_local, ...), custom_call_target="tpu_custom_call" | custom-call | tf_op jit(solution)/shard_map/exchange_chain/pallas_call | solution.py:254
  274.0 2.6 multiply_reduce_fusion.4
  277.1 2.9 fusion.31
  280.0 2.1 copy.178
  282.1 3.5 fusion.23
  285.7 1.4 copy.169
  287.0 2.4 convert_multiply_fusion.6
  289.5 2.5 copy.170
  292.0 2.2 fusion.33
  294.6 1.3 copy.172
  296.0 2.4 fusion.55
  298.3 2.0 copy.173
  300.4 1.5 fusion.39
  302.1 2.6 convolution_add_fusion.3
  304.7 1.3 multiply_multiply_fusion
  307.4 1.0 fusion.53
  308.5 1.1 fusion.74
  310.3 1.9 convert_multiply_fusion.4
  312.1 1.7 reshape.757
  313.8 1.3 fusion.61
  315.6 0.8 convolution_multiply_fusion.1
  316.3 0.7 reshape.759
  318.1 0.7 reshape.756
  318.8 1.7 reshape.760
  320.5 4.0 fusion.25
  324.8 0.9 fusion.5.ws
  326.8 1.4 fusion.wp
  328.3 2.8 fusion.26
  331.1 2.9 copy.164
  334.0 1.9 reshape.781
  337.3 1.1 reshape.763.bs
  338.4 2.4 convolution_convert_fusion.3
  340.9 2.3 copy.183
  343.2 99.7 %back.1 = (bf16[64,2,2048]{2,1,0:T(2,128)(2,1)}, bf16[64,2,2048]{2,1,0:T(2,128)(2,1)}, bf16[8,256,256]{2,1,0:T(8,128)(2,1)}, bf16[8,32,256]{2,1,0:T(8,128)(2,1)}) custom-call(bf16[64,2,2048]{2,1,0:T(2,128)(2,1)} %bitcast.404, bf16[64,2,2048]{2,1,0:T(2,128)(2,1)} %reshape.763.bs, bf16[2048,256]{1,0:T(8,128)(2,1)} %fusion.wp, bf16[32,2048]{1,0:T(8,128)(2,1)} %fusion.5.ws), custom_call_target="tpu_custom_call" | custom-call | tf_op jit(solution)/shard_map/back/pallas_call | solution.py:333
  442.9 1.2 reshape.785
  444.1 1.5 multiply_reduce_fusion
  445.8 1.5 reduce.19
  447.7 0.7 copy.187
  448.4 20.1 %plane.1 = bf16[64,16,128]{2,1,0:T(8,128)(2,1)} custom-call(bf16[64,16,128]{2,1,0:T(8,128)(2,1)} %bitcast.414), custom_call_target="tpu_custom_call" | custom-call | tf_op jit(solution)/shard_map/plane/pallas_call | solution.py:367
  468.5 1.0 bitcast_reduce_fusion
  470.2 1.6 convert_reduce_fusion.weights
  471.8 11.3 %deliver.1 = (f32[8,16,128]{2,1,0:T(8,128)}, f32[8,8,128]{2,1,0:T(8,128)}) custom-call(f32[16,128]{1,0:T(8,128)} %convert_reduce_fusion.weights, f32[8,128]{1,0:T(8,128)} %pad.32.mods), custom_call_target="tpu_custom_call" | custom-call | tf_op jit(solution)/shard_map/deliver/pallas_call | solution.py:458
  483.0 0.9 copy.208
  483.9 0.6 mul.570
  484.6 0.7 mul.573
  485.2 0.8 reduce_sum.274
  486.0 0.9 convolution_multiply_fusion
  486.9 1.1 fusion.68
  488.2 1.6 copy.154
  489.8 1.9 fusion.66
  491.8 2.6 copy.153
  494.4 2.4 fusion.57
  (192 shorter events, 13.6 us)
Async XLA Ops:
  0.6 0.8 copy-start
  1.4 0.5 copy-start.41
  1.5 0.6 copy-start.43
  35.9 2.7 copy-start.6
  35.9 2.8 copy-start.1
  38.7 0.8 copy-start.7
  38.7 1.1 copy-start.10
  38.7 1.1 slice-start
  38.9 1.1 copy-start.45
  38.9 1.5 copy-start.48
  38.9 2.0 copy-start.2
  40.0 1.3 copy-start.3
  276.7 3.3 copy-start.30
  276.8 5.3 %copy-start.35 = (f32[32,128]{1,0:T(8,128)}, f32[32,128]{1,0:T(8,128)S(1)}, u32[]{:S(2)}) copy-start(f32[32,128]{1,0:T(8,128)S(1)} %fusion.196) | copy-start | bytes 49156
  276.8 3.2 copy-start.37
  277.1 5.0 %copy-start.24 = (bf16[128,32,64]{0,2,1:T(8,128)(2,1)S(1)}, bf16[128,32,64]{0,2,1:T(8,128)(2,1)}, u32[]{:S(2)}) copy-start(bf16[128,32,64]{0,2,1:T(8,128)(2,1)} %get-tuple-element.49) | copy-start | bytes 1572868
  287.0 5.0 %copy-start.13 = (bf16[2048,128]{1,0:T(8,128)(2,1)S(1)}, bf16[2048,128]{1,0:T(8,128)(2,1)}, u32[]{:S(2)}) copy-start(bf16[2048,128]{1,0:T(8,128)(2,1)} %get-tuple-element.27) | copy-start | bytes 1572868
  296.0 6.0 %copy-start.47 = (f32[32]{0:T(128)S(1)}, f32[32]{0:T(128)}, u32[]{:S(2)}) copy-start(f32[32]{0:T(128)} %param.21) | copy-start | bytes 388
  296.0 6.1 %copy-start.8 = (bf16[64,32,128]{2,1,0:T(8,128)(2,1)S(1)}, bf16[64,32,128]{2,1,0:T(8,128)(2,1)}, u32[]{:S(2)}) copy-start(bf16[64,32,128]{2,1,0:T(8,128)(2,1)} %copy-done.7) | copy-start | bytes 1572868
  296.0 6.1 %copy-start.11 = (bf16[64,32,128]{2,1,0:T(8,128)(2,1)S(1)}, bf16[64,32,128]{2,1,0:T(8,128)(2,1)}, u32[]{:S(2)}) copy-start(bf16[64,32,128]{2,1,0:T(8,128)(2,1)} %copy-done.10) | copy-start | bytes 1572868
  302.1 2.6 copy-start.14
  304.7 1.5 copy-start.15
  304.7 2.8 copy-start.49
  304.7 4.9 copy-start.19
  306.2 4.1 copy-start.20
  308.4 3.7 copy-start.39
  315.5 1.7 copy-start.4
  316.3 1.4 copy-start.46
  316.3 1.5 copy-start.50
  317.1 1.1 copy-start.18
  317.2 1.6 copy-start.26
  317.8 6.7 %copy-start.33 = (f32[2,32,64]{2,1,0:T(8,128)}, f32[2,32,64]{2,1,0:T(8,128)S(1)}, u32[]{:S(2)}) copy-start(f32[2,32,64]{2,1,0:T(8,128)S(1)} %compare_select_fusion.3) | copy-start | bytes 49156
  318.1 6.4 %copy-start.51 = (f32[2,32,64]{2,1,0:T(8,128)}, f32[2,32,64]{2,1,0:T(8,128)S(1)}, u32[]{:S(2)}) copy-start(f32[2,32,64]{2,1,0:T(8,128)S(1)} %fusion.98) | copy-start | bytes 49156
  318.8 5.7 %copy-start.21 = (bf16[2,64,32,64]{3,2,0,1:T(8,128)(2,1)}, bf16[2,64,32,64]{3,2,0,1:T(8,128)(2,1)S(1)}, u32[]{:S(2)}) copy-start(bf16[2,64,32,64]{3,2,0,1:T(8,128)(2,1)S(1)} %reshape.756) | copy-start | bytes 1572868
  320.5 4.3 copy-start.28
  326.6 1.6 copy-start.32
  326.6 1.6 copy-start.34
  326.7 1.6 copy-start.52
  326.8 1.5 copy-start.23
  331.1 4.8 copy-start.9
  331.1 4.8 copy-start.12
  335.9 1.0 copy-start.5
  337.0 1.5 copy-start.22
  343.1 100.9 %copy-start.16 = (f32[128,2048]{1,0:T(8,128)S(1)}, f32[128,2048]{1,0:T(8,128)}, u32[]{:S(2)}) copy-start(f32[128,2048]{1,0:T(8,128)} %convolution_add_fusion.3) | copy-start | bytes 3145732
  343.1 100.9 %copy-start.40 = (bf16[128,32]{0,1:T(8,128)(2,1)S(1)}, bf16[128,32]{0,1:T(8,128)(2,1)}, u32[]{:S(2)}) copy-start(bf16[128,32]{0,1:T(8,128)(2,1)} %copy-done.39) | copy-start | bytes 24580
  444.1 3.3 copy-start.29
  445.8 40.2 %copy-start.42 = (f32[4,128]{1,0:T(4,128)S(1)}, f32[4,128]{1,0:T(4,128)}, u32[]{:S(2)}) copy-start(f32[4,128]{1,0:T(4,128)} %copy-done.41) | copy-start | bytes 6148
  445.8 40.2 %copy-start.44 = (f32[4,128]{1,0:T(4,128)S(1)}, f32[4,128]{1,0:T(4,128)}, u32[]{:S(2)}) copy-start(f32[4,128]{1,0:T(4,128)} %copy-done.43) | copy-start | bytes 6148
  445.8 41.1 %copy-start.17 = (f32[128,2048]{1,0:T(8,128)S(1)}, f32[128,2048]{1,0:T(8,128)}, u32[]{:S(2)}) copy-start(f32[128,2048]{1,0:T(8,128)} %get-tuple-element.78) | copy-start | bytes 3145732
  447.7 40.3 %copy-start.27 = (bf16[64,2,2048]{2,1,0:T(2,128)(2,1)S(1)}, bf16[64,2,2048]{2,1,0:T(2,128)(2,1)}, u32[]{:S(2)}) copy-start(bf16[64,2,2048]{2,1,0:T(2,128)(2,1)} %get-tuple-element.31) | copy-start | bytes 1572868
  488.0 1.8 copy-start.25
  488.0 1.8 copy-start.31
  488.0 1.8 copy-start.36
  488.0 1.8 copy-start.38

commit v2 on v1

v2 whole, which is shorter than its diff:
```python
import functools
import math

import jax
import jax.numpy as jnp
from jax import lax
from jax.experimental import pallas as pl
from jax.experimental.pallas import tpu as pltpu
from jax.sharding import PartitionSpec as P

norm_eps = 1e-05
MESH = pl.DeviceIdType.MESH
ANY = pl.BlockSpec(memory_space=pl.ANY)
VMEM = pl.BlockSpec(memory_space=pltpu.VMEM)
SMEM = pl.BlockSpec(memory_space=pltpu.SMEM)
CHAIN_CHUNKS = 16
CHAIN_LAG = 6
PLANE_WIDE = 4
PLANE_AHEAD = 8
PLANE_LATEST = 24


def at(frame=None, row=None):
    place = {}
    if frame is not None:
        place["frame"] = frame
    if row is not None:
        place["row"] = row
    return place


def tell(sem, **place):
    pl.semaphore_signal(sem, inc=1, device_id=at(**place), device_id_type=MESH)


def push(src, dst, send_sem, recv_sem, **place):
    return pltpu.make_async_remote_copy(
        src_ref=src,
        dst_ref=dst,
        send_sem=send_sem,
        recv_sem=recv_sem,
        device_id=at(**place),
        device_id_type=MESH,
    )


def each(start, stop, body):
    def step(k, carry):
        body(k)
        return carry

    lax.fori_loop(start, stop, step, 0)


def gather_kernel(src, out, y_send, y_recv, x_send, x_recv, c_send, c_recv, local_sem):
    high, wide = out.shape[0], out.shape[1]
    frame = lax.axis_index("frame")
    core, x, y = frame % 2, frame // 2 % wide, frame // (2 * wide)

    def index(y, x, core):
        return (y * wide + x) * 2 + core

    sibling = index(y, x, 1 - core)
    barrier = pltpu.get_barrier_semaphore()
    for k in range(1, high):
        tell(barrier, frame=index((y + k) % high, x, core))
    for k in range(1, wide):
        tell(barrier, frame=index(y, (x + k) % wide, core))
    tell(barrier, frame=sibling)
    own = pltpu.make_async_copy(src, out.at[y, x, core], local_sem)
    own.start()
    pl.semaphore_wait(barrier, high + wide - 1)

    def along_y(k, back=False):
        place = (y + high - k) % high if back else y
        peer = index((y + k) % high, x, core)
        return push(src, out.at[place, x, core], y_send.at[k], y_recv.at[k], frame=peer)

    def along_x(k, i, back=False):
        place = (y + high - k) % high
        held = src if k == 0 else out.at[place, x, core]
        column = (x + wide - i) % wide if back else x
        return push(
            held, out.at[place, column, core], x_send.at[k, i], x_recv.at[k, i],
            frame=index(y, (x + i) % wide, core),
        )

    def across(k, back=False):
        place = (y + high - k) % high
        side = 1 - core if back else core
        held = out.at[place, :, side]
        return push(out.at[place, :, core], held, c_send.at[k], c_recv.at[k], frame=sibling)

    near = sorted(range(1, high), key=lambda k: min(k, high - k))
    for k in near:
        along_y(k).start()
    for i in range(1, wide):
        along_x(0, i).start()
    for k in near:
        along_y(k, True).wait_recv()
        for i in range(1, wide):
            along_x(k, i).start()
    own.wait()
    for k in [0, *near]:
        for i in range(1, wide):
            along_x(k, i, True).wait_recv()
        across(k).start()
    for k in [0, *near]:
        across(k, True).wait_recv()
    for k in near:
        along_y(k).wait_send()
    for k in [0, *near]:
        for i in range(1, wide):
            along_x(k, i).wait_send()
        across(k).wait_send()


def gather(chunk):
    count = lax.axis_size("frame")
    wide = PLANE_WIDE
    high = count // (2 * wide)
    out = pl.pallas_call(
        gather_kernel,
        out_shape=jax.ShapeDtypeStruct((high, wide, 2, *chunk.shape), chunk.dtype),
        in_specs=[VMEM],
        out_specs=VMEM,
        scratch_shapes=[
            pltpu.SemaphoreType.DMA((high,)),
            pltpu.SemaphoreType.DMA((high,)),
            pltpu.SemaphoreType.DMA((high, wide)),
            pltpu.SemaphoreType.DMA((high, wide)),
            pltpu.SemaphoreType.DMA((high,)),
            pltpu.SemaphoreType.DMA((high,)),
            pltpu.SemaphoreType.DMA,
        ],
        compiler_params=pltpu.CompilerParams(collective_id=0, has_side_effects=True),
        name="gather",
    )(chunk)
    return out.reshape(count, *chunk.shape)


def plane_copies(frame, count, pairs, send, recv):
    def out_piece(i, k):
        peer = (frame + k) % count
        src, dst = pairs[i]
        return push(src.at[peer], dst.at[frame], send.at[i, k], recv.at[i, k], frame=peer)

    def in_piece(i, k):
        origin = (frame + count - k) % count
        src, dst = pairs[i]
        return push(src.at[origin], dst.at[origin], send.at[i, k], recv.at[i, k], frame=origin)

    return out_piece, in_piece


def plane_start(frame, count, pairs, send, recv, own_sem, some=None):
    out_piece, unused = plane_copies(frame, count, pairs, send, recv)
    for i, (src, dst) in enumerate(pairs):
        pltpu.make_async_copy(src.at[frame], dst.at[frame], own_sem.at[i]).start()

    def begin(k):
        for i in range(len(pairs)):
            out_piece(i, k).start()

    each(1, count if some is None else some, begin)
    return begin


def plane_wait(frame, count, pairs, send, recv, own_sem):
    out_piece, in_piece = plane_copies(frame, count, pairs, send, recv)

    def end(k):
        for i in range(len(pairs)):
            in_piece(i, k).wait_recv()
            out_piece(i, k).wait_send()

    each(1, count, end)
    for i, (src, dst) in enumerate(pairs):
        pltpu.make_async_copy(src.at[frame], dst.at[frame], own_sem.at[i]).wait()


def exchange_chain_kernel(
    xs, gs, end_local, own_grad, decay, rx, rg, state_in, later, fwd_out, bwd_out, send, recv, own_sem,
    fwd_send, fwd_recv, bwd_send, bwd_recv,
):
    frame, row = lax.axis_index("frame"), lax.axis_index("row")
    count, bands = lax.axis_size("frame"), lax.axis_size("row")
    height = end_local.shape[0] // CHAIN_CHUNKS
    heads = decay.shape[0]
    per_head = end_local.shape[0] // heads
    barrier = pltpu.get_barrier_semaphore()
    each(1, count, lambda k: tell(barrier, frame=(frame + k) % count))

    @pl.when(row > 0)
    def _():
        tell(barrier, row=row - 1)

    @pl.when(row < bands - 1)
    def _():
        tell(barrier, row=row + 1)

    neighbours = jnp.where(row > 0, 1, 0) + jnp.where(row < bands - 1, 1, 0)
    pl.semaphore_wait(barrier, count - 1 + neighbours)

    def rows_of(c):
        return pl.ds(pl.multiple_of(c * height, height), height)

    def fwd(c):
        where = rows_of(c)
        return push(fwd_out.at[where], state_in.at[where], fwd_send.at[c], fwd_recv.at[c], row=row + 1)

    def bwd(c):
        where = rows_of(c)
        return push(bwd_out.at[where], later.at[where], bwd_send.at[c], bwd_recv.at[c], row=row - 1)

    def fwd_in(c):
        where = rows_of(c)
        return push(fwd_out.at[where], state_in.at[where], fwd_send.at[c], fwd_recv.at[c], row=row - 1)

    def bwd_in(c):
        where = rows_of(c)
        return push(bwd_out.at[where], later.at[where], bwd_send.at[c], bwd_recv.at[c], row=row + 1)

    def join(c, before, own, result):
        for j in range(height // per_head):
            where = pl.ds(pl.multiple_of(c * height + j * per_head, per_head), per_head)
            factor = decay[c * (height // per_head) + j]
            result[where, :] = (
                before[where, :].astype(jnp.float32) * factor + own[where, :]
            ).astype(result.dtype)

    @pl.when(row == 0)
    def _():
        state_in[...] = jnp.zeros_like(state_in)
        for c in range(CHAIN_CHUNKS):
            fwd_out[rows_of(c), :] = end_local[rows_of(c), :].astype(fwd_out.dtype)
            fwd(c).start()

    @pl.when(row == bands - 1)
    def _():
        later[...] = jnp.zeros_like(later)
        for c in range(CHAIN_CHUNKS):
            bwd_out[rows_of(c), :] = own_grad[rows_of(c), :].astype(bwd_out.dtype)
            bwd(c).start()

    slots = CHAIN_CHUNKS + (bands - 1) * CHAIN_LAG
    ahead = 1 + PLANE_AHEAD
    per_slot = -(-(count - ahead) // (slots - PLANE_LATEST))
    begin = plane_start(frame, count, [(xs, rx), (gs, rg)], send, recv, own_sem, ahead)

    def slot(s):
        f = s - row * CHAIN_LAG
        b = s - (bands - 1 - row) * CHAIN_LAG

        @pl.when(jnp.logical_and(row > 0, jnp.logical_and(f >= 0, f < CHAIN_CHUNKS)))
        def _():
            fwd_in(f).wait_recv()

            @pl.when(row < bands - 1)
            def _():
                join(f, state_in, end_local, fwd_out)
                fwd(f).start()

        @pl.when(jnp.logical_and(row < bands - 1, jnp.logical_and(b >= 0, b < CHAIN_CHUNKS)))
        def _():
            bwd_in(b).wait_recv()

            @pl.when(row > 0)
            def _():
                join(b, later, own_grad, bwd_out)
                bwd(b).start()

        first = jnp.minimum(ahead + s * per_slot, count)
        each(first, jnp.minimum(first + per_slot, count), begin)

    each(0, slots, slot)
    plane_wait(frame, count, [(xs, rx), (gs, rg)], send, recv, own_sem)

    @pl.when(row < bands - 1)
    def _():
        for c in range(CHAIN_CHUNKS):
            fwd(c).wait_send()

    @pl.when(row > 0)
    def _():
        for c in range(CHAIN_CHUNKS):
            bwd(c).wait_send()


def exchange_chain(xs, gs, end_local, own_grad, decay):
    count = lax.axis_size("frame")
    state = jax.ShapeDtypeStruct(end_local.shape, jnp.bfloat16)
    return pl.pallas_call(
        exchange_chain_kernel,
        out_shape=(
            jax.ShapeDtypeStruct(xs.shape, xs.dtype),
            jax.ShapeDtypeStruct(gs.shape, gs.dtype),
            state,
            state,
        ),
        in_specs=[ANY, ANY, VMEM, VMEM, SMEM],
        out_specs=(ANY, ANY, VMEM, VMEM),
        scratch_shapes=[
            pltpu.VMEM(end_local.shape, jnp.bfloat16),
            pltpu.VMEM(end_local.shape, jnp.bfloat16),
            pltpu.SemaphoreType.DMA((2, count)),
            pltpu.SemaphoreType.DMA((2, count)),
            pltpu.SemaphoreType.DMA((2,)),
            pltpu.SemaphoreType.DMA((CHAIN_CHUNKS,)),
            pltpu.SemaphoreType.DMA((CHAIN_CHUNKS,)),
            pltpu.SemaphoreType.DMA((CHAIN_CHUNKS,)),
            pltpu.SemaphoreType.DMA((CHAIN_CHUNKS,)),
        ],
        compiler_params=pltpu.CompilerParams(collective_id=1, has_side_effects=True),
        name="exchange_chain",
    )(xs, gs, end_local, own_grad, decay)


def back_kernel(
    ts, bs, wg, rt, rb, rw, send, recv, own_sem, z_send, z_recv, z_own
):
    frame, row = lax.axis_index("frame"), lax.axis_index("row")
    count, bands = lax.axis_size("frame"), lax.axis_size("row")
    share = wg.shape[1] // bands
    barrier = pltpu.get_barrier_semaphore()
    each(1, count, lambda k: tell(barrier, frame=(frame + k) % count))
    each(1, bands, lambda k: tell(barrier, row=(row + k) % bands))
    pl.semaphore_wait(barrier, count - 1 + bands - 1)

    def piece(j):
        return wg.at[:, pl.ds(pl.multiple_of(j * share, share), share)]

    def z_out(k):
        peer = (row + k) % bands
        return push(piece(peer), rw.at[row], z_send.at[k], z_recv.at[k], row=peer)

    def z_in(k):
        origin = (row + bands - k) % bands
        return push(piece(origin), rw.at[origin], z_send.at[k], z_recv.at[k], row=origin)

    z_self = pltpu.make_async_copy(piece(row), rw.at[row], z_own)
    z_self.start()
    each(1, bands, lambda k: z_out(k).start())
    plane_start(frame, count, [(ts, rt), (bs, rb)], send, recv, own_sem)
    plane_wait(frame, count, [(ts, rt), (bs, rb)], send, recv, own_sem)

    def end(k):
        z_in(k).wait_recv()
        z_out(k).wait_send()

    each(1, bands, end)
    z_self.wait()


def back(ts, bs, wg):
    count, bands = lax.axis_size("frame"), lax.axis_size("row")
    share = wg.shape[1] // bands
    return pl.pallas_call(
        back_kernel,
        out_shape=(
            jax.ShapeDtypeStruct(ts.shape, ts.dtype),
            jax.ShapeDtypeStruct(bs.shape, bs.dtype),
            jax.ShapeDtypeStruct((bands, wg.shape[0], share), wg.dtype),
        ),
        in_specs=[ANY] * 3,
        out_specs=(ANY,) * 3,
        scratch_shapes=[
            pltpu.SemaphoreType.DMA((2, count)),
            pltpu.SemaphoreType.DMA((2, count)),
            pltpu.SemaphoreType.DMA((2,)),
            pltpu.SemaphoreType.DMA((bands,)),
            pltpu.SemaphoreType.DMA((bands,)),
            pltpu.SemaphoreType.DMA,
        ],
        compiler_params=pltpu.CompilerParams(collective_id=2, has_side_effects=True),
        name="back",
    )(ts, bs, wg)


def plane_kernel(src, out, send, recv, own_sem):
    frame, count = lax.axis_index("frame"), lax.axis_size("frame")
    barrier = pltpu.get_barrier_semaphore()
    each(1, count, lambda k: tell(barrier, frame=(frame + k) % count))
    pl.semaphore_wait(barrier, count - 1)
    plane_start(frame, count, [(src, out)], send, recv, own_sem)
    plane_wait(frame, count, [(src, out)], send, recv, own_sem)


def plane(src):
    count = lax.axis_size("frame")
    return pl.pallas_call(
        plane_kernel,
        out_shape=jax.ShapeDtypeStruct(src.shape, src.dtype),
        in_specs=[VMEM],
        out_specs=VMEM,
        scratch_shapes=[
            pltpu.SemaphoreType.DMA((1, count)),
            pltpu.SemaphoreType.DMA((1, count)),
            pltpu.SemaphoreType.DMA((1,)),
        ],
        compiler_params=pltpu.CompilerParams(collective_id=3, has_side_effects=True),
        name="plane",
    )(src)


def deliver_kernel(weights, mods, rw, rm, w_send, w_recv, w_own, m_send, m_recv, m_own):
    frame, row = lax.axis_index("frame"), lax.axis_index("row")
    count, bands = lax.axis_size("frame"), lax.axis_size("row")
    per = count // bands
    home = row * per + frame // bands
    slot = frame % bands
    from_row, from_frame = frame // per, (frame % per) * bands
    barrier = pltpu.get_barrier_semaphore()

    def other(f, r):
        return jnp.logical_or(f != frame, r != row)

    def ready(i):
        @pl.when(other(from_frame + i, from_row))
        def _():
            tell(barrier, frame=from_frame + i, row=from_row)

    each(0, bands, ready)
    each(1, bands, lambda k: tell(barrier, row=(row + k) % bands))
    local = jnp.where(home == frame, 1, 0)
    pl.semaphore_wait(barrier, bands - local + bands - 1)

    def w_out(r):
        return push(weights, rw.at[slot], w_send.at[r], w_recv.at[slot], frame=home, row=r)

    def w_in(i):
        return push(weights, rw.at[i], w_send.at[i], w_recv.at[i], frame=from_frame + i, row=from_row)

    w_self = pltpu.make_async_copy(weights, rw.at[slot], w_own)
    m_self = pltpu.make_async_copy(mods, rm.at[row], m_own)
    m_self.start()

    def m_out(k):
        return push(mods, rm.at[row], m_send.at[k], m_recv.at[k], row=(row + k) % bands)

    def m_in(k):
        origin = (row + bands - k) % bands
        return push(mods, rm.at[origin], m_send.at[k], m_recv.at[k], row=origin)

    def start_weights(r):
        @pl.when(other(home, r))
        def _():
            w_out(r).start()

        @pl.when(jnp.logical_not(other(home, r)))
        def _():
            w_self.start()

    each(0, bands, start_weights)
    each(1, bands, lambda k: m_out(k).start())

    def end_weights(i):
        @pl.when(other(from_frame + i, from_row))
        def _():
            w_in(i).wait_recv()

        @pl.when(jnp.logical_not(other(from_frame + i, from_row)))
        def _():
            w_self.wait()

        @pl.when(other(home, i))
        def _():
            w_out(i).wait_send()

    each(0, bands, end_weights)

    def end_mods(k):
        m_in(k).wait_recv()
        m_out(k).wait_send()

    each(1, bands, end_mods)
    m_self.wait()


def deliver(weights, mods):
    bands = lax.axis_size("row")
    return pl.pallas_call(
        deliver_kernel,
        out_shape=(
            jax.ShapeDtypeStruct((bands, *weights.shape), weights.dtype),
            jax.ShapeDtypeStruct((bands, *mods.shape), mods.dtype),
        ),
        in_specs=[VMEM, VMEM],
        out_specs=(VMEM, VMEM),
        scratch_shapes=[
            pltpu.SemaphoreType.DMA((bands,)),
            pltpu.SemaphoreType.DMA((bands,)),
            pltpu.SemaphoreType.DMA,
            pltpu.SemaphoreType.DMA((bands,)),
            pltpu.SemaphoreType.DMA((bands,)),
            pltpu.SemaphoreType.DMA,
        ],
        compiler_params=pltpu.CompilerParams(collective_id=4, has_side_effects=True),
        name="deliver",
    )(weights, mods)


def time_embed(timestep, embed_dim):
    half_dim = embed_dim // 2
    frequency = jnp.exp(-math.log(10000.0) * jnp.arange(half_dim, dtype=jnp.float32) / half_dim)
    angles = timestep.astype(jnp.float32)[:, None] * frequency[None, :]
    return jax.nn.silu(jnp.concatenate([jnp.cos(angles), jnp.sin(angles)], axis=1))


def halves(values):
    high = values.astype(jnp.bfloat16)
    return high, (values - high.astype(jnp.float32)).astype(jnp.bfloat16)


def mm(a, b):
    return jnp.dot(a, b, preferred_element_type=jnp.float32)


def mm_nt(a, b):
    return lax.dot_general(a, b, (((1,), (1,)), ((), ())), preferred_element_type=jnp.float32)


def mm_tn(a, b):
    return lax.dot_general(a, b, (((0,), (0,)), ((), ())), preferred_element_type=jnp.float32)


def with_ones(ones, values, dot):
    first = values.astype(jnp.bfloat16)
    rest = values - first.astype(jnp.float32)
    second = rest.astype(jnp.bfloat16)
    third = (rest - second.astype(jnp.float32)).astype(jnp.bfloat16)
    return dot(ones, first) + dot(ones, second) + dot(ones, third)


def earlier_mask(length, sites):
    t = lax.broadcasted_iota(jnp.int32, (length, length), 0)
    u = lax.broadcasted_iota(jnp.int32, (length, length), 1)
    return jnp.logical_and(u <= t, lax.rem(t, sites) == lax.rem(u, sites))


def steps_of(logits, bias, rate, mask):
    raised = logits.astype(jnp.float32) + bias
    step = jnp.maximum(raised, 0.0) + jnp.log1p(jnp.exp(-jnp.abs(raised)))
    lower = jnp.where(mask, 1.0, 0.0).astype(jnp.bfloat16)
    return raised, step, with_ones(lower, -step * rate, mm)


def spread(values, expand, where):
    high, low = halves(values)
    return mm(high, expand[:, where]) + mm(low, expand[:, where])


def per_head(values, collect, where):
    high, low = halves(values)
    return mm(high, collect[where, :]) + mm(low, collect[where, :])


def head_kernel(
    tokens, grad, weights, step_w, shift, scale, bias, rate, expand,
    normed_out, coeff_out, logit_out, end_out, own_out, decay_out,
):
    length, width = tokens.shape
    lanes = step_w.shape[1]
    values = tokens[...].astype(jnp.float32)
    inverse = lax.rsqrt(jnp.mean(values * values, axis=1, keepdims=True) + norm_eps)
    normed_out[...] = (values * inverse * (1.0 + scale[...]) + shift[...]).astype(jnp.bfloat16)
    project(normed_out, weights, step_w, coeff_out, logit_out)
    b_part, c_part = coeff_out[:, :lanes], coeff_out[:, lanes:]
    mask = earlier_mask(length, 1)
    unused, step, log = steps_of(logit_out[...], bias[...], rate[...], mask)
    last = log[length - 1 :, :]
    decay_out[...] = jnp.exp(last)
    lead = jnp.exp(last - log) * step
    reach = jnp.exp(log) * (1.0 / lanes)
    for j in range(width // lanes):
        where = slice(j * lanes, (j + 1) * lanes)
        scaled = (normed_out[:, where].astype(jnp.float32) * spread(lead, expand, where)).astype(jnp.bfloat16)
        end_out[where, :] = mm_tn(scaled, b_part)
        pulled = (grad[:, where].astype(jnp.float32) * spread(reach, expand, where)).astype(jnp.bfloat16)
        own_out[where, :] = mm_tn(pulled, c_part)


def project(normed, weights, step_w, coeff_out, logit_out):
    lanes = step_w.shape[1]
    depth = weights.shape[1] // 2
    count = weights.shape[0]
    for i in range(2):
        w = weights[:, i * depth : (i + 1) * depth, :].reshape(count * depth, lanes)
        coeff_out[:, i * lanes : (i + 1) * lanes] = mm(normed[...], w).astype(jnp.bfloat16)
    logit_out[...] = mm(normed[...], step_w[...]).astype(jnp.bfloat16)


def scan_pass(
    x_ref, g_ref, coeffs, logits, bias, rate, weights, step_w, expand, collect, skip, state, later,
    mixed_ref, dx_ref, back_ref, wg_ref, sites, first,
):
    length, width = x_ref.shape
    lanes = coeffs.shape[1] // 2
    space = state is not None
    b_part, c_part = coeffs[:, :lanes], coeffs[:, lanes:]
    mask = earlier_mask(length, sites)
    raised, step, log = steps_of(logits[...], bias[...], rate[...], mask)
    log_t = log.T
    scores = jnp.where(mask, mm_nt(c_part, b_part) * (1.0 / lanes), 0.0)
    left = lax.broadcasted_iota(jnp.int32, (length, lanes), 1) < lanes // 2
    d_scores = jnp.zeros((length, length), jnp.float32)
    pull_out = jnp.zeros((length, lanes), jnp.float32)
    pull_in = jnp.zeros((length, lanes), jnp.float32)
    d_b = jnp.zeros((length, lanes), jnp.float32)
    d_c = jnp.zeros((length, lanes), jnp.float32)
    if space:
        last = log[length - 1 :, :]
        reach_all = jnp.exp(log) * (1.0 / lanes)
        fade_all = jnp.exp(last - log)
        d_last = jnp.zeros((8, lanes), jnp.float32)
        state_rows = []
    for j in range(width // lanes):
        where = slice(j * lanes, (j + 1) * lanes)
        x, g = x_ref[:, where], g_ref[:, where]
        wide_x, wide_g = x.astype(jnp.float32), g.astype(jnp.float32)
        step_x = spread(step, expand, where)
        stepped_wide = wide_x * step_x
        stepped = stepped_wide.astype(jnp.bfloat16)
        outs, backs = [], []
        for i in range(2):
            h = 2 * j + i
            fall = jnp.exp(jnp.minimum(log[:, h : h + 1] - log_t[h : h + 1, :], 0.0))
            w = (scores * fall).astype(jnp.bfloat16)
            outs.append(mm(w, stepped))
            backs.append(mm_tn(w, g))
            own_half = left if i == 0 else jnp.logical_not(left)
            half_g = jnp.where(own_half, wide_g, 0.0).astype(jnp.bfloat16)
            d_scores += mm_nt(half_g, stepped) * fall
        out = jnp.where(left, outs[0], outs[1])
        d_step_x = jnp.where(left, backs[0], backs[1])
        if space:
            held, late = state[where, :], later[where, :]
            reach = spread(reach_all, expand, where)
            fade = spread(fade_all, expand, where)
            out += mm_nt(c_part, held) * reach
            d_c += mm((wide_g * reach).astype(jnp.bfloat16), held)
            from_end = mm_nt(b_part, late) * fade
            d_step_x += from_end
            d_b += mm((stepped_wide * fade).astype(jnp.bfloat16), late)
            to_last = jnp.sum(stepped_wide * from_end, axis=0, keepdims=True)
            d_last += per_head(jnp.broadcast_to(to_last, (8, lanes)), collect, where)
            both = held.astype(jnp.float32) * late.astype(jnp.float32)
            half = lanes // 2
            state_rows += [
                jnp.sum(both[:half], axis=0, keepdims=True),
                jnp.sum(both[half:], axis=0, keepdims=True),
            ]
            mixed_ref[:, where] = out + skip[:, where] * wide_x
            direct = (wide_g * skip[:, where]).astype(jnp.bfloat16).astype(jnp.float32)
            dx_ref[:, where] = step_x * d_step_x + direct
        else:
            mixed_ref[:, where] = out.astype(mixed_ref.dtype)
            dx_ref[:, where] = step_x * d_step_x
        pull_out += per_head(wide_g * out, collect, where)
        pull_in += per_head(wide_x * d_step_x, collect, where)
    d_low = (jnp.where(mask, d_scores, 0.0) * (1.0 / lanes)).astype(jnp.bfloat16)
    d_c += mm(d_low, b_part)
    d_b += mm_tn(d_low, c_part)
    d_log = pull_out - step * pull_in
    if space:
        states = jnp.concatenate([*state_rows, jnp.zeros((lanes - len(state_rows), lanes), jnp.float32)], axis=0)
        high, low = halves(states)
        ones = jnp.ones((8, lanes), jnp.bfloat16)
        d_last += (mm_nt(ones, high) + mm_nt(ones, low)) * jnp.exp(last)
        at_end = lax.broadcasted_iota(jnp.int32, (length, lanes), 0) == length - 1
        d_log += jnp.where(at_end, d_last[:1, :], 0.0)
    lower = jnp.where(mask, 1.0, 0.0).astype(jnp.bfloat16)
    d_fall = with_ones(lower, d_log, mm_tn)
    d_step = pull_in - rate[...] * d_fall
    d_logit = (d_step * jax.nn.sigmoid(raised)).astype(jnp.bfloat16)
    low_b, low_c = d_b.astype(jnp.bfloat16), d_c.astype(jnp.bfloat16)
    count, depth = weights.shape[0], weights.shape[1] // 2
    block = 8
    for k in range(count // block):
        cols = slice(k * block * depth, (k + 1) * block * depth)
        w_b = weights[k * block : (k + 1) * block, :depth, :].reshape(block * depth, lanes)
        w_c = weights[k * block : (k + 1) * block, depth:, :].reshape(block * depth, lanes)
        total = (
            dx_ref[:, cols] + mm_nt(low_b, w_b) + mm_nt(low_c, w_c) + mm_nt(d_logit, step_w[cols, :])
        )
        back_ref[:, cols] = total.astype(back_ref.dtype)
        x = x_ref[:, cols]
        heads = wg_ref.shape[0] - 2 * lanes
        terms = (mm_tn(low_b, x), mm_tn(low_c, x), mm_tn(d_logit, x)[:heads])
        for i, term in enumerate(terms):
            rows = slice(i * lanes, i * lanes + term.shape[0])
            wg_ref[rows, cols] = term if first else wg_ref[rows, cols] + term


def core_kernel(
    normed, grad, coeffs, logits, state, later, site_tokens, site_grad, weights, step_w, shift_all, scale_all,
    bias, rate_space, rate_time, skip, expand, collect,
    mixed_out, pre_out, time_out, back_out, wg_out, site_normed, site_coeffs, site_logits, dx, wg,
):
    length, width = normed.shape
    clips = shift_all.shape[0]
    sites = length // weights.shape[0]
    part = length // clips
    for c in range(clips):
        rows = slice(c * part, (c + 1) * part)
        values = site_tokens[rows, :].astype(jnp.float32)
        inverse = lax.rsqrt(jnp.mean(values * values, axis=1, keepdims=True) + norm_eps)
        site_normed[rows, :] = (
            values * inverse * (1.0 + scale_all[c : c + 1, :]) + shift_all[c : c + 1, :]
        ).astype(jnp.bfloat16)
    project(site_normed, weights, step_w, site_coeffs, site_logits)
    scan_pass(
        site_normed, site_grad, site_coeffs, site_logits, bias, rate_time, weights, step_w, expand, collect,
        None, None, None, time_out, dx, back_out, wg, sites, True,
    )
    scan_pass(
        normed, grad, coeffs, logits, bias, rate_space, weights, step_w, expand, collect,
        skip, state, later, mixed_out, dx, pre_out, wg, 1, False,
    )
    wg_out[...] = wg[...].astype(jnp.bfloat16)


BIG = 56 * 2**20


def head(tokens, grad, weights, step_w, shift, scale, bias, rate, expand):
    length, width = tokens.shape
    lanes = step_w.shape[1]
    low = functools.partial(jax.ShapeDtypeStruct, dtype=jnp.bfloat16)
    wide = functools.partial(jax.ShapeDtypeStruct, dtype=jnp.float32)
    return pl.pallas_call(
        head_kernel,
        out_shape=(
            low((length, width)),
            low((length, 2 * lanes)),
            low((length, lanes)),
            wide((width, lanes)),
            wide((width, lanes)),
            wide((1, lanes)),
        ),
        in_specs=[VMEM] * 9,
        out_specs=(VMEM,) * 6,
        compiler_params=pltpu.CompilerParams(vmem_limit_bytes=BIG),
        name="head",
    )(tokens, grad, weights, step_w, shift, scale, bias, rate, expand)


def core(heads, *operands):
    normed, coeffs, weights = operands[0], operands[2], operands[8]
    length, width = normed.shape
    lanes = coeffs.shape[1] // 2
    low = functools.partial(jax.ShapeDtypeStruct, dtype=jnp.bfloat16)
    wide = functools.partial(jax.ShapeDtypeStruct, dtype=jnp.float32)
    rows = 2 * lanes + heads
    return pl.pallas_call(
        core_kernel,
        out_shape=(
            wide((length, width)),
            wide((length, width)),
            low((length, width)),
            low((length, width)),
            low((rows, width)),
        ),
        in_specs=[VMEM] * 18,
        out_specs=(VMEM,) * 5,
        scratch_shapes=[
            pltpu.VMEM((length, width), jnp.bfloat16),
            pltpu.VMEM((length, 2 * lanes), jnp.bfloat16),
            pltpu.VMEM((length, lanes), jnp.bfloat16),
            pltpu.VMEM((length, width), jnp.float32),
            pltpu.VMEM((rows, width), jnp.float32),
        ],
        compiler_params=pltpu.CompilerParams(vmem_limit_bytes=BIG),
        name="core",
    )(*operands)


def three_parts(values):
    first = lax.reduce_precision(values, 8, 7)
    second = lax.reduce_precision(values - first, 8, 7)
    return first, second, values - first - second


def per_device(
    tokens,
    cotangent,
    timestep,
    mod_weight,
    proj_weight,
    step_weight,
    step_bias,
    rate_space,
    rate_time,
    skip_gain,
):
    frame_count = lax.axis_size("frame")
    row_count = lax.axis_size("row")
    frame_id = lax.axis_index("frame")
    feat_width = tokens.shape[-1]
    band_len = tokens.shape[1] * tokens.shape[2]
    clip_count = timestep.shape[0]
    clip_frames = frame_count // clip_count
    site_count = band_len // frame_count
    head_count = rate_space.shape[0]
    state_size = proj_weight.shape[1] // 2
    depth = proj_weight.shape[0]
    clip_id = frame_id // clip_frames
    factor = (frame_count * row_count * band_len) ** (-0.5)
    tokens = tokens.reshape(band_len, feat_width)
    flat_grad = cotangent.reshape(band_len, feat_width)

    activated = time_embed(timestep, mod_weight.shape[0]).astype(jnp.bfloat16)
    mod_cols = jnp.dot(activated, mod_weight, preferred_element_type=jnp.float32)
    lane = state_size
    mod_rows = [part.reshape(-1, lane).astype(jnp.bfloat16) for part in three_parts(mod_cols)]
    rows = [proj_weight[:, :state_size], proj_weight[:, state_size:], step_weight.reshape(-1, lane), *mod_rows]
    used = sum(r.shape[0] for r in rows)
    chunk = jnp.concatenate([*rows, jnp.zeros((-used % 16, lane), jnp.bfloat16)], axis=0)
    gathered = gather(chunk)
    weights = gathered[:, : 2 * depth]
    step_rows = depth * head_count // lane
    step_full = gathered[:, 2 * depth : 2 * depth + step_rows].reshape(feat_width, head_count)
    step_w = jnp.pad(step_full, ((0, 0), (0, lane - head_count)))
    mod_height = mod_rows[0].shape[0]
    mod_parts = gathered[:, 2 * depth + step_rows : 2 * depth + step_rows + 3 * mod_height]
    mod_parts = mod_parts.astype(jnp.float32).reshape(frame_count, 3, clip_count, -1)
    modulation = mod_parts[:, 0] + mod_parts[:, 1] + mod_parts[:, 2]
    modulation = modulation.transpose(1, 0, 2).reshape(clip_count, 2 * feat_width)
    shift_all, scale_all = modulation[:, :feat_width], modulation[:, feat_width:]
    shift_vec = lax.dynamic_index_in_dim(shift_all, clip_id, 0)
    scale_vec = lax.dynamic_index_in_dim(scale_all, clip_id, 0)

    def on_lanes(vector):
        return jnp.pad(vector, (0, lane - head_count)).reshape(1, lane)

    bias, fade_space, fade_time = on_lanes(step_bias), on_lanes(rate_space), on_lanes(rate_time)
    channel_head = jnp.arange(feat_width) // (feat_width // head_count)
    expand = (channel_head[None, :] == jnp.arange(lane)[:, None]).astype(jnp.bfloat16)
    collect = (channel_head[:, None] == jnp.arange(lane)[None, :]).astype(jnp.bfloat16)
    skip_full = jnp.repeat(skip_gain, feat_width // head_count).reshape(1, feat_width)
    normed, coeffs, logits, end_local, own_grad, end_decay = head(
        tokens, flat_grad, weights, step_w, shift_vec, scale_vec, bias, fade_space, expand
    )
    site_tokens, site_grad, state_in, later_grad = exchange_chain(
        tokens.reshape(frame_count, site_count, feat_width),
        flat_grad.reshape(frame_count, site_count, feat_width),
        end_local,
        own_grad,
        end_decay[0, :head_count],
    )
    mixed_part, pre_part, time_out, time_back, weight_grad = core(
        head_count,
        normed,
        flat_grad,
        coeffs,
        logits,
        state_in,
        later_grad,
        site_tokens.reshape(band_len, feat_width),
        site_grad.reshape(band_len, feat_width),
        weights,
        step_w,
        shift_all,
        scale_all,
        bias,
        fade_space,
        fade_time,
        skip_full,
        expand,
        collect,
    )
    frame_time, frame_back, weight_parts = back(
        time_out.reshape(frame_count, site_count, feat_width),
        time_back.reshape(frame_count, site_count, feat_width),
        weight_grad,
    )
    frame_time = frame_time.reshape(band_len, feat_width).astype(jnp.float32)
    mixed = (mixed_part + frame_time).astype(jnp.bfloat16)
    pre_grad = pre_part + frame_back.reshape(band_len, feat_width).astype(jnp.float32)
    tokens_wide = tokens.astype(jnp.float32)
    inverse = lax.rsqrt(jnp.mean(tokens_wide * tokens_wide, axis=-1, keepdims=True) + norm_eps)
    unit_rows = tokens_wide * inverse
    shift_grad = jnp.sum(pre_grad, axis=0)
    scale_grad = jnp.sum(pre_grad * unit_rows, axis=0)
    unit_grad = pre_grad * (1.0 + scale_vec)
    d_tokens = inverse * (unit_grad - unit_rows * jnp.mean(unit_grad * unit_rows, axis=-1, keepdims=True))

    band_sum = jnp.sum(weight_parts.astype(jnp.float32), axis=0).T.reshape(frame_count, -1)
    mod_term = jnp.concatenate([shift_grad, scale_grad]).reshape(frame_count, -1)
    payload = jnp.concatenate([band_sum, mod_term], axis=1)
    payload = jnp.pad(payload, ((0, 0), (0, -payload.shape[1] % (16 * lane))))
    arrived = plane(payload.reshape(frame_count, -1, lane).astype(jnp.bfloat16)).astype(jnp.float32)
    by_clip = jnp.sum(arrived.reshape(clip_count, clip_frames, *arrived.shape[1:]), axis=1)
    weight_sum = jnp.sum(by_clip, axis=0)
    mod_start = band_sum.shape[1]
    mod_width = mod_term.shape[1]
    mod_part = by_clip.reshape(clip_count, -1)[:, mod_start : mod_start + mod_width]
    mod_box = jnp.pad(mod_part, ((0, -clip_count % 8), (0, -mod_width % 128)))
    weight_box, mod_boxes = deliver(weight_sum, mod_box)
    weight_rows = weight_box.reshape(row_count, -1)[:, :mod_start].reshape(depth, -1) * factor
    grad_proj, grad_step = weight_rows[:, : 2 * state_size], weight_rows[:, 2 * state_size :]
    mod_sum = jnp.sum(mod_boxes, axis=0)[:clip_count, :mod_width]
    grad_mod = (
        jnp.dot(activated.astype(jnp.float32).T, mod_sum, precision=lax.Precision.HIGHEST) * factor
    )
    shape = cotangent.shape
    return (
        mixed.reshape(shape),
        d_tokens.astype(jnp.bfloat16).reshape(shape),
        grad_proj,
        grad_step,
        grad_mod,
    )


def solution(mesh):
    placed = (
        P("frame", "row", None, None),
        P("frame", "row", None, None),
        P(),
        P(None, "frame"),
        P("frame", None),
        P("frame", None),
        P(),
        P(),
        P(),
        P(),
    )
    return jax.shard_map(
        per_device,
        mesh=mesh,
        in_specs=placed,
        out_specs=(
            P("frame", "row", None, None),
            P("frame", "row", None, None),
            P("frame", None),
            P("frame", None),
            P(None, "frame"),
        ),
        check_vma=False,
    )
```

time: 501 us -> 215 us (0.43)
  Pallas kernels: 386 us -> 172 us
  matrix products: 42.4 us -> 0.99 us
  local copies, waits for them, and re-layouts: 43.8 us -> 25.2 us
  other arithmetic: 22.5 us -> 13.3 us
    pallas_call x1, Pallas kernels: 226 us -> 47.9 us  [exchange_chain(): pl.pallas_call(exchange_chain_kernel, out_shape=(jax.ShapeDtypeStruct(xs....]
    pallas_call x1, Pallas kernels: 99.7 us -> 35.5 us  [back(): pl.pallas_call(back_kernel, out_shape=(jax.ShapeDtypeStruct(ts.shape, ts....]
    dot_general x34 -> x0, matrix products: 41.4 us -> none  [the longest x6 17.7 us: block_parts(): jnp.einsum('shtu,suhp->sthp', weights, inputs, preferred_element_type=jnp...]
    pallas_call x1 -> x3, Pallas kernels: 29.9 us -> 55.1 us  [the longest x1 22.7 us: gather(): pl.pallas_call(gather_kernel, out_shape=jax.ShapeDtypeStruct((high, wide,...]
    convert_element_type x11 -> x2, local copies, waits for them, and re-layouts: 11.1 us -> 1.34 us  [the longest x1 1.19 us: per_device(): frame_back.reshape(band_len, feat_width).astype(jnp.float32)]
    mul x10 -> x1, local copies, waits for them, and re-layouts: 6.87 us -> 0.08 us  [per_device(): weight_box.reshape(row_count, -1)[:, :mod_start].reshape(depth, -1) * factor]
    convert_element_type x6 -> x2, other arithmetic: 7.77 us -> 2.03 us  [the longest x1 1.12 us: per_device(): (channel_head[:, None] == jnp.arange(lane)[None, :]).astype(jnp.bfloat16)]
    reshape x13 -> x6, local copies, waits for them, and re-layouts: 11.4 us -> 6.67 us  [the longest x1 2.23 us: per_device(): time_out.reshape(frame_count, site_count, feat_width)]
where the time goes in v2:
time: 215 us; the launch traced here: 212 us
  Pallas kernels  172 us (80%)
  local copies, waits for them, and re-layouts  25.2 us (12%)
  other arithmetic  13.3 us (6%)
    pallas_call x1, Pallas kernels, exchange_chain(): pl.pallas_call(exchange_chain_kernel, out_shape=(jax.ShapeDtypeStruct(xs....  47.9 us
    pallas_call x1, Pallas kernels, back(): pl.pallas_call(back_kernel, out_shape=(jax.ShapeDtypeStruct(ts.shape, ts....  35.5 us
    pallas_call x1, Pallas kernels, gather(): pl.pallas_call(gather_kernel, out_shape=jax.ShapeDtypeStruct((high, wide,...  22.7 us
    pallas_call x1, Pallas kernels, core(): pl.pallas_call(core_kernel, out_shape=(wide((length, width)), wide((lengt...  21.6 us
    pallas_call x1, Pallas kernels, plane(): pl.pallas_call(plane_kernel, out_shape=jax.ShapeDtypeStruct(src.shape, sr...  19.3 us
    pallas_call x1, Pallas kernels, deliver(): pl.pallas_call(deliver_kernel, out_shape=(jax.ShapeDtypeStruct((bands, *w...  14.3 us
    pallas_call x1, Pallas kernels, head(): pl.pallas_call(head_kernel, out_shape=(low((length, width)), low((length,...  10.7 us

profile of v2, /device:TPU:1, one launch (start us, length us, event | category | flops | bytes accessed | tf_op | source)
XLA Modules:
  0.0 212.4 jit_solution(17169675167180633126)
XLA Ops:
  0.6 0.0 copy-start
  0.7 0.7 convert_element_type.74
  1.3 0.1 multiply_cosine_fusion
  1.5 0.1 fusion.24
  1.6 0.1 convert_element_type.77
  1.7 0.1 convert_element_type.79
  1.8 0.1 convert_element_type.81
  1.8 0.7 fusion.30
  2.6 0.8 reshape.144
  3.4 2.4 %concatenate.20.src = bf16[80,128]{1,0:T(8,128)(2,1)} concatenate(bf16[32,128]{1,0:T(8,128)(2,1)S(1)} %get-tuple-element.54, bf16[32,128]{1,0:T(8,128)(2,1)S(1)} %get-tuple-element.53, bf16[8,128]{1,0:T(8,128)(2,1)S(1)} %reshape.144, bf16[2,128]{1,0:T(2,128)(2,1)S(1)} %convert_element_type.77, bf16[2,128]{1,0:T(2,128)(2,1)S(1)} %convert_element_type.79, ...), dimensions={0} | concatenate | bytes 40960 | tf_op jit(solution)/shard_map/concatenate | solution.py:818
  5.7 22.7 %gather.1 = bf16[8,4,2,80,128]{4,3,2,1,0:T(8,128)(2,1)} custom-call(bf16[80,128]{1,0:T(8,128)(2,1)} %concatenate.20.src), custom_call_target="tpu_custom_call" | custom-call | tf_op jit(solution)/shard_map/gather/pallas_call | solution.py:122
  28.5 1.0 slice_convert_fusion
  29.5 0.2 reshape.164
  29.8 0.1 reshape.149
  29.9 0.6 broadcast_add_fusion
  30.6 0.2 reshape.146
  30.8 0.9 pad.23.step_w
  31.7 1.1 slice.64.weights
  32.9 0.9 fusion.9.expand
  33.8 0.6 pad_bitcast_fusion.1
  34.4 10.7 %head.1 = (bf16[128,2048]{1,0:T(8,128)(2,1)}, bf16[128,256]{1,0:T(8,128)(2,1)}, bf16[128,128]{1,0:T(8,128)(2,1)}, f32[2048,128]{1,0:T(8,128)}, f32[2048,128]{1,0:T(8,128)}, /*index=5*/f32[1,128]{1,0:T(1,128)}) custom-call(bf16[128,2048]{1,0:T(8,128)(2,1)} %bitcast.43, bf16[128,2048]{1,0:T(8,128)(2,1)} %bitcast.47, bf16[64,64,128]{2,1,0:T(8,128)(2,1)} %slice.64.weights, ...), custom_call_target="tpu_custom_call" | custom-call | tf_op jit(solution)/shard_map/head/pallas_call | solution.py:731
  45.1 1.3 slice_bitcast_fusion.decay
  46.3 1.1 reshape_reshape.10.gs
  47.5 1.1 reshape_reshape.9.xs
  48.6 47.9 %exchange_chain.1 = (bf16[64,2,2048]{2,1,0:T(2,128)(2,1)}, bf16[64,2,2048]{2,1,0:T(2,128)(2,1)}, bf16[2048,128]{1,0:T(8,128)(2,1)}, bf16[2048,128]{1,0:T(8,128)(2,1)}) custom-call(bf16[64,2,2048]{2,1,0:T(2,128)(2,1)} %reshape_reshape.9.xs, bf16[64,2,2048]{2,1,0:T(2,128)(2,1)} %reshape_reshape.10.gs, f32[2048,128]{1,0:T(8,128)} %get-tuple-element.28.end_local, ...), custom_call_target="tpu_custom_call" | custom-call | tf_op jit(solution)/shard_map/exchange_chain/pallas_call | solution.py:293
  96.6 0.0 copy-start.10
  96.6 0.0 copy-start.13
  96.6 2.1 reshape.152.site_tokens
  98.7 1.0 reshape.153.site_grad
  99.7 1.1 fusion.10.collect
  100.8 0.1 broadcast_in_dim.5
  100.9 0.7 reshape_reshape.11.skip
  101.6 0.5 pad_bitcast_fusion.rate_time
  102.1 21.6 %core.1 = (f32[128,2048]{1,0:T(8,128)}, f32[128,2048]{1,0:T(8,128)}, bf16[128,2048]{1,0:T(8,128)(2,1)}, bf16[128,2048]{1,0:T(8,128)(2,1)}, bf16[288,2048]{1,0:T(8,128)(2,1)}) custom-call(bf16[128,2048]{1,0:T(8,128)(2,1)} %get-tuple-element.25.normed, bf16[128,2048]{1,0:T(8,128)(2,1)} %bitcast.48, bf16[128,256]{1,0:T(8,128)(2,1)} %get-tuple-element.26.coeffs, ...), custom_call_target="tpu_custom_call" | custom-call | tf_op jit(solution)/shard_map/core/pallas_call | solution.py:755
  123.7 2.2 %reshape.155.ts = bf16[64,2,2048]{2,1,0:T(2,128)(2,1)} reshape(bf16[128,2048]{1,0:T(8,128)(2,1)} %get-tuple-element.36) | data formatting | bytes 1048576 | tf_op jit(solution)/shard_map/reshape | solution.py:873
  125.9 0.0 copy-done.6
  126.0 1.1 reshape.156.bs
  127.1 35.5 %back.1 = (bf16[64,2,2048]{2,1,0:T(2,128)(2,1)}, bf16[64,2,2048]{2,1,0:T(2,128)(2,1)}, bf16[8,288,256]{2,1,0:T(8,128)(2,1)}) custom-call(bf16[64,2,2048]{2,1,0:T(2,128)(2,1)} %reshape.155.ts, bf16[64,2,2048]{2,1,0:T(2,128)(2,1)} %reshape.156.bs, bf16[288,2048]{1,0:T(8,128)(2,1)} %get-tuple-element.38.wg), custom_call_target="tpu_custom_call" | custom-call | tf_op jit(solution)/shard_map/back/pallas_call | solution.py:358
  162.6 1.2 reshape.166
  163.7 0.2 fusion.8
  163.9 1.7 fusion.7
  165.6 0.1 concatenate.21
  165.7 0.1 concatenate.22
  165.8 1.4 reduce.2
  167.2 0.2 copy.20
  167.4 0.2 reshape.159
  167.7 0.7 copy.21
  168.4 19.3 %plane.1 = bf16[64,16,128]{2,1,0:T(8,128)(2,1)} custom-call(bf16[64,16,128]{2,1,0:T(8,128)(2,1)} %bitcast.49), custom_call_target="tpu_custom_call" | custom-call | tf_op jit(solution)/shard_map/plane/pallas_call | solution.py:391
  187.7 1.0 bitcast_reduce_fusion
  188.8 0.6 pad.28.mods
  189.4 1.6 convert_reduce_fusion.weights
  191.0 14.3 %deliver.1 = (f32[8,16,128]{2,1,0:T(8,128)}, f32[8,8,128]{2,1,0:T(8,128)}) custom-call(f32[16,128]{1,0:T(8,128)} %convert_reduce_fusion.weights, f32[8,128]{1,0:T(8,128)} %pad.28.mods), custom_call_target="tpu_custom_call" | custom-call | tf_op jit(solution)/shard_map/deliver/pallas_call | solution.py:482
  205.3 0.0 copy-start.5
  205.3 0.9 copy.26
  206.2 0.1 mul.93
  206.3 0.6 slice.74
  206.9 0.6 slice.75
  207.5 0.8 reduce_sum.79
  208.3 0.9 convolution_multiply_fusion
  209.2 1.1 fusion.12
  210.3 0.0 copy-done.5
  210.3 0.1 reshape.165
  210.4 1.1 copy-done.4
  211.5 0.9 fusion.11
  (34 shorter events, 0.2 us)
Async XLA Ops:
  0.6 0.8 copy-start
  28.5 2.1 copy-start.2
  29.9 2.9 %copy-start.8 = (f32[4,2048]{1,0:T(4,128)}, f32[4,2048]{1,0:T(4,128)S(1)}, u32[]{:S(2)}) copy-start(f32[4,2048]{1,0:T(4,128)S(1)} %get-tuple-element.51.scale_all) | copy-start | bytes 98308
  29.9 2.9 %copy-start.9 = (f32[4,2048]{1,0:T(4,128)}, f32[4,2048]{1,0:T(4,128)S(1)}, u32[]{:S(2)}) copy-start(f32[4,2048]{1,0:T(4,128)S(1)} %get-tuple-element.52.shift_all) | copy-start | bytes 98308
  31.7 2.0 copy-start.11
  31.7 2.0 copy-start.12
  34.4 12.0 %copy-start.3 = (bf16[1,1,128,2048]{3,2,1,0:T(8,128)(2,1)S(1)}, bf16[1,1,128,2048]{3,2,1,0:T(8,128)(2,1)}, u32[]{:S(2)}) copy-start(bf16[1,1,128,2048]{3,2,1,0:T(8,128)(2,1)} %param.11) | copy-start | bytes 1572868
  45.1 2.4 %copy-start.1 = (bf16[1,1,128,2048]{3,2,1,0:T(8,128)(2,1)S(1)}, bf16[1,1,128,2048]{3,2,1,0:T(8,128)(2,1)}, u32[]{:S(2)}) copy-start(bf16[1,1,128,2048]{3,2,1,0:T(8,128)(2,1)} %param.10) | copy-start | bytes 1572868
  96.5 2.1 %copy-start.7 = (bf16[64,2,2048]{2,1,0:T(2,128)(2,1)S(1)}, bf16[64,2,2048]{2,1,0:T(2,128)(2,1)}, u32[]{:S(2)}) copy-start(bf16[64,2,2048]{2,1,0:T(2,128)(2,1)} %get-tuple-element.34) | copy-start | bytes 1572868
  96.6 4.3 %copy-start.10 = (f32[32]{0:T(128)S(1)}, f32[32]{0:T(128)}, u32[]{:S(2)}) copy-start(f32[32]{0:T(128)} %param.19) | copy-start | bytes 388
  96.6 5.0 %copy-start.13 = (f32[32]{0:T(128)S(1)}, f32[32]{0:T(128)}, u32[]{:S(2)}) copy-start(f32[32]{0:T(128)} %param.18) | copy-start | bytes 388
  123.7 2.2 %copy-start.6 = (bf16[128,2048]{1,0:T(8,128)(2,1)S(1)}, bf16[128,2048]{1,0:T(8,128)(2,1)}, u32[]{:S(2)}) copy-start(bf16[128,2048]{1,0:T(8,128)(2,1)} %get-tuple-element.37) | copy-start | bytes 1572868
  205.3 5.0 %copy-start.5 = (bf16[64,2,2048]{2,1,0:T(2,128)(2,1)S(1)}, bf16[64,2,2048]{2,1,0:T(2,128)(2,1)}, u32[]{:S(2)}) copy-start(bf16[64,2,2048]{2,1,0:T(2,128)(2,1)} %get-tuple-element.39) | copy-start | bytes 1572868
  210.3 1.2 copy-start.4

commit v3 on v2

v3 whole, which is shorter than its diff:
```python
import functools
import math

import jax
import jax.numpy as jnp
from jax import lax
from jax.experimental import pallas as pl
from jax.experimental.pallas import tpu as pltpu
from jax.sharding import PartitionSpec as P

norm_eps = 1e-05
MESH = pl.DeviceIdType.MESH
ANY = pl.BlockSpec(memory_space=pl.ANY)
VMEM = pl.BlockSpec(memory_space=pltpu.VMEM)
SMEM = pl.BlockSpec(memory_space=pltpu.SMEM)
CHAIN_CHUNKS = 16
CHAIN_LAG = 6
PLANE_WIDE = 4
CLIPS = 4
BIG = 56 * 2**20
PLANE_AHEAD = 8
PLANE_LATEST = 24


def at(frame=None, row=None):
    place = {}
    if frame is not None:
        place["frame"] = frame
    if row is not None:
        place["row"] = row
    return place


def tell(sem, **place):
    pl.semaphore_signal(sem, inc=1, device_id=at(**place), device_id_type=MESH)


def push(src, dst, send_sem, recv_sem, **place):
    return pltpu.make_async_remote_copy(
        src_ref=src,
        dst_ref=dst,
        send_sem=send_sem,
        recv_sem=recv_sem,
        device_id=at(**place),
        device_id_type=MESH,
    )


def each(start, stop, body):
    def step(k, carry):
        body(k)
        return carry

    lax.fori_loop(start, stop, step, 0)


def gather_kernel(src, out, y_send, y_recv, x_send, x_recv, c_send, c_recv, local_sem):
    high, wide = out.shape[0], out.shape[1]
    frame = lax.axis_index("frame")
    core, x, y = frame % 2, frame // 2 % wide, frame // (2 * wide)

    def index(y, x, core):
        return (y * wide + x) * 2 + core

    sibling = index(y, x, 1 - core)
    barrier = pltpu.get_barrier_semaphore()
    for k in range(1, high):
        tell(barrier, frame=index((y + k) % high, x, core))
    for k in range(1, wide):
        tell(barrier, frame=index(y, (x + k) % wide, core))
    tell(barrier, frame=sibling)
    own = pltpu.make_async_copy(src, out.at[y, x, core], local_sem)
    own.start()
    pl.semaphore_wait(barrier, high + wide - 1)

    def along_y(k, back=False):
        place = (y + high - k) % high if back else y
        peer = index((y + k) % high, x, core)
        return push(src, out.at[place, x, core], y_send.at[k], y_recv.at[k], frame=peer)

    def along_x(k, i, back=False):
        place = (y + high - k) % high
        held = src if k == 0 else out.at[place, x, core]
        column = (x + wide - i) % wide if back else x
        return push(
            held, out.at[place, column, core], x_send.at[k, i], x_recv.at[k, i],
            frame=index(y, (x + i) % wide, core),
        )

    def across(k, back=False):
        place = (y + high - k) % high
        side = 1 - core if back else core
        held = out.at[place, :, side]
        return push(out.at[place, :, core], held, c_send.at[k], c_recv.at[k], frame=sibling)

    near = sorted(range(1, high), key=lambda k: min(k, high - k))
    for k in near:
        along_y(k).start()
    for i in range(1, wide):
        along_x(0, i).start()
    for k in near:
        along_y(k, True).wait_recv()
        for i in range(1, wide):
            along_x(k, i).start()
    own.wait()
    for k in [0, *near]:
        for i in range(1, wide):
            along_x(k, i, True).wait_recv()
        across(k).start()
    for k in [0, *near]:
        across(k, True).wait_recv()
    for k in near:
        along_y(k).wait_send()
    for k in [0, *near]:
        for i in range(1, wide):
            along_x(k, i).wait_send()
        across(k).wait_send()


def gather(chunk):
    count = lax.axis_size("frame")
    wide = PLANE_WIDE
    high = count // (2 * wide)
    out = pl.pallas_call(
        gather_kernel,
        out_shape=jax.ShapeDtypeStruct((high, wide, 2, *chunk.shape), chunk.dtype),
        in_specs=[VMEM],
        out_specs=VMEM,
        scratch_shapes=[
            pltpu.SemaphoreType.DMA((high,)),
            pltpu.SemaphoreType.DMA((high,)),
            pltpu.SemaphoreType.DMA((high, wide)),
            pltpu.SemaphoreType.DMA((high, wide)),
            pltpu.SemaphoreType.DMA((high,)),
            pltpu.SemaphoreType.DMA((high,)),
            pltpu.SemaphoreType.DMA,
        ],
        compiler_params=pltpu.CompilerParams(collective_id=0, has_side_effects=True),
        name="gather",
    )(chunk)
    return out.reshape(count, *chunk.shape)


def plane_copies(frame, count, pairs, send, recv):
    def out_piece(i, k):
        peer = (frame + k) % count
        src, dst = pairs[i]
        return push(src.at[peer], dst.at[frame], send.at[i, k], recv.at[i, k], frame=peer)

    def in_piece(i, k):
        origin = (frame + count - k) % count
        src, dst = pairs[i]
        return push(src.at[origin], dst.at[origin], send.at[i, k], recv.at[i, k], frame=origin)

    return out_piece, in_piece


def plane_start(frame, count, pairs, send, recv, own_sem, some=None):
    out_piece, unused = plane_copies(frame, count, pairs, send, recv)
    for i, (src, dst) in enumerate(pairs):
        pltpu.make_async_copy(src.at[frame], dst.at[frame], own_sem.at[i]).start()

    def begin(k):
        for i in range(len(pairs)):
            out_piece(i, k).start()

    each(1, count if some is None else some, begin)
    return begin


def plane_wait(frame, count, pairs, send, recv, own_sem):
    out_piece, in_piece = plane_copies(frame, count, pairs, send, recv)

    def end(k):
        for i in range(len(pairs)):
            in_piece(i, k).wait_recv()
            out_piece(i, k).wait_send()

    each(1, count, end)
    for i, (src, dst) in enumerate(pairs):
        pltpu.make_async_copy(src.at[frame], dst.at[frame], own_sem.at[i]).wait()


def exchange_chain_kernel(
    per_head, xs, gs, end_local, own_grad, decay, rx, rg, state_in, later, fwd_out, bwd_out, send, recv, own_sem,
    fwd_send, fwd_recv, bwd_send, bwd_recv,
):
    frame, row = lax.axis_index("frame"), lax.axis_index("row")
    count, bands = lax.axis_size("frame"), lax.axis_size("row")
    height = end_local.shape[0] // CHAIN_CHUNKS
    barrier = pltpu.get_barrier_semaphore()
    each(1, count, lambda k: tell(barrier, frame=(frame + k) % count))

    @pl.when(row > 0)
    def _():
        tell(barrier, row=row - 1)

    @pl.when(row < bands - 1)
    def _():
        tell(barrier, row=row + 1)

    neighbours = jnp.where(row > 0, 1, 0) + jnp.where(row < bands - 1, 1, 0)
    pl.semaphore_wait(barrier, count - 1 + neighbours)

    def rows_of(c):
        return pl.ds(pl.multiple_of(c * height, height), height)

    def fwd(c):
        where = rows_of(c)
        return push(fwd_out.at[where], state_in.at[where], fwd_send.at[c], fwd_recv.at[c], row=row + 1)

    def bwd(c):
        where = rows_of(c)
        return push(bwd_out.at[where], later.at[where], bwd_send.at[c], bwd_recv.at[c], row=row - 1)

    def fwd_in(c):
        where = rows_of(c)
        return push(fwd_out.at[where], state_in.at[where], fwd_send.at[c], fwd_recv.at[c], row=row - 1)

    def bwd_in(c):
        where = rows_of(c)
        return push(bwd_out.at[where], later.at[where], bwd_send.at[c], bwd_recv.at[c], row=row + 1)

    def join(c, before, own, result):
        for j in range(height // per_head):
            where = pl.ds(pl.multiple_of(c * height + j * per_head, per_head), per_head)
            factor = decay[0, c * (height // per_head) + j]
            result[where, :] = (
                before[where, :].astype(jnp.float32) * factor + own[where, :]
            ).astype(result.dtype)

    @pl.when(row == 0)
    def _():
        state_in[...] = jnp.zeros_like(state_in)
        for c in range(CHAIN_CHUNKS):
            fwd_out[rows_of(c), :] = end_local[rows_of(c), :].astype(fwd_out.dtype)
            fwd(c).start()

    @pl.when(row == bands - 1)
    def _():
        later[...] = jnp.zeros_like(later)
        for c in range(CHAIN_CHUNKS):
            bwd_out[rows_of(c), :] = own_grad[rows_of(c), :].astype(bwd_out.dtype)
            bwd(c).start()

    slots = CHAIN_CHUNKS + (bands - 1) * CHAIN_LAG
    ahead = 1 + PLANE_AHEAD
    per_slot = -(-(count - ahead) // (slots - PLANE_LATEST))
    begin = plane_start(frame, count, [(xs, rx), (gs, rg)], send, recv, own_sem, ahead)

    def slot(s):
        f = s - row * CHAIN_LAG
        b = s - (bands - 1 - row) * CHAIN_LAG

        @pl.when(jnp.logical_and(row > 0, jnp.logical_and(f >= 0, f < CHAIN_CHUNKS)))
        def _():
            fwd_in(f).wait_recv()

            @pl.when(row < bands - 1)
            def _():
                join(f, state_in, end_local, fwd_out)
                fwd(f).start()

        @pl.when(jnp.logical_and(row < bands - 1, jnp.logical_and(b >= 0, b < CHAIN_CHUNKS)))
        def _():
            bwd_in(b).wait_recv()

            @pl.when(row > 0)
            def _():
                join(b, later, own_grad, bwd_out)
                bwd(b).start()

        first = jnp.minimum(ahead + s * per_slot, count)
        each(first, jnp.minimum(first + per_slot, count), begin)

    each(0, slots, slot)
    plane_wait(frame, count, [(xs, rx), (gs, rg)], send, recv, own_sem)

    @pl.when(row < bands - 1)
    def _():
        for c in range(CHAIN_CHUNKS):
            fwd(c).wait_send()

    @pl.when(row > 0)
    def _():
        for c in range(CHAIN_CHUNKS):
            bwd(c).wait_send()


def exchange_chain(per_head, xs, gs, end_local, own_grad, decay):
    count = lax.axis_size("frame")
    state = jax.ShapeDtypeStruct(end_local.shape, jnp.bfloat16)
    return pl.pallas_call(
        functools.partial(exchange_chain_kernel, per_head),
        out_shape=(
            jax.ShapeDtypeStruct(xs.shape, xs.dtype),
            jax.ShapeDtypeStruct(gs.shape, gs.dtype),
            state,
            state,
        ),
        in_specs=[ANY, ANY, VMEM, VMEM, SMEM],
        out_specs=(ANY, ANY, VMEM, VMEM),
        scratch_shapes=[
            pltpu.VMEM(end_local.shape, jnp.bfloat16),
            pltpu.VMEM(end_local.shape, jnp.bfloat16),
            pltpu.SemaphoreType.DMA((2, count)),
            pltpu.SemaphoreType.DMA((2, count)),
            pltpu.SemaphoreType.DMA((2,)),
            pltpu.SemaphoreType.DMA((CHAIN_CHUNKS,)),
            pltpu.SemaphoreType.DMA((CHAIN_CHUNKS,)),
            pltpu.SemaphoreType.DMA((CHAIN_CHUNKS,)),
            pltpu.SemaphoreType.DMA((CHAIN_CHUNKS,)),
        ],
        compiler_params=pltpu.CompilerParams(collective_id=1, has_side_effects=True),
        name="exchange_chain",
    )(xs, gs, end_local, own_grad, decay)


def finish_kernel(
    ts, bs, wp, ws, mixed_part, pre_part, tokens, scale,
    mixed_out, tokens_out, mod_out, weight_out,
    rt, rb, proj_parts, step_parts, pre, band, band_low, core_part, half, half_low, y_parts, x_parts, total,
    mod_src, a_parts, b_src, b_parts, z_src, z_parts,
    c_send, c_recv, y_send, y_recv, x_send, x_recv, d_send, d_recv, d_own,
    a_send, a_recv, b_send, b_recv, z_send, z_recv, t_send, t_recv, t_own, w_send, w_recv, w_own,
):
    frame, row = lax.axis_index("frame"), lax.axis_index("row")
    bands = lax.axis_size("row")
    length, width = pre.shape
    lanes = mod_src.shape[2]
    blocks = width // lanes
    wide, high = x_parts.shape[0], y_parts.shape[0]
    tall = total.shape[0]
    core, x, y = frame % 2, frame // 2 % wide, frame // (2 * wide)
    side = half.shape[0]
    coef = proj_parts.shape[2]

    def index(y, x, core):
        return (y * wide + x) * 2 + core

    sibling = index(y, x, 1 - core)
    per_home = 2
    home = row * high + core * (high // 2) + y // per_home
    piece = y % per_home
    from_row, from_core, from_x = frame // high, frame % high // (high // 2), row // per_home

    def source(i):
        return index(frame % (high // 2) * per_home + i, from_x, from_core)

    def other(f, r):
        return jnp.logical_or(f != frame, r != row)

    group = 2 * wide
    own = x * 2 + core

    def mate(k):
        return y * group + (own + k) % group

    barrier = pltpu.get_barrier_semaphore()
    count = lax.axis_size("frame")
    each(1, count, lambda k: tell(barrier, frame=(frame + k) % count))
    each(1, bands, lambda k: tell(barrier, row=(row + k) % bands))
    for i in range(per_home):

        @pl.when(other(source(i), from_row))
        def _():
            tell(barrier, frame=source(i), row=from_row)

    local = jnp.where(home == frame, jnp.where(row // per_home == x, 1, 0), 0)

    squares = jnp.zeros((length, lanes), jnp.float32)
    for j in range(blocks):
        where = slice(j * lanes, (j + 1) * lanes)
        squares += tokens[:, where].astype(jnp.float32) ** 2
    inverse = lax.rsqrt(jnp.sum(squares, axis=1, keepdims=True) * (1.0 / width) + norm_eps)
    pl.semaphore_wait(barrier, count - 1 + bands - 1 + per_home - local)

    def rows_at(k, size):
        return pl.ds(pl.multiple_of(k * size, size), size)

    share = band.shape[0]

    def pieces(j):
        return (wp.at[rows_at(j, share), :], proj_parts), (ws.at[:, rows_at(j, share)], step_parts)

    def w_out(i, k):
        peer = (row + k) % bands
        src, dst = pieces(peer)[i]
        return push(src, dst.at[row], w_send.at[i, k], w_recv.at[i, k], row=peer)

    def w_in(i, k):
        origin = (row + bands - k) % bands
        src, dst = pieces(origin)[i]
        return push(src, dst.at[origin], w_send.at[i, k], w_recv.at[i, k], row=origin)

    def w_self(i):
        src, dst = pieces(row)[i]
        return pltpu.make_async_copy(src, dst.at[row], w_own.at[i])

    def w_begin(k):
        for i in range(2):
            w_out(i, k).start()

    def w_end(k):
        for i in range(2):
            w_in(i, k).wait_recv()
            w_out(i, k).wait_send()

    for i in range(2):
        w_self(i).start()
    each(1, bands, w_begin)
    plane_start(frame, count, [(bs, rb), (ts, rt)], t_send, t_recv, t_own)
    each(1, bands, w_end)
    for i in range(2):
        w_self(i).wait()

    step = 2 * tall
    for i in range(band.shape[0] // step):
        rows = slice(i * step, (i + 1) * step)
        part = proj_parts[0, rows, :].astype(jnp.float32)
        for j in range(1, proj_parts.shape[0]):
            part += proj_parts[j, rows, :].astype(jnp.float32)
        band[rows, :coef] = part
    part = step_parts[0].astype(jnp.float32)
    for j in range(1, step_parts.shape[0]):
        part += step_parts[j].astype(jnp.float32)
    filled = jnp.concatenate([part, jnp.zeros((lanes - part.shape[0], part.shape[1]), jnp.float32)], axis=0)
    band[:, coef:] = filled.T
    band_low[...] = band[...].astype(band_low.dtype)
    across = push(band_low.at[rows_at(1 - core, side), :], core_part, c_send, c_recv, frame=sibling)
    across.start()

    across.wait_recv()
    half[...] = band[rows_at(core, side), :] + core_part[...].astype(jnp.float32)
    half_low[...] = half[...].astype(half_low.dtype)

    def y_out(k):
        peer = (y + k) % high
        return push(
            half_low.at[rows_at(peer, tall), :], y_parts.at[y], y_send.at[k], y_recv.at[k],
            frame=index(peer, x, core),
        )

    def y_in(k):
        origin = (y + high - k) % high
        return push(
            half_low.at[rows_at(0, tall), :], y_parts.at[origin], y_send.at[k], y_recv.at[k],
            frame=index(origin, x, core),
        )

    for k in range(1, high):
        y_out(k).start()
    y_parts[pl.ds(y, 1)] = half_low[rows_at(y, tall), :][None]

    for k in range(1, high):
        y_in(k).wait_recv()
    x_parts[pl.ds(x, 1)] = jnp.sum(y_parts[...].astype(jnp.float32), axis=0)[None]

    def x_out(k):
        return push(
            x_parts.at[x], x_parts.at[x], x_send.at[k], x_recv.at[k], frame=index(y, (x + k) % wide, core)
        )

    def x_in(k):
        origin = (x + wide - k) % wide
        return push(
            x_parts.at[origin], x_parts.at[origin], x_send.at[k], x_recv.at[k], frame=index(y, origin, core)
        )

    for k in range(1, wide):
        x_out(k).start()
    for k in range(1, wide):
        x_in(k).wait_recv()
    total[...] = jnp.sum(x_parts[...], axis=0)

    def d_out(i):
        return push(total, weight_out.at[piece], d_send.at[i], d_recv.at[piece], frame=home, row=x * per_home + i)

    def d_in(i):
        return push(total, weight_out.at[i], d_send.at[0], d_recv.at[i], frame=source(i), row=from_row)

    d_self = pltpu.make_async_copy(total, weight_out.at[piece], d_own)
    for i in range(per_home):
        away = other(home, x * per_home + i)

        @pl.when(away)
        def _():
            d_out(i).start()

        @pl.when(jnp.logical_not(away))
        def _():
            d_self.start()

    plane_wait(frame, count, [(bs, rb), (ts, rt)], t_send, t_recv, t_own)

    along = jnp.zeros((length, lanes), jnp.float32)
    for j in range(blocks):
        where = slice(j * lanes, (j + 1) * lanes)
        value = pre_part[:, where] + read(rb, where).astype(jnp.float32)
        pre[:, where] = value
        matched = value * (tokens[:, where].astype(jnp.float32) * inverse)
        to_y, to_x = j // wide, j % wide
        mod_src[to_x, to_y : to_y + 1, :] = jnp.sum(value, axis=0, keepdims=True)
        to_y += blocks // wide
        mod_src[to_x, to_y : to_y + 1, :] = jnp.sum(matched, axis=0, keepdims=True)
        along += matched * (1.0 + scale[:, where])

    def a_out(k):
        peer = (own + k) % group
        return push(mod_src.at[peer // 2], a_parts.at[own], a_send.at[k], a_recv.at[k], frame=mate(k))

    def a_in(k):
        origin = (own + group - k) % group
        return push(mod_src.at[0], a_parts.at[origin], a_send.at[k], a_recv.at[k], frame=mate(k))

    for k in range(1, group):
        a_out(k).start()
    a_parts[pl.ds(own, 1)] = mod_src[pl.ds(x, 1)]
    along = jnp.sum(along, axis=1, keepdims=True) * (1.0 / width)
    for j in range(blocks):
        where = slice(j * lanes, (j + 1) * lanes)
        unit = tokens[:, where].astype(jnp.float32) * inverse
        pulled = pre[:, where] * (1.0 + scale[:, where])
        tokens_out[:, where] = (inverse * (pulled - unit * along)).astype(tokens_out.dtype)
        mixed_out[:, where] = (mixed_part[:, where] + read(rt, where).astype(jnp.float32)).astype(
            mixed_out.dtype
        )

    for k in range(1, group):
        a_in(k).wait_recv()
    b_src[...] = jnp.sum(a_parts[...], axis=0)

    def b_out(k):
        return push(
            b_src, b_parts.at[y], b_send.at[k], b_recv.at[k], frame=index((y + k) % high, x, core)
        )

    def b_in(k):
        origin = (y + high - k) % high
        return push(b_src, b_parts.at[origin], b_send.at[k], b_recv.at[k], frame=index(origin, x, core))

    for k in range(1, high):
        b_out(k).start()
    b_parts[pl.ds(y, 1)] = b_src[...][None]
    for k in range(1, high):
        b_in(k).wait_recv()
    z_src[...] = jnp.zeros_like(z_src)
    per_clip = high // CLIPS
    for c in range(CLIPS):
        chosen = b_parts[c * per_clip, pl.ds(y, 1), :]
        for i in range(1, per_clip):
            chosen += b_parts[c * per_clip + i, pl.ds(y, 1), :]
        z_src[c : c + 1, :] = chosen

    def z_out(k):
        return push(z_src, z_parts.at[row], z_send.at[k], z_recv.at[k], row=(row + k) % bands)

    def z_in(k):
        origin = (row + bands - k) % bands
        return push(z_src, z_parts.at[origin], z_send.at[k], z_recv.at[k], row=origin)

    for k in range(1, z_parts.shape[0]):
        z_out(k).start()
    z_parts[pl.ds(row, 1)] = z_src[...][None]
    for k in range(1, z_parts.shape[0]):
        z_in(k).wait_recv()
    mod_out[...] = jnp.sum(z_parts[...], axis=0)
    for i in range(per_home):
        came = other(source(i), from_row)

        @pl.when(came)
        def _():
            d_in(i).wait_recv()

        @pl.when(jnp.logical_not(came))
        def _():
            d_self.wait()

    across.wait_send()
    for k in range(1, group):
        a_out(k).wait_send()
    for k in range(1, high):
        y_out(k).wait_send()
        b_out(k).wait_send()
    for k in range(1, wide):
        x_out(k).wait_send()
    for k in range(1, z_parts.shape[0]):
        z_out(k).wait_send()
    for i in range(per_home):

        @pl.when(other(home, x * per_home + i))
        def _():
            d_out(i).wait_send()


def finish(ts, bs, wp, ws, mixed_part, pre_part, tokens, scale):
    count, bands = lax.axis_size("frame"), lax.axis_size("row")
    length, width = tokens.shape
    lanes = 128
    wide = PLANE_WIDE
    high = count // (2 * wide)
    share, coef = width // bands, wp.shape[1] + lanes
    tall = share // 2 // high
    low = jax.ShapeDtypeStruct(tokens.shape, tokens.dtype)
    f32, bf16 = jnp.float32, jnp.bfloat16
    sems = pltpu.SemaphoreType.DMA
    return pl.pallas_call(
        finish_kernel,
        out_shape=(
            low,
            low,
            jax.ShapeDtypeStruct((8, lanes), f32),
            jax.ShapeDtypeStruct((2, tall, coef), f32),
        ),
        in_specs=[VMEM] * 8,
        out_specs=(VMEM,) * 4,
        scratch_shapes=[
            pltpu.VMEM(ts.shape, bf16),
            pltpu.VMEM(bs.shape, bf16),
            pltpu.VMEM((bands, share, wp.shape[1]), bf16),
            pltpu.VMEM((bands, ws.shape[0], share), bf16),
            pltpu.VMEM((length, width), f32),
            pltpu.VMEM((share, coef), f32),
            pltpu.VMEM((share, coef), bf16),
            pltpu.VMEM((share // 2, coef), bf16),
            pltpu.VMEM((share // 2, coef), f32),
            pltpu.VMEM((share // 2, coef), bf16),
            pltpu.VMEM((high, tall, coef), bf16),
            pltpu.VMEM((wide, tall, coef), f32),
            pltpu.VMEM((tall, coef), f32),
            pltpu.VMEM((wide, high, lanes), f32),
            pltpu.VMEM((2 * wide, high, lanes), f32),
            pltpu.VMEM((high, lanes), f32),
            pltpu.VMEM((high, high, lanes), f32),
            pltpu.VMEM((8, lanes), f32),
            pltpu.VMEM((bands, 8, lanes), f32),
            sems,
            sems,
            sems((high,)),
            sems((high,)),
            sems((wide,)),
            sems((wide,)),
            sems((2,)),
            sems((2,)),
            sems,
            sems((2 * wide,)),
            sems((2 * wide,)),
            sems((high,)),
            sems((high,)),
            sems((bands,)),
            sems((bands,)),
            sems((2, count)),
            sems((2, count)),
            sems((2,)),
            sems((2, bands)),
            sems((2, bands)),
            sems((2,)),
        ],
        compiler_params=pltpu.CompilerParams(collective_id=3, has_side_effects=True, vmem_limit_bytes=BIG),
        name="finish",
    )(ts, bs, wp, ws, mixed_part, pre_part, tokens, scale)


def time_embed(timestep, embed_dim):
    half_dim = embed_dim // 2
    frequency = jnp.exp(-math.log(10000.0) * jnp.arange(half_dim, dtype=jnp.float32) / half_dim)
    angles = timestep.astype(jnp.float32)[:, None] * frequency[None, :]
    return jax.nn.silu(jnp.concatenate([jnp.cos(angles), jnp.sin(angles)], axis=1))


def halves(values):
    high = values.astype(jnp.bfloat16)
    return high, (values - high.astype(jnp.float32)).astype(jnp.bfloat16)


def mm(a, b):
    return jnp.dot(a, b, preferred_element_type=jnp.float32)


def mm_nt(a, b):
    return lax.dot_general(a, b, (((1,), (1,)), ((), ())), preferred_element_type=jnp.float32)


def mm_tn(a, b):
    return lax.dot_general(a, b, (((0,), (0,)), ((), ())), preferred_element_type=jnp.float32)


def with_ones(ones, values, dot):
    first = values.astype(jnp.bfloat16)
    rest = values - first.astype(jnp.float32)
    second = rest.astype(jnp.bfloat16)
    third = (rest - second.astype(jnp.float32)).astype(jnp.bfloat16)
    return dot(ones, first) + dot(ones, second) + dot(ones, third)


def earlier_mask(length, sites):
    t = lax.broadcasted_iota(jnp.int32, (length, length), 0)
    u = lax.broadcasted_iota(jnp.int32, (length, length), 1)
    return jnp.logical_and(u <= t, lax.rem(t, sites) == lax.rem(u, sites))


def steps_of(logits, bias, rate, mask):
    raised = logits.astype(jnp.float32) + bias
    step = jnp.maximum(raised, 0.0) + jnp.log1p(jnp.exp(-jnp.abs(raised)))
    lower = jnp.where(mask, 1.0, 0.0).astype(jnp.bfloat16)
    return raised, step, with_ones(lower, -step * rate, mm)


def stacked(values):
    parts = [halves(v) for v in values]
    return jnp.concatenate([p[0] for p in parts] + [p[1] for p in parts], axis=0)


def split_sum(product, sizes):
    total = sum(sizes)
    result, start = [], 0
    for size in sizes:
        result.append(product[start : start + size] + product[total + start : total + start + size])
        start += size
    return result


def spread(columns, expand, where):
    length = columns.shape[0]
    return split_sum(mm(columns, expand[:, where]), [length // 2])[0]


def per_head(values, expand, where):
    return split_sum(mm_nt(stacked(values), expand[:, where]), [v.shape[0] for v in values])


def head_kernel(
    tokens, grad, weights, step_w, shift, scale, small, expand,
    normed_out, coeff_out, logit_out, end_out, own_out, decay_out,
):
    length, width = tokens.shape
    lanes = step_w.shape[1]
    values = tokens[...].astype(jnp.float32)
    inverse = lax.rsqrt(jnp.mean(values * values, axis=1, keepdims=True) + norm_eps)
    normed_out[...] = (values * inverse * (1.0 + scale[...]) + shift[...]).astype(jnp.bfloat16)
    project(normed_out, weights, step_w, coeff_out, logit_out)
    b_part, c_part = coeff_out[:, :lanes], coeff_out[:, lanes:]
    mask = earlier_mask(length, 1)
    unused, step, log = steps_of(logit_out[...], small[0:1, :], small[1:2, :], mask)
    last = log[length - 1 :, :]
    decay_out[...] = jnp.exp(last)
    lead = jnp.exp(last - log) * step
    reach = jnp.exp(log) * (1.0 / lanes)
    columns = stacked([lead, reach])
    for j in range(width // lanes):
        where = slice(j * lanes, (j + 1) * lanes)
        wide = spread(columns, expand, where)
        scaled = (normed_out[:, where].astype(jnp.float32) * wide[:length]).astype(jnp.bfloat16)
        end_out[where, :] = mm_tn(scaled, b_part)
        pulled = (grad[:, where].astype(jnp.float32) * wide[length:]).astype(jnp.bfloat16)
        own_out[where, :] = mm_tn(pulled, c_part)


def project(normed, weights, step_w, coeff_out, logit_out):
    lanes = step_w.shape[1]
    count = weights.shape[0]
    depth = normed.shape[1] // count
    for i in range(2):
        w = weights[:, i * depth : (i + 1) * depth, :].reshape(count * depth, lanes)
        coeff_out[:, i * lanes : (i + 1) * lanes] = mm(normed[...], w).astype(jnp.bfloat16)
    logit_out[...] = mm(normed[...], step_w[...]).astype(jnp.bfloat16)


def read(ref, where):
    if len(ref.shape) == 2:
        return ref[:, where]
    values = ref[:, :, where]
    return values.reshape(ref.shape[0] * ref.shape[1], values.shape[2])


def write(ref, where, values):
    values = values.astype(ref.dtype)
    if len(ref.shape) == 2:
        ref[:, where] = values
    else:
        ref[:, :, where] = values.reshape(*ref.shape[:2], values.shape[1])


def scan_pass(
    x_ref, g_ref, coeffs, logits, bias, rate, weights, step_w, expand, skip, state, later,
    mixed_ref, dx_ref, back_ref, wp_ref, ws_ref, sites, first,
):
    length, width = x_ref.shape
    lanes = coeffs.shape[1] // 2
    space = state is not None
    b_part, c_part = coeffs[:, :lanes], coeffs[:, lanes:]
    mask = earlier_mask(length, sites)
    raised, step, log = steps_of(logits[...], bias, rate, mask)
    log_t = log.T
    scores = jnp.where(mask, mm_nt(c_part, b_part) * (1.0 / lanes), 0.0)
    left = lax.broadcasted_iota(jnp.int32, (length, lanes), 1) < lanes // 2
    d_scores = jnp.zeros((length, length), jnp.float32)
    pull_out = jnp.zeros((length, lanes), jnp.float32)
    pull_in = jnp.zeros((length, lanes), jnp.float32)
    d_b = jnp.zeros((length, lanes), jnp.float32)
    d_c = jnp.zeros((length, lanes), jnp.float32)
    if space:
        last = log[length - 1 :, :]
        reach_all = jnp.exp(log) * (1.0 / lanes)
        fade_all = jnp.exp(last - log)
        d_last = jnp.zeros((16, lanes), jnp.float32)
        state_rows = []
        columns = stacked([step, reach_all, fade_all, skip])
    else:
        columns = stacked([step])
    for j in range(width // lanes):
        where = slice(j * lanes, (j + 1) * lanes)
        x, g = read(x_ref, where), read(g_ref, where)
        wide_x, wide_g = x.astype(jnp.float32), g.astype(jnp.float32)
        spread_all = spread(columns, expand, where)
        step_x = spread_all[:length]
        stepped_wide = wide_x * step_x
        stepped = stepped_wide.astype(jnp.bfloat16)
        falls = []
        for h in (2 * j, 2 * j + 1):
            falls.append(jnp.exp(jnp.minimum(log[:, h : h + 1] - log_t[h : h + 1, :], 0.0)))
        pair = [(scores * fall).astype(jnp.bfloat16) for fall in falls]
        outs = mm(jnp.concatenate(pair, axis=0), stepped)
        backs = mm_tn(jnp.concatenate(pair, axis=1), g)
        left_g = jnp.where(left, wide_g, 0.0).astype(jnp.bfloat16)
        right_g = jnp.where(left, 0.0, wide_g).astype(jnp.bfloat16)
        d_pair = mm_nt(jnp.concatenate([left_g, right_g], axis=0), stepped)
        d_scores += d_pair[:length] * falls[0] + d_pair[length:] * falls[1]
        out = jnp.where(left, outs[:length], outs[length:])
        d_step_x = jnp.where(left, backs[:length], backs[length:])
        if space:
            held, late = state[where, :], later[where, :]
            reach, fade = spread_all[length : 2 * length], spread_all[2 * length : 3 * length]
            gain = spread_all[3 * length : 3 * length + 1]
            out += mm_nt(c_part, held) * reach
            d_c += mm((wide_g * reach).astype(jnp.bfloat16), held)
            from_end = mm_nt(b_part, late) * fade
            d_step_x += from_end
            d_b += mm((stepped_wide * fade).astype(jnp.bfloat16), late)
            to_last = jnp.sum(stepped_wide * from_end, axis=0, keepdims=True)
            both = held.astype(jnp.float32) * late.astype(jnp.float32)
            half = lanes // 2
            state_rows += [
                jnp.sum(both[:half], axis=0, keepdims=True),
                jnp.sum(both[half:], axis=0, keepdims=True),
            ]
            mixed_ref[:, where] = out + gain * wide_x
            direct = (wide_g * gain).astype(jnp.bfloat16).astype(jnp.float32)
            dx_ref[:, where] = step_x * d_step_x + direct
        else:
            write(mixed_ref, where, out)
            dx_ref[:, where] = step_x * d_step_x
        sums = [wide_g * out, wide_x * d_step_x]
        if space:
            sums.append(jnp.broadcast_to(to_last, (16, lanes)))
        sums = per_head(sums, expand, where)
        pull_out += sums[0]
        pull_in += sums[1]
        if space:
            d_last += sums[2]
    d_low = (jnp.where(mask, d_scores, 0.0) * (1.0 / lanes)).astype(jnp.bfloat16)
    d_c += mm(d_low, b_part)
    d_b += mm_tn(d_low, c_part)
    d_log = pull_out - step * pull_in
    if space:
        states = jnp.concatenate([*state_rows, jnp.zeros((lanes - len(state_rows), lanes), jnp.float32)], axis=0)
        high, low = halves(states)
        ones = jnp.ones((16, lanes), jnp.bfloat16)
        d_last += (mm_nt(ones, high) + mm_nt(ones, low)) * jnp.exp(last)
        at_end = lax.broadcasted_iota(jnp.int32, (length, lanes), 0) == length - 1
        d_log += jnp.where(at_end, d_last[:1, :], 0.0)
    lower = jnp.where(mask, 1.0, 0.0).astype(jnp.bfloat16)
    d_fall = with_ones(lower, d_log, mm_tn)
    d_step = pull_in - rate * d_fall
    d_logit = (d_step * jax.nn.sigmoid(raised)).astype(jnp.bfloat16)
    low_b, low_c = d_b.astype(jnp.bfloat16), d_c.astype(jnp.bfloat16)
    count = weights.shape[0]
    depth = width // count
    block = 8
    for k in range(count // block):
        cols = slice(k * block * depth, (k + 1) * block * depth)
        w_b = weights[k * block : (k + 1) * block, :depth, :].reshape(block * depth, lanes)
        w_c = weights[k * block : (k + 1) * block, depth : 2 * depth, :].reshape(block * depth, lanes)
        total = (
            dx_ref[:, cols] + mm_nt(low_b, w_b) + mm_nt(low_c, w_c) + mm_nt(d_logit, step_w[cols, :])
        )
        write(back_ref, cols, total)
        x = x_ref[:, cols]
        terms = ((wp_ref, cols, slice(0, lanes), mm_tn(x, low_b)), (wp_ref, cols, slice(lanes, None), mm_tn(x, low_c)))
        terms += ((ws_ref, slice(None), cols, mm_tn(d_logit, x)[: ws_ref.shape[0]]),)
        for ref, rows, columns, term in terms:
            ref[rows, columns] = term if first else ref[rows, columns] + term


def core_kernel(
    normed, grad, coeffs, logits, state, later, site_tokens, site_grad, weights, step_w, shift_all, scale_all,
    small, expand,
    mixed_out, pre_out, time_out, back_out, wp_out, ws_out, site_normed, site_coeffs, site_logits, dx, wp, ws,
):
    length, width = normed.shape
    bias, rate_space, rate_time = (small[i : i + 1, :] for i in range(3))
    skip = jnp.broadcast_to(small[3:4, :], (16, small.shape[1]))
    clips = shift_all.shape[0]
    sites = length // weights.shape[0]
    part = length // clips
    for c in range(clips):
        rows = slice(c * part, (c + 1) * part)
        frames = slice(c * part // sites, (c + 1) * part // sites)
        values = site_tokens[frames].reshape(part, width).astype(jnp.float32)
        inverse = lax.rsqrt(jnp.mean(values * values, axis=1, keepdims=True) + norm_eps)
        site_normed[rows, :] = (
            values * inverse * (1.0 + scale_all[c : c + 1, :]) + shift_all[c : c + 1, :]
        ).astype(jnp.bfloat16)
    project(site_normed, weights, step_w, site_coeffs, site_logits)
    scan_pass(
        site_normed, site_grad, site_coeffs, site_logits, bias, rate_time, weights, step_w, expand,
        None, None, None, time_out, dx, back_out, wp, ws, sites, True,
    )
    scan_pass(
        normed, grad, coeffs, logits, bias, rate_space, weights, step_w, expand,
        skip, state, later, mixed_out, dx, pre_out, wp, ws, 1, False,
    )
    wp_out[...] = wp[...].astype(jnp.bfloat16)
    ws_out[...] = ws[...].astype(jnp.bfloat16)


def head(tokens, grad, weights, step_w, shift, scale, small, expand):
    length, width = tokens.shape
    lanes = step_w.shape[1]
    low = functools.partial(jax.ShapeDtypeStruct, dtype=jnp.bfloat16)
    wide = functools.partial(jax.ShapeDtypeStruct, dtype=jnp.float32)
    return pl.pallas_call(
        head_kernel,
        out_shape=(
            low((length, width)),
            low((length, 2 * lanes)),
            low((length, lanes)),
            wide((width, lanes)),
            wide((width, lanes)),
            wide((1, lanes)),
        ),
        in_specs=[VMEM] * 8,
        out_specs=(VMEM,) * 6,
        compiler_params=pltpu.CompilerParams(vmem_limit_bytes=BIG),
        name="head",
    )(tokens, grad, weights, step_w, shift, scale, small, expand)


def core(heads, *operands):
    normed, coeffs, weights = operands[0], operands[2], operands[8]
    length, width = normed.shape
    lanes = coeffs.shape[1] // 2
    low = functools.partial(jax.ShapeDtypeStruct, dtype=jnp.bfloat16)
    wide = functools.partial(jax.ShapeDtypeStruct, dtype=jnp.float32)
    return pl.pallas_call(
        core_kernel,
        out_shape=(
            wide((length, width)),
            wide((length, width)),
            low(operands[6].shape),
            low(operands[6].shape),
            low((width, 2 * lanes)),
            low((heads, width)),
        ),
        in_specs=[VMEM] * 14,
        out_specs=(VMEM,) * 6,
        scratch_shapes=[
            pltpu.VMEM((length, width), jnp.bfloat16),
            pltpu.VMEM((length, 2 * lanes), jnp.bfloat16),
            pltpu.VMEM((length, lanes), jnp.bfloat16),
            pltpu.VMEM((length, width), jnp.float32),
            pltpu.VMEM((width, 2 * lanes), jnp.float32),
            pltpu.VMEM((heads, width), jnp.float32),
        ],
        compiler_params=pltpu.CompilerParams(vmem_limit_bytes=BIG),
        name="core",
    )(*operands)


def three_parts(values):
    first = lax.reduce_precision(values, 8, 7)
    second = lax.reduce_precision(values - first, 8, 7)
    return first, second, values - first - second


def per_device(
    tokens,
    cotangent,
    timestep,
    mod_weight,
    proj_weight,
    step_weight,
    step_bias,
    rate_space,
    rate_time,
    skip_gain,
):
    frame_count = lax.axis_size("frame")
    row_count = lax.axis_size("row")
    frame_id = lax.axis_index("frame")
    feat_width = tokens.shape[-1]
    band_len = tokens.shape[1] * tokens.shape[2]
    clip_count = timestep.shape[0]
    clip_frames = frame_count // clip_count
    site_count = band_len // frame_count
    head_count = rate_space.shape[0]
    state_size = proj_weight.shape[1] // 2
    depth = proj_weight.shape[0]
    clip_id = frame_id // clip_frames
    factor = (frame_count * row_count * band_len) ** (-0.5)
    tokens = tokens.reshape(band_len, feat_width)
    flat_grad = cotangent.reshape(band_len, feat_width)

    activated = time_embed(timestep, mod_weight.shape[0]).astype(jnp.bfloat16)
    mod_cols = jnp.dot(activated, mod_weight, preferred_element_type=jnp.float32)
    lane = state_size
    mod_rows = [part.reshape(-1, lane).astype(jnp.bfloat16) for part in three_parts(mod_cols)]
    rows = [proj_weight[:, :state_size], proj_weight[:, state_size:], step_weight.reshape(-1, lane), *mod_rows]
    used = sum(r.shape[0] for r in rows)
    chunk = jnp.concatenate([*rows, jnp.zeros((-used % 16, lane), jnp.bfloat16)], axis=0)
    gathered = gather(chunk)
    step_rows = depth * head_count // lane
    step_full = gathered[:, 2 * depth : 2 * depth + step_rows].reshape(feat_width, head_count)
    step_w = jnp.pad(step_full, ((0, 0), (0, lane - head_count)))
    mod_height = mod_rows[0].shape[0]
    mod_parts = gathered[:, 2 * depth + step_rows : 2 * depth + step_rows + 3 * mod_height]
    mod_parts = mod_parts.astype(jnp.float32).reshape(frame_count, 3, clip_count, -1)
    modulation = mod_parts[:, 0] + mod_parts[:, 1] + mod_parts[:, 2]
    modulation = modulation.transpose(1, 0, 2).reshape(clip_count, 2 * feat_width)
    shift_all, scale_all = modulation[:, :feat_width], modulation[:, feat_width:]
    shift_vec = lax.dynamic_index_in_dim(shift_all, clip_id, 0)
    scale_vec = lax.dynamic_index_in_dim(scale_all, clip_id, 0)

    small = jnp.pad(jnp.stack([step_bias, rate_space, rate_time, skip_gain]), ((0, 4), (0, lane - head_count)))
    channel_head = jnp.arange(feat_width) // (feat_width // head_count)
    expand = (channel_head[None, :] == jnp.arange(lane)[:, None]).astype(jnp.bfloat16)
    normed, coeffs, logits, end_local, own_grad, end_decay = head(
        tokens, flat_grad, gathered, step_w, shift_vec, scale_vec, small, expand
    )
    site_tokens, site_grad, state_in, later_grad = exchange_chain(
        feat_width // head_count,
        tokens.reshape(frame_count, site_count, feat_width),
        flat_grad.reshape(frame_count, site_count, feat_width),
        end_local,
        own_grad,
        end_decay,
    )
    mixed_part, pre_part, time_out, time_back, proj_grad, step_grad = core(
        head_count,
        normed,
        flat_grad,
        coeffs,
        logits,
        state_in,
        later_grad,
        site_tokens,
        site_grad,
        gathered,
        step_w,
        shift_all,
        scale_all,
        small,
        expand,
    )
    mixed, d_tokens, mod_sum, weight_sum = finish(
        time_out,
        time_back,
        proj_grad,
        step_grad,
        mixed_part,
        pre_part,
        tokens,
        scale_vec,
    )
    weight_rows = weight_sum.reshape(depth, -1) * factor
    grad_proj = weight_rows[:, : 2 * state_size]
    grad_step = weight_rows[:, 2 * state_size : 2 * state_size + head_count]
    mod_width = mod_weight.shape[1]
    mod_half = lax.dynamic_slice_in_dim(mod_sum[:clip_count], frame_id % 2 * mod_width, mod_width, axis=1)
    grad_mod = (
        jnp.dot(activated.astype(jnp.float32).T, mod_half, precision=lax.Precision.HIGHEST) * factor
    )
    shape = cotangent.shape
    return (
        mixed.reshape(shape),
        d_tokens.reshape(shape),
        grad_proj,
        grad_step,
        grad_mod,
    )


def solution(mesh):
    placed = (
        P("frame", "row", None, None),
        P("frame", "row", None, None),
        P(),
        P(None, "frame"),
        P("frame", None),
        P("frame", None),
        P(),
        P(),
        P(),
        P(),
    )
    return jax.shard_map(
        per_device,
        mesh=mesh,
        in_specs=placed,
        out_specs=(
            P("frame", "row", None, None),
            P("frame", "row", None, None),
            P("frame", None),
            P("frame", None),
            P(None, "frame"),
        ),
        check_vma=False,
    )
```

time: 215 us -> 185 us (0.86)
  local copies, waits for them, and re-layouts: 25.2 us -> 15.1 us
  Pallas kernels: 172 us -> 162 us
  other arithmetic: 13.3 us -> 4.82 us
    reshape x7 -> x0, local copies, waits for them, and re-layouts: 7.8 us -> none  [the longest x1 2.23 us: per_device(): time_out.reshape(frame_count, site_count, feat_width)]
    reduce_sum x6 -> x0, other arithmetic: 6.67 us -> none  [the longest x1 1.67 us: per_device(): scale_grad = jnp.sum(pre_grad * unit_rows, axis=0)]
    pallas_call x1, Pallas kernels: 21.6 us -> 16.8 us  [core(): pl.pallas_call(core_kernel, out_shape=(wide((length, width)), wide((lengt...]
    pallas_call x1, Pallas kernels: 10.7 us -> 8.03 us  [head(): pl.pallas_call(head_kernel, out_shape=(low((length, width)), low((length,...]
    pallas_call x4 -> x2, Pallas kernels: 117 us -> 115 us  [the longest x1 66.9 us: finish(): pl.pallas_call(finish_kernel, out_shape=(low, low, jax.ShapeDtypeStruct((...]
where the time goes in v3:
time: 185 us; the launch traced here: 184 us
  Pallas kernels  162 us (88%)
  local copies, waits for them, and re-layouts  15.1 us (8%)
  other arithmetic  4.82 us (3%)
    pallas_call x1, Pallas kernels, finish(): pl.pallas_call(finish_kernel, out_shape=(low, low, jax.ShapeDtypeStruct((...  66.9 us
    pallas_call x1, Pallas kernels, exchange_chain(): pl.pallas_call(functools.partial(exchange_chain_kernel, per_head), out_sh...  48 us
    pallas_call x1, Pallas kernels, gather(): pl.pallas_call(gather_kernel, out_shape=jax.ShapeDtypeStruct((high, wide,...  22.7 us
    pallas_call x1, Pallas kernels, core(): pl.pallas_call(core_kernel, out_shape=(wide((length, width)), wide((lengt...  16.8 us
    pallas_call x1, Pallas kernels, head(): pl.pallas_call(head_kernel, out_shape=(low((length, width)), low((length,...  8.03 us

profile of v3, /device:TPU:1, one launch (start us, length us, event | category | flops | bytes accessed | tf_op | source)
XLA Modules:
  0.0 184.2 jit_solution(16678603408240415997)
XLA Ops:
  0.6 0.0 copy-start
  0.6 0.0 copy-start.1
  0.7 0.7 convert_element_type.35
  1.4 0.8 reshape.72
  2.2 0.1 multiply_cosine_fusion
  2.3 0.0 copy-done
  2.3 0.1 fusion.6
  2.4 0.1 convert_element_type.42
  2.5 0.1 convert_element_type.40
  2.6 0.1 convert_element_type.38
  2.7 1.3 select_maximum_fusion.small
  4.0 0.7 fusion.13
  4.7 2.4 %concatenate.7.src = bf16[80,128]{1,0:T(8,128)(2,1)} concatenate(bf16[32,128]{1,0:T(8,128)(2,1)S(1)} %get-tuple-element.48, bf16[32,128]{1,0:T(8,128)(2,1)S(1)} %get-tuple-element.47, bf16[8,128]{1,0:T(8,128)(2,1)S(1)} %reshape.72, bf16[2,128]{1,0:T(2,128)(2,1)S(1)} %convert_element_type.38, bf16[2,128]{1,0:T(2,128)(2,1)S(1)} %convert_element_type.40, ...), dimensions={0} | concatenate | bytes 40960 | tf_op jit(solution)/shard_map/concatenate | solution.py:1020
  7.1 0.9 fusion.expand
  8.0 2.2 %reshape_reshape.6.xs = bf16[64,2,2048]{2,1,0:T(2,128)(2,1)} reshape(bf16[1,1,128,2048]{3,2,1,0:T(8,128)(2,1)} %param.10) | data formatting | bytes 1048576 | tf_op jit(solution)/shard_map/reshape;reshape | solution.py:1042
  10.2 0.0 copy-done.1
  10.2 1.1 reshape_reshape.7.gs
  11.3 22.7 %gather.1 = bf16[8,4,2,80,128]{4,3,2,1,0:T(8,128)(2,1)} custom-call(bf16[80,128]{1,0:T(8,128)(2,1)} %concatenate.7.src), custom_call_target="tpu_custom_call" | custom-call | tf_op jit(solution)/shard_map/gather/pallas_call | solution.py:124
  34.1 0.9 slice.48
  35.0 0.9 slice_convert_fusion
  35.9 0.2 reshape.81
  36.2 0.1 reshape.77
  36.3 0.0 copy-start.3
  36.3 0.0 copy-start.4
  36.4 0.6 constant_dynamic-slice_fusion
  37.0 0.2 reshape.74
  37.2 0.9 pad.8.step_w
  38.1 8.0 %head.1 = (bf16[128,2048]{1,0:T(8,128)(2,1)}, bf16[128,256]{1,0:T(8,128)(2,1)}, bf16[128,128]{1,0:T(8,128)(2,1)}, f32[2048,128]{1,0:T(8,128)}, f32[2048,128]{1,0:T(8,128)}, /*index=5*/f32[1,128]{1,0:T(1,128)}) custom-call(bf16[128,2048]{1,0:T(8,128)(2,1)} %bitcast.25, bf16[128,2048]{1,0:T(8,128)(2,1)} %bitcast.23, bf16[64,80,128]{2,1,0:T(8,128)(2,1)} %bitcast.21, ...), custom_call_target="tpu_custom_call" | custom-call | tf_op jit(solution)/shard_map/head/pallas_call | solution.py:932
  46.2 0.0 copy-done.3
  46.2 0.0 copy-done.4
  46.2 48.0 %exchange_chain.1 = (bf16[64,2,2048]{2,1,0:T(2,128)(2,1)}, bf16[64,2,2048]{2,1,0:T(2,128)(2,1)}, bf16[2048,128]{1,0:T(8,128)(2,1)}, bf16[2048,128]{1,0:T(8,128)(2,1)}) custom-call(bf16[64,2,2048]{2,1,0:T(2,128)(2,1)} %reshape_reshape.6.xs, bf16[64,2,2048]{2,1,0:T(2,128)(2,1)} %reshape_reshape.7.gs, f32[2048,128]{1,0:T(8,128)} %get-tuple-element.28.end_local, ...), custom_call_target="tpu_custom_call" | custom-call | tf_op jit(solution)/shard_map/exchange_chain/pallas_call | solution.py:293
  94.1 16.8 %core.1 = (f32[128,2048]{1,0:T(8,128)}, f32[128,2048]{1,0:T(8,128)}, bf16[64,2,2048]{2,1,0:T(2,128)(2,1)}, bf16[64,2,2048]{2,1,0:T(2,128)(2,1)}, bf16[2048,256]{1,0:T(8,128)(2,1)}, /*index=5*/bf16[32,2048]{1,0:T(8,128)(2,1)}) custom-call(bf16[128,2048]{1,0:T(8,128)(2,1)} %get-tuple-element.25.normed, bf16[128,2048]{1,0:T(8,128)(2,1)} %bitcast.24, ...), custom_call_target="tpu_custom_call" | custom-call | tf_op jit(solution)/shard_map/core/pallas_call | solution.py:955
  110.9 66.9 %finish.1 = (bf16[128,2048]{1,0:T(8,128)(2,1)}, bf16[128,2048]{1,0:T(8,128)(2,1)}, f32[8,128]{1,0:T(8,128)}, f32[2,16,384]{2,1,0:T(8,128)}) custom-call(bf16[64,2,2048]{2,1,0:T(2,128)(2,1)} %get-tuple-element.35.ts, bf16[64,2,2048]{2,1,0:T(2,128)(2,1)} %get-tuple-element.36.bs, bf16[2048,256]{1,0:T(8,128)(2,1)} %get-tuple-element.37.wp, ...), custom_call_target="tpu_custom_call" | custom-call | tf_op jit(solution)/shard_map/finish/pallas_call | solution.py:607
  177.8 0.0 copy-start.2
  177.8 0.7 slice.47
  178.6 0.8 broadcast_multiply_fusion
  179.4 0.6 slice.56
  180.0 0.6 slice.55
  180.6 0.9 convolution_multiply_fusion
  181.5 1.9 %copy.21 = bf16[1,1,128,2048]{3,2,1,0:T(8,128)(2,1)} copy(bf16[1,1,128,2048]{3,2,1,0:T(8,128)(2,1)} %bitcast.28) | data formatting | bytes 1048576
  183.4 0.0 copy-done.2
  183.4 0.8 copy.22
  (6 shorter events, 0.1 us)
Async XLA Ops:
  0.6 1.7 copy-start
  0.6 9.6 %copy-start.1 = (bf16[1,1,128,2048]{3,2,1,0:T(8,128)(2,1)S(1)}, bf16[1,1,128,2048]{3,2,1,0:T(8,128)(2,1)}, u32[]{:S(2)}) copy-start(bf16[1,1,128,2048]{3,2,1,0:T(8,128)(2,1)} %param.11) | copy-start | bytes 1572868
  36.3 9.8 %copy-start.3 = (f32[4,2048]{1,0:T(4,128)}, f32[4,2048]{1,0:T(4,128)S(1)}, u32[]{:S(2)}) copy-start(f32[4,2048]{1,0:T(4,128)S(1)} %get-tuple-element.45.scale_all) | copy-start | bytes 98308
  36.3 9.8 %copy-start.4 = (f32[4,2048]{1,0:T(4,128)}, f32[4,2048]{1,0:T(4,128)S(1)}, u32[]{:S(2)}) copy-start(f32[4,2048]{1,0:T(4,128)S(1)} %get-tuple-element.46.shift_all) | copy-start | bytes 98308
  177.8 5.6 %copy-start.2 = (bf16[128,2048]{1,0:T(8,128)(2,1)S(1)}, bf16[128,2048]{1,0:T(8,128)(2,1)}, u32[]{:S(2)}) copy-start(bf16[128,2048]{1,0:T(8,128)(2,1)} %get-tuple-element.42) | copy-start | bytes 1572868

commit v4 on v3

--- a/solution.py
+++ b/solution.py
@@ -452,45 +452,6 @@
         y_out(k).start()
     y_parts[pl.ds(y, 1)] = half_low[rows_at(y, tall), :][None]
 
-    for k in range(1, high):
-        y_in(k).wait_recv()
-    x_parts[pl.ds(x, 1)] = jnp.sum(y_parts[...].astype(jnp.float32), axis=0)[None]
-
-    def x_out(k):
-        return push(
-            x_parts.at[x], x_parts.at[x], x_send.at[k], x_recv.at[k], frame=index(y, (x + k) % wide, core)
-        )
-
-    def x_in(k):
-        origin = (x + wide - k) % wide
-        return push(
-            x_parts.at[origin], x_parts.at[origin], x_send.at[k], x_recv.at[k], frame=index(y, origin, core)
-        )
-
-    for k in range(1, wide):
-        x_out(k).start()
-    for k in range(1, wide):
-        x_in(k).wait_recv()
-    total[...] = jnp.sum(x_parts[...], axis=0)
-
-    def d_out(i):
-        return push(total, weight_out.at[piece], d_send.at[i], d_recv.at[piece], frame=home, row=x * per_home + i)
-
-    def d_in(i):
-        return push(total, weight_out.at[i], d_send.at[0], d_recv.at[i], frame=source(i), row=from_row)
-
-    d_self = pltpu.make_async_copy(total, weight_out.at[piece], d_own)
-    for i in range(per_home):
-        away = other(home, x * per_home + i)
-
-        @pl.when(away)
-        def _():
-            d_out(i).start()
-
-        @pl.when(jnp.logical_not(away))
-        def _():
-            d_self.start()
-
     plane_wait(frame, count, [(bs, rb), (ts, rt)], t_send, t_recv, t_own)
 
     along = jnp.zeros((length, lanes), jnp.float32)
@@ -516,6 +477,23 @@
     for k in range(1, group):
         a_out(k).start()
     a_parts[pl.ds(own, 1)] = mod_src[pl.ds(x, 1)]
+    for k in range(1, high):
+        y_in(k).wait_recv()
+    x_parts[pl.ds(x, 1)] = jnp.sum(y_parts[...].astype(jnp.float32), axis=0)[None]
+
+    def x_out(k):
+        return push(
+            x_parts.at[x], x_parts.at[x], x_send.at[k], x_recv.at[k], frame=index(y, (x + k) % wide, core)
+        )
+
+    def x_in(k):
+        origin = (x + wide - k) % wide
+        return push(
+            x_parts.at[origin], x_parts.at[origin], x_send.at[k], x_recv.at[k], frame=index(y, origin, core)
+        )
+
+    for k in range(1, wide):
+        x_out(k).start()
     along = jnp.sum(along, axis=1, keepdims=True) * (1.0 / width)
     for j in range(blocks):
         where = slice(j * lanes, (j + 1) * lanes)
@@ -542,6 +520,28 @@
     for k in range(1, high):
         b_out(k).start()
     b_parts[pl.ds(y, 1)] = b_src[...][None]
+    for k in range(1, wide):
+        x_in(k).wait_recv()
+    total[...] = jnp.sum(x_parts[...], axis=0)
+
+    def d_out(i):
+        return push(total, weight_out.at[piece], d_send.at[i], d_recv.at[piece], frame=home, row=x * per_home + i)
+
+    def d_in(i):
+        return push(total, weight_out.at[i], d_send.at[0], d_recv.at[i], frame=source(i), row=from_row)
+
+    d_self = pltpu.make_async_copy(total, weight_out.at[piece], d_own)
+    for i in range(per_home):
+        away = other(home, x * per_home + i)
+
+        @pl.when(away)
+        def _():
+            d_out(i).start()
+
+        @pl.when(jnp.logical_not(away))
+        def _():
+            d_self.start()
+
     for k in range(1, high):
         b_in(k).wait_recv()
     z_src[...] = jnp.zeros_like(z_src)

time: 185 us -> 180 us (0.973)
  the two profiles are of different devices: /device:TPU:1 before, /device:TPU:16 now
where the time goes in v4:
time: 180 us
  Pallas kernels  158 us (88%)
  local copies, waits for them, and re-layouts  15.1 us (8%)
  other arithmetic  4.82 us (3%)
    pallas_call x1, Pallas kernels, finish(): pl.pallas_call(finish_kernel, out_shape=(low, low, jax.ShapeDtypeStruct((...  62.7 us
    pallas_call x1, Pallas kernels, exchange_chain(): pl.pallas_call(functools.partial(exchange_chain_kernel, per_head), out_sh...  49.6 us
    pallas_call x1, Pallas kernels, gather(): pl.pallas_call(gather_kernel, out_shape=jax.ShapeDtypeStruct((high, wide,...  20.8 us
    pallas_call x1, Pallas kernels, core(): pl.pallas_call(core_kernel, out_shape=(wide((length, width)), wide((lengt...  16.8 us
    pallas_call x1, Pallas kernels, head(): pl.pallas_call(head_kernel, out_shape=(low((length, width)), low((length,...  8.03 us

profile of v4, /device:TPU:16, one launch (start us, length us, event | category | flops | bytes accessed | tf_op | source)
XLA Modules:
  0.0 179.8 jit_solution(13179829967113813134)
XLA Ops:
  0.6 0.0 copy-start
  0.6 0.0 copy-start.1
  0.7 0.7 convert_element_type.35
  1.4 0.8 reshape.72
  2.2 0.1 multiply_cosine_fusion
  2.3 0.0 copy-done
  2.3 0.1 fusion.6
  2.4 0.1 convert_element_type.42
  2.5 0.1 convert_element_type.40
  2.6 0.1 convert_element_type.38
  2.7 1.3 select_maximum_fusion.small
  4.0 0.7 fusion.13
  4.7 2.4 %concatenate.7.src = bf16[80,128]{1,0:T(8,128)(2,1)} concatenate(bf16[32,128]{1,0:T(8,128)(2,1)S(1)} %get-tuple-element.48, bf16[32,128]{1,0:T(8,128)(2,1)S(1)} %get-tuple-element.47, bf16[8,128]{1,0:T(8,128)(2,1)S(1)} %reshape.72, bf16[2,128]{1,0:T(2,128)(2,1)S(1)} %convert_element_type.38, bf16[2,128]{1,0:T(2,128)(2,1)S(1)} %convert_element_type.40, ...), dimensions={0} | concatenate | bytes 40960 | tf_op jit(solution)/shard_map/concatenate | solution.py:1020
  7.1 0.9 fusion.expand
  8.0 2.2 %reshape_reshape.6.xs = bf16[64,2,2048]{2,1,0:T(2,128)(2,1)} reshape(bf16[1,1,128,2048]{3,2,1,0:T(8,128)(2,1)} %param.10) | data formatting | bytes 1048576 | tf_op jit(solution)/shard_map/reshape;reshape | solution.py:1042
  10.2 0.0 copy-done.1
  10.2 1.1 reshape_reshape.7.gs
  11.3 20.8 %gather.1 = bf16[8,4,2,80,128]{4,3,2,1,0:T(8,128)(2,1)} custom-call(bf16[80,128]{1,0:T(8,128)(2,1)} %concatenate.7.src), custom_call_target="tpu_custom_call" | custom-call | tf_op jit(solution)/shard_map/gather/pallas_call | solution.py:124
  32.1 0.9 slice.48
  33.0 0.9 slice_convert_fusion
  34.0 0.2 reshape.81
  34.2 0.1 reshape.77
  34.4 0.0 copy-start.3
  34.4 0.0 copy-start.4
  34.4 0.6 constant_dynamic-slice_fusion
  35.0 0.2 reshape.74
  35.3 0.9 pad.8.step_w
  36.2 8.0 %head.1 = (bf16[128,2048]{1,0:T(8,128)(2,1)}, bf16[128,256]{1,0:T(8,128)(2,1)}, bf16[128,128]{1,0:T(8,128)(2,1)}, f32[2048,128]{1,0:T(8,128)}, f32[2048,128]{1,0:T(8,128)}, /*index=5*/f32[1,128]{1,0:T(1,128)}) custom-call(bf16[128,2048]{1,0:T(8,128)(2,1)} %bitcast.25, bf16[128,2048]{1,0:T(8,128)(2,1)} %bitcast.23, bf16[64,80,128]{2,1,0:T(8,128)(2,1)} %bitcast.21, ...), custom_call_target="tpu_custom_call" | custom-call | tf_op jit(solution)/shard_map/head/pallas_call | solution.py:932
  44.2 0.0 copy-done.3
  44.2 0.0 copy-done.4
  44.2 49.6 %exchange_chain.1 = (bf16[64,2,2048]{2,1,0:T(2,128)(2,1)}, bf16[64,2,2048]{2,1,0:T(2,128)(2,1)}, bf16[2048,128]{1,0:T(8,128)(2,1)}, bf16[2048,128]{1,0:T(8,128)(2,1)}) custom-call(bf16[64,2,2048]{2,1,0:T(2,128)(2,1)} %reshape_reshape.6.xs, bf16[64,2,2048]{2,1,0:T(2,128)(2,1)} %reshape_reshape.7.gs, f32[2048,128]{1,0:T(8,128)} %get-tuple-element.28.end_local, ...), custom_call_target="tpu_custom_call" | custom-call | tf_op jit(solution)/shard_map/exchange_chain/pallas_call | solution.py:293
  93.8 16.8 %core.1 = (f32[128,2048]{1,0:T(8,128)}, f32[128,2048]{1,0:T(8,128)}, bf16[64,2,2048]{2,1,0:T(2,128)(2,1)}, bf16[64,2,2048]{2,1,0:T(2,128)(2,1)}, bf16[2048,256]{1,0:T(8,128)(2,1)}, /*index=5*/bf16[32,2048]{1,0:T(8,128)(2,1)}) custom-call(bf16[128,2048]{1,0:T(8,128)(2,1)} %get-tuple-element.25.normed, bf16[128,2048]{1,0:T(8,128)(2,1)} %bitcast.24, ...), custom_call_target="tpu_custom_call" | custom-call | tf_op jit(solution)/shard_map/core/pallas_call | solution.py:955
  110.6 62.7 %finish.1 = (bf16[128,2048]{1,0:T(8,128)(2,1)}, bf16[128,2048]{1,0:T(8,128)(2,1)}, f32[8,128]{1,0:T(8,128)}, f32[2,16,384]{2,1,0:T(8,128)}) custom-call(bf16[64,2,2048]{2,1,0:T(2,128)(2,1)} %get-tuple-element.35.ts, bf16[64,2,2048]{2,1,0:T(2,128)(2,1)} %get-tuple-element.36.bs, bf16[2048,256]{1,0:T(8,128)(2,1)} %get-tuple-element.37.wp, ...), custom_call_target="tpu_custom_call" | custom-call | tf_op jit(solution)/shard_map/finish/pallas_call | solution.py:607
  173.4 0.0 copy-start.2
  173.4 0.7 slice.47
  174.1 0.8 broadcast_multiply_fusion
  174.9 0.6 slice.56
  175.5 0.6 slice.55
  176.2 0.9 convolution_multiply_fusion
  177.1 1.9 %copy.21 = bf16[1,1,128,2048]{3,2,1,0:T(8,128)(2,1)} copy(bf16[1,1,128,2048]{3,2,1,0:T(8,128)(2,1)} %bitcast.28) | data formatting | bytes 1048576
  179.0 0.0 copy-done.2
  179.0 0.8 copy.22
  (6 shorter events, 0.1 us)
Async XLA Ops:
  0.6 1.7 copy-start
  0.6 9.6 %copy-start.1 = (bf16[1,1,128,2048]{3,2,1,0:T(8,128)(2,1)S(1)}, bf16[1,1,128,2048]{3,2,1,0:T(8,128)(2,1)}, u32[]{:S(2)}) copy-start(bf16[1,1,128,2048]{3,2,1,0:T(8,128)(2,1)} %param.11) | copy-start | bytes 1572868
  34.4 9.8 %copy-start.3 = (f32[4,2048]{1,0:T(4,128)}, f32[4,2048]{1,0:T(4,128)S(1)}, u32[]{:S(2)}) copy-start(f32[4,2048]{1,0:T(4,128)S(1)} %get-tuple-element.45.scale_all) | copy-start | bytes 98308
  34.4 9.8 %copy-start.4 = (f32[4,2048]{1,0:T(4,128)}, f32[4,2048]{1,0:T(4,128)S(1)}, u32[]{:S(2)}) copy-start(f32[4,2048]{1,0:T(4,128)S(1)} %get-tuple-element.46.shift_all) | copy-start | bytes 98308
  173.4 5.6 %copy-start.2 = (bf16[128,2048]{1,0:T(8,128)(2,1)S(1)}, bf16[128,2048]{1,0:T(8,128)(2,1)}, u32[]{:S(2)}) copy-start(bf16[128,2048]{1,0:T(8,128)(2,1)} %get-tuple-element.42) | copy-start | bytes 1572868
